TPU v7x, 32 devices: a whole 2x2x4 slice. The times are simulated.
32 devices in a mesh: fsdp: 8 (over z, y), mp: 4 (over x, core).
Axes of the slice: x: 2, y: 2, z: 4, core: 2. Of those that a mesh axis runs over, the one named last changes fastest.
Arguments:
- tokens: bfloat16 [2048, 2048], P('fsdp'), may hold values from -6 to 6
- cotangent: bfloat16 [2048, 2048], P('fsdp'), may hold values from -6 to 6
- segment_ids: int32 [2048], P('fsdp'), may hold values from 0 to 3, as said below
- span_map: int32 [16], P('fsdp'), may hold values from 0 to 15, as said below
- norm_params: float32 [4, 2048], P(None, 'fsdp'), may hold values from -0.5 to 1.4, as said below
- norm_first: float32 [4, 2048], P(None, 'fsdp'), may hold values from -512 to 512
- norm_second: float32 [4, 2048], P(None, 'fsdp'), may hold values from 430.08 to 1720.32
- attention_input: float32 [2048, 3, 2048], P('fsdp', None, 'mp'), may hold values from -0.125 to 0.125
- attention_input_first: float32 [2048, 3, 2048], P('fsdp', None, 'mp'), may hold values from -448 to 448
- attention_input_second: float32 [2048, 3, 2048], P('fsdp', None, 'mp'), may hold values from 276.48 to 1105.92
- attention_output: float32 [2048, 2048], P('mp', 'fsdp'), may hold values from -1.5 to 1.5
- attention_output_first: float32 [2048, 2048], P('mp', 'fsdp'), may hold values from -40 to 40
- attention_output_second: float32 [2048, 2048], P('mp', 'fsdp'), may hold values from 2.10944 to 8.3968
- expand_weight: float32 [2048, 8192], P('fsdp', 'mp'), may hold values from -0.125 to 0.125
- expand_first: float32 [2048, 8192], P('fsdp', 'mp'), may hold values from -80 to 80
- expand_second: float32 [2048, 8192], P('fsdp', 'mp'), may hold values from 9.68704 to 38.7072
- reduce_weight: float32 [8192, 2048], P('mp', 'fsdp'), may hold values from -0.0625 to 0.0625
- reduce_first: float32 [8192, 2048], P('mp', 'fsdp'), may hold values from -160 to 160
- reduce_second: float32 [8192, 2048], P('mp', 'fsdp'), may hold values from 38.7072 to 155.0336
Outputs:
- output: bfloat16 [2048, 2048], P('fsdp')
- input_grad: float32 [2048, 2048], P('fsdp')
- attention_input_moment: float32 [2048, 3, 2048], P('fsdp', None, 'mp')
- attention_input_square: float32 [2048, 3, 2048], P('fsdp', None, 'mp')
- attention_input_master: float32 [2048, 3, 2048], P('fsdp', None, 'mp')
- attention_input_rounded: bfloat16 [2048, 3, 2048], P('fsdp', None, 'mp')
- attention_output_moment: float32 [2048, 2048], P('mp', 'fsdp')
- attention_output_square: float32 [2048, 2048], P('mp', 'fsdp')
- attention_output_master: float32 [2048, 2048], P('mp', 'fsdp')
- attention_output_rounded: bfloat16 [2048, 2048], P('mp', 'fsdp')
- expand_moment: float32 [2048, 8192], P('fsdp', 'mp')
- expand_square: float32 [2048, 8192], P('fsdp', 'mp')
- expand_master: float32 [2048, 8192], P('fsdp', 'mp')
- expand_rounded: bfloat16 [2048, 8192], P('fsdp', 'mp')
- reduce_moment: float32 [8192, 2048], P('mp', 'fsdp')
- reduce_square: float32 [8192, 2048], P('mp', 'fsdp')
- reduce_master: float32 [8192, 2048], P('mp', 'fsdp')
- reduce_rounded: bfloat16 [8192, 2048], P('mp', 'fsdp')
- norm_moment: float32 [4, 2048], P(None, 'fsdp')
- norm_square: float32 [4, 2048], P(None, 'fsdp')
- norm_master: float32 [4, 2048], P(None, 'fsdp')
Inputs may be any that keep to these rules, and one draw needn't show every extreme that they name: `span_map`: each number appears once. The packed row of span c is c // 16; slot s of the dealt order is held at index s // 2 of fsdp. `segment_ids`: in the order of the packed rows, ids never fall along a row and are 4 * row plus 0 to 3; tokens of different rows never share an id. `norm_params`: rows 0 and 2 are gains from 0.6 to 1.4, rows 1 and 3 biases from -0.5 to 0.5.
All inputs are finite; a program needn't handle non-finite values.
Results may differ from a plain program's by a relative error of at most 0.024.
Values may be sent and summed in bfloat16 or wider, within the bound.
No kernel may reach another device: no remote copies, remote signals or barrier semaphores. Data moves between devices by JAX's collectives and lax.ppermute only.
A program may use at most 256 MiB of HBM per device.

v0:
```python
from functools import partial
import math

import jax
import jax.numpy as jnp
from jax import lax
from jax.sharding import PartitionSpec as P

D = 2048
HEADS = 16
SPAN = 128
ROW_LEN = 2048
STEP = 7


first_decay = 0.5
second_decay = 0.95
adam_epsilon = 1e-08
norm_epsilon = 1e-05
matrix_shrink = 0.1
input_rate = 0.02
output_rate = 0.45
expand_rate = 0.02
reduce_rate = 0.01
gain_rate = 0.2


def layer_norm(features, gain_row, bias_row):
    centre = jnp.mean(features, axis=-1, keepdims=True)
    centred = features - centre
    spread = jnp.mean(centred * centred, axis=-1, keepdims=True)
    return centred * lax.rsqrt(spread + norm_epsilon) * gain_row + bias_row


def smooth_gelu(values):
    return jax.nn.gelu(values, approximate=True)


def adamw_update(master, moment_one, moment_two, gradient, step_rate, shrink_rate):
    moment_one = first_decay * moment_one + (1.0 - first_decay) * gradient
    moment_two = second_decay * moment_two + (1.0 - second_decay) * gradient * gradient
    mean_part = moment_one / (1.0 - first_decay**STEP)
    square_part = moment_two / (1.0 - second_decay**STEP)
    updated = master - step_rate * (
        mean_part / (jnp.sqrt(square_part) + adam_epsilon) + shrink_rate * master
    )
    return (moment_one, moment_two, updated)


def visible_scores(queries, key_part, query_labels, query_places, key_labels, key_places, scaling):
    scores = (
        jnp.einsum("qhe,khe->qhk", queries, key_part, preferred_element_type=jnp.float32) * scaling
    )
    allowed = (query_labels[:, None] == key_labels[None, :]) & (
        key_places[None, :] <= query_places[:, None]
    )
    return (scores, allowed[:, None, :])


def attend_block(running, pieces, offset, queries, query_labels, query_places, scaling):
    largest, totals, summed = running
    key_part, value_part, key_labels, key_places = pieces
    width = key_part.shape[0]
    key_part = key_part.reshape(width, queries.shape[1], queries.shape[2])
    value_part = value_part.reshape(width, queries.shape[1], queries.shape[2])
    scores, allowed = visible_scores(
        queries, key_part, query_labels, query_places, key_labels, key_places, scaling
    )
    newest = jnp.maximum(largest, jnp.max(jnp.where(allowed, scores, -1e30), axis=2))
    weights = jnp.where(allowed, jnp.exp(scores - newest[:, :, None]), 0.0)
    totals = jnp.sum(weights, axis=2)
    summed = jnp.einsum(
        "qhk,khe->qhe", weights.astype(jnp.bfloat16), value_part, preferred_element_type=jnp.float32
    )
    return (newest, totals, summed)


def query_block(
    running,
    pieces,
    offset,
    queries,
    grad_heads,
    logsum,
    row_dots,
    query_labels,
    query_places,
    scaling,
):
    key_part, value_part, key_labels, key_places = pieces
    width = key_part.shape[0]
    key_part = key_part.reshape(width, queries.shape[1], queries.shape[2])
    value_part = value_part.reshape(width, queries.shape[1], queries.shape[2])
    scores, allowed = visible_scores(
        queries, key_part, query_labels, query_places, key_labels, key_places, scaling
    )
    probs = jnp.where(allowed, jnp.exp(scores - logsum[:, :, None]), 0.0)
    prob_grad = jnp.einsum(
        "qhe,khe->qhk", grad_heads, value_part, preferred_element_type=jnp.float32
    )
    score_grad = (probs * (prob_grad - row_dots[:, :, None])).astype(jnp.bfloat16)
    return running + jnp.einsum(
        "qhk,khe->qhe", score_grad, key_part, preferred_element_type=jnp.float32
    )


def over_blocks(advance, start_state, gathered):
    extent = gathered[0].shape[0]
    block_size = math.gcd(extent, 2048)
    block_count = extent // block_size
    stacked = tuple(
        (member.reshape((block_count, block_size) + member.shape[1:]) for member in gathered)
    )

    def scan_step(running, pieces):
        return (advance(running, pieces, 0), None)

    return lax.scan(scan_step, start_state, stacked)[0]


def local(
    tokens,
    cotangent,
    segment_ids,
    span_map,
    norm_params,
    norm_first,
    norm_second,
    attention_input,
    attention_input_first,
    attention_input_second,
    attention_output,
    attention_output_first,
    attention_output_second,
    expand_weight,
    expand_first,
    expand_second,
    reduce_weight,
    reduce_first,
    reduce_second,
):
    head_size = D // HEADS
    scaling = head_size ** (-0.5)
    local_tokens = tokens.shape[0]
    places = (
        span_map[:, None] % (ROW_LEN // SPAN) * SPAN + jnp.arange(SPAN, dtype=jnp.int32)[None, :]
    ).reshape(-1)
    input_low = attention_input.astype(jnp.bfloat16)
    output_low = attention_output.astype(jnp.bfloat16)
    expand_low = expand_weight.astype(jnp.bfloat16)
    reduce_low = reduce_weight.astype(jnp.bfloat16)
    norm_low = norm_params.astype(jnp.bfloat16)
    input_full, output_full, expand_full, reduce_full, norm_full = (
        lax.all_gather(input_low, "fsdp", axis=0, tiled=True),
        lax.all_gather(output_low, "fsdp", axis=1, tiled=True),
        lax.all_gather(expand_low, "fsdp", axis=0, tiled=True),
        lax.all_gather(reduce_low, "fsdp", axis=1, tiled=True),
        lax.all_gather(norm_low, "fsdp", axis=1, tiled=True),
    )
    norm_values = norm_full.astype(jnp.float32)
    local_width = input_full.shape[2]
    head_count = local_width // head_size
    features = tokens.astype(jnp.float32)
    normed_one = layer_norm(features, norm_values[0], norm_values[1]).astype(jnp.bfloat16)
    projected = jnp.einsum(
        "td,dcm->tcm", normed_one, input_full, preferred_element_type=jnp.float32
    ).astype(jnp.bfloat16)
    key_rows = projected[:, 1]
    value_rows = projected[:, 2]
    query_rows = projected[:, 0]
    query_heads = query_rows.reshape(local_tokens, head_count, head_size)
    start_state = (
        jnp.full((local_tokens, head_count), -1e30, jnp.float32),
        jnp.zeros((local_tokens, head_count), jnp.float32),
        jnp.zeros((local_tokens, head_count, head_size), jnp.float32),
    )
    attend = partial(
        attend_block,
        queries=query_heads,
        query_labels=segment_ids,
        query_places=places,
        scaling=scaling,
    )
    largest, totals, summed = attend(
        start_state,
        (
            lax.all_gather(key_rows, "fsdp", axis=0, tiled=True),
            lax.all_gather(value_rows, "fsdp", axis=0, tiled=True),
            lax.all_gather(segment_ids, "fsdp", axis=0, tiled=True),
            lax.all_gather(places, "fsdp", axis=0, tiled=True),
        ),
        jnp.int32(0),
    )
    attended = summed / totals[:, :, None]
    logsum = largest + jnp.log(totals)
    mixed = attended.reshape(local_tokens, local_width).astype(jnp.bfloat16)
    branch = lax.psum(
        jnp.dot(mixed, output_full, preferred_element_type=jnp.float32).astype(jnp.bfloat16), "mp"
    ).astype(jnp.float32)
    middle = features + branch
    normed_two = layer_norm(middle, norm_values[2], norm_values[3]).astype(jnp.bfloat16)
    hidden = jnp.dot(normed_two, expand_full, preferred_element_type=jnp.float32)
    active = smooth_gelu(hidden).astype(jnp.bfloat16)
    feed = lax.psum(
        jnp.dot(active, reduce_full, preferred_element_type=jnp.float32).astype(jnp.bfloat16), "mp"
    ).astype(jnp.float32)
    output = (middle + feed).astype(jnp.bfloat16)
    input_full, output_full, expand_full, reduce_full = (
        lax.all_gather(input_low, "fsdp", axis=0, tiled=True),
        lax.all_gather(output_low, "fsdp", axis=1, tiled=True),
        lax.all_gather(expand_low, "fsdp", axis=0, tiled=True),
        lax.all_gather(reduce_low, "fsdp", axis=1, tiled=True),
    )
    active_grad = jnp.einsum(
        "td,fd->tf", cotangent, reduce_full, preferred_element_type=jnp.float32
    )
    hidden_grad = jax.vjp(smooth_gelu, hidden)[1](active_grad)[0].astype(jnp.bfloat16)
    second_grad = lax.psum(
        jnp.einsum(
            "tf,df->td", hidden_grad, expand_full, preferred_element_type=jnp.float32
        ).astype(jnp.bfloat16),
        "mp",
    ).astype(jnp.float32)
    second_pull = jax.vjp(layer_norm, middle, norm_values[2], norm_values[3])[1]
    middle_part, gain_two, bias_two = second_pull(second_grad)
    middle_grad = cotangent.astype(jnp.float32) + middle_part
    branch_grad = middle_grad.astype(jnp.bfloat16)
    mixed_grad = jnp.einsum(
        "td,md->tm", branch_grad, output_full, preferred_element_type=jnp.float32
    ).astype(jnp.bfloat16)
    grad_heads = mixed_grad.reshape(local_tokens, head_count, head_size)
    row_dots = jnp.sum(grad_heads.astype(jnp.float32) * attended, axis=2)
    key_set = (
        lax.all_gather(key_rows, "fsdp", axis=0, tiled=True),
        lax.all_gather(value_rows, "fsdp", axis=0, tiled=True),
        lax.all_gather(segment_ids, "fsdp", axis=0, tiled=True),
        lax.all_gather(places, "fsdp", axis=0, tiled=True),
    )
    key_all, value_all, label_all, place_all = key_set
    query_step = partial(
        query_block,
        queries=query_heads,
        grad_heads=grad_heads,
        logsum=logsum,
        row_dots=row_dots,
        query_labels=segment_ids,
        query_places=places,
        scaling=scaling,
    )
    query_grad = over_blocks(
        query_step, jnp.zeros((local_tokens, head_count, head_size), jnp.float32), key_set
    )
    query_grad = (query_grad * scaling).reshape(local_tokens, local_width).astype(jnp.bfloat16)
    length = local_tokens * lax.axis_size("fsdp")
    key_part = key_all.reshape(length, head_count, head_size)
    value_part = value_all.reshape(length, head_count, head_size)
    scores, allowed = visible_scores(
        query_heads, key_part, segment_ids, places, label_all, place_all, scaling
    )
    probs = jnp.where(allowed, jnp.exp(scores - logsum[:, :, None]), 0.0)
    prob_grad = jnp.einsum(
        "qhe,khe->qhk", grad_heads, value_part, preferred_element_type=jnp.float32
    )
    score_grad = (probs * (prob_grad - row_dots[:, :, None])).astype(jnp.bfloat16)
    value_term = jnp.einsum(
        "qhk,qhe->khe", probs.astype(jnp.bfloat16), grad_heads, preferred_element_type=jnp.float32
    )
    key_term = (
        jnp.einsum("qhk,qhe->khe", score_grad, query_heads, preferred_element_type=jnp.float32)
        * scaling
    )
    key_value_grad = lax.psum_scatter(
        jnp.concatenate(
            [key_term.reshape(length, local_width), value_term.reshape(length, local_width)], axis=1
        ).astype(jnp.bfloat16),
        "fsdp",
        scatter_dimension=0,
        tiled=True,
    ).astype(jnp.float32)
    key_grad = key_value_grad[:, :local_width].astype(jnp.bfloat16)
    value_grad = key_value_grad[:, local_width:].astype(jnp.bfloat16)
    projected_grad = jnp.stack([query_grad, key_grad, value_grad], axis=1)
    first_grad = lax.psum(
        jnp.einsum(
            "tcm,dcm->td", projected_grad, input_full, preferred_element_type=jnp.float32
        ).astype(jnp.bfloat16),
        "mp",
    ).astype(jnp.float32)
    first_pull = jax.vjp(layer_norm, features, norm_values[0], norm_values[1])[1]
    input_part, gain_one, bias_one = first_pull(first_grad)
    input_grad = middle_grad + input_part
    grad_input = jnp.einsum(
        "td,tcm->dcm", normed_one, projected_grad, preferred_element_type=jnp.float32
    )
    grad_output = jnp.einsum("tm,td->md", mixed, branch_grad, preferred_element_type=jnp.float32)
    grad_expand = jnp.einsum(
        "td,tf->df", normed_two, hidden_grad, preferred_element_type=jnp.float32
    )
    grad_reduce = jnp.einsum("tf,td->fd", active, cotangent, preferred_element_type=jnp.float32)
    grad_norm = jnp.stack([gain_one, bias_one, gain_two, bias_two])
    share_input, share_output, share_expand, share_reduce, share_norm = (
        lax.psum_scatter(
            grad_input.astype(jnp.bfloat16), "fsdp", scatter_dimension=0, tiled=True
        ).astype(jnp.float32),
        lax.psum_scatter(
            grad_output.astype(jnp.bfloat16), "fsdp", scatter_dimension=1, tiled=True
        ).astype(jnp.float32),
        lax.psum_scatter(
            grad_expand.astype(jnp.bfloat16), "fsdp", scatter_dimension=0, tiled=True
        ).astype(jnp.float32),
        lax.psum_scatter(
            grad_reduce.astype(jnp.bfloat16), "fsdp", scatter_dimension=1, tiled=True
        ).astype(jnp.float32),
        lax.psum_scatter(
            grad_norm.astype(jnp.bfloat16), "fsdp", scatter_dimension=1, tiled=True
        ).astype(jnp.float32),
    )
    input_new = adamw_update(
        attention_input,
        attention_input_first,
        attention_input_second,
        share_input,
        input_rate,
        matrix_shrink,
    )
    output_new = adamw_update(
        attention_output,
        attention_output_first,
        attention_output_second,
        share_output,
        output_rate,
        matrix_shrink,
    )
    expand_new = adamw_update(
        expand_weight, expand_first, expand_second, share_expand, expand_rate, matrix_shrink
    )
    reduce_new = adamw_update(
        reduce_weight, reduce_first, reduce_second, share_reduce, reduce_rate, matrix_shrink
    )
    norm_new = adamw_update(norm_params, norm_first, norm_second, share_norm, gain_rate, 0.0)
    return (
        output,
        input_grad,
        input_new[0],
        input_new[1],
        input_new[2],
        input_new[2].astype(jnp.bfloat16),
        output_new[0],
        output_new[1],
        output_new[2],
        output_new[2].astype(jnp.bfloat16),
        expand_new[0],
        expand_new[1],
        expand_new[2],
        expand_new[2].astype(jnp.bfloat16),
        reduce_new[0],
        reduce_new[1],
        reduce_new[2],
        reduce_new[2].astype(jnp.bfloat16),
        norm_new[0],
        norm_new[1],
        norm_new[2],
    )


def solution(mesh):
    return jax.shard_map(
        local,
        mesh=mesh,
        in_specs=(
            P("fsdp", None),
            P("fsdp", None),
            P("fsdp"),
            P("fsdp"),
            P(None, "fsdp"),
            P(None, "fsdp"),
            P(None, "fsdp"),
            P("fsdp", None, "mp"),
            P("fsdp", None, "mp"),
            P("fsdp", None, "mp"),
            P("mp", "fsdp"),
            P("mp", "fsdp"),
            P("mp", "fsdp"),
            P("fsdp", "mp"),
            P("fsdp", "mp"),
            P("fsdp", "mp"),
            P("mp", "fsdp"),
            P("mp", "fsdp"),
            P("mp", "fsdp"),
        ),
        out_specs=(
            P("fsdp", None),
            P("fsdp", None),
            P("fsdp", None, "mp"),
            P("fsdp", None, "mp"),
            P("fsdp", None, "mp"),
            P("fsdp", None, "mp"),
            P("mp", "fsdp"),
            P("mp", "fsdp"),
            P("mp", "fsdp"),
            P("mp", "fsdp"),
            P("fsdp", "mp"),
            P("fsdp", "mp"),
            P("fsdp", "mp"),
            P("fsdp", "mp"),
            P("mp", "fsdp"),
            P("mp", "fsdp"),
            P("mp", "fsdp"),
            P("mp", "fsdp"),
            P(None, "fsdp"),
            P(None, "fsdp"),
            P(None, "fsdp"),
        ),
        check_vma=False,
    )
```

profile of v0, /device:TPU:9, one launch (start us, length us, event | category | flops | bytes accessed | tf_op | source)
XLA Modules:
  0.0 1385.0 jit_solution(2999350856255674024)
XLA Ops:
  9.8 20.4 %all_gather.35 = bf16[4,2048]{1,0:T(4,128)(2,1)S(1)} all-gather(bf16[4,256]{1,0:T(4,128)(2,1)S(1)} %convert_element_type.153), channel_id=1, replica_groups=mesh['fsdp'=8,'mp'=4] {'fsdp'}, dimensions={1}, use_global_device_ids=true | all-gather | bytes 18432 | tf_op jit(solution)/shard_map/all_gather | solution.py:158
  30.9 77.9 %all-gather.11.cloned.1.call-done = bf16[2048,3,512]{2,0,1:T(8,128)(2,1)} async-done(((bf16[256,3,512]{2,0,1:T(8,128)(2,1)}), bf16[2048,3,512]{2,0,1:T(8,128)(2,1)}) %all-gather.11.cloned.1.call-update) | async-done | bytes 6291472 | tf_op jit(solution)/shard_map/all_gather | solution.py:154
  116.1 14.1 %all-gather.3 = s32[8,1,256]{2,1,0:T(1,128)S(1)} all-gather(s32[1,1,256]{2,1,0:T(1,128)S(1)} %bitcast.136), channel_id=1, replica_groups=mesh['fsdp'=8,'mp'=4] {'fsdp'}, dimensions={0}, use_global_device_ids=true | all-gather | bytes 9216 | tf_op jit(solution)/shard_map/all_gather | solution.py:190
  130.3 12.7 all-gather.2
  144.5 19.0 %all-gather.19.cloned.1.call-done = bf16[2048,1,512]{2,0,1:T(8,128)(2,1)} async-done(((bf16[256,1,512]{2,0,1:T(8,128)(2,1)}), bf16[2048,1,512]{2,0,1:T(8,128)(2,1)}) %all-gather.19.cloned.1.call-update) | async-done | bytes 2097168 | tf_op jit(solution)/shard_map/all_gather | solution.py:188
  167.5 46.6 %all-gather.21.cloned.1.call-done = bf16[2048,1,512]{2,0,1:T(8,128)(2,1)} async-done(((bf16[256,1,512]{2,0,1:T(8,128)(2,1)}), bf16[2048,1,512]{2,0,1:T(8,128)(2,1)}) %all-gather.21.cloned.1.call-update) | async-done | bytes 2097168 | tf_op jit(solution)/shard_map/all_gather | solution.py:187
  228.0 36.7 %all-gather.13.cloned.1.call-done = bf16[512,2048]{1,0:T(8,128)(2,1)} async-done(((bf16[512,256]{1,0:T(8,128)(2,1)}), bf16[512,2048]{1,0:T(8,128)(2,1)}) %all-gather.13.cloned.1.call-update) | async-done | bytes 2097168 | tf_op jit(solution)/shard_map/all_gather | solution.py:155
  271.4 32.9 %all-reduce.5.cloned.1.call-done = bf16[256,2048]{1,0:T(8,128)(2,1)} async-done(((bf16[256,2048]{1,0:T(8,128)(2,1)}), bf16[256,2048]{1,0:T(8,128)(2,1)}) %all-reduce.5.cloned.1.call-update) | async-done | bytes 1048592 | tf_op jit(solution)/shard_map/psum | solution.py:197
  306.4 124.1 %all-gather.15.cloned.1.call-done = bf16[2048,2048]{1,0:T(8,128)(2,1)} async-done(((bf16[256,2048]{1,0:T(8,128)(2,1)}), bf16[2048,2048]{1,0:T(8,128)(2,1)}) %all-gather.15.cloned.1.call-update) | async-done | bytes 8388624 | tf_op jit(solution)/shard_map/all_gather | solution.py:156
  430.6 5.9 fusion.86
  437.8 5.9 convolution_convert_fusion
  443.8 148.4 %reduce-scatter.17.cloned.1.call-done = bf16[2048,256]{1,0:T(8,128)(2,1)} async-done(((bf16[2048,2048]{1,0:T(8,128)(2,1)}), bf16[2048,256]{1,0:T(8,128)(2,1)}) %reduce-scatter.17.cloned.1.call-update) | async-done | bytes 1048592 | tf_op jit(solution)/shard_map/reduce_scatter | solution.py:311
  592.2 9.2 fusion.88
  601.5 123.8 %all-gather.17.cloned.1.call-done = bf16[2048,2048]{1,0:T(8,128)(2,1)} async-done(((bf16[2048,256]{1,0:T(8,128)(2,1)}), bf16[2048,2048]{1,0:T(8,128)(2,1)}) %all-gather.17.cloned.1.call-update) | async-done | bytes 8388624 | tf_op jit(solution)/shard_map/all_gather | solution.py:157
  725.3 7.3 fusion.42
  733.6 6.7 convolution_convert_fusion.5
  740.6 35.9 %all-reduce.7.cloned.1.call-done = bf16[256,2048]{1,0:T(8,128)(2,1)} async-done(((bf16[256,2048]{1,0:T(8,128)(2,1)}), bf16[256,2048]{1,0:T(8,128)(2,1)}) %all-reduce.7.cloned.1.call-update) | async-done | bytes 1048592 | tf_op jit(solution)/shard_map/psum | solution.py:218
  786.6 7.0 fusion.23
  793.6 5.1 fusion.1
  809.3 4.8 pad_maximum_fusion
  814.4 7.7 convolution_convert_fusion.6
  823.7 79.4 %reduce-scatter.9.cloned.1.call-done = bf16[256,1024]{1,0:T(8,128)(2,1)} async-done(((bf16[2048,1024]{1,0:T(8,128)(2,1)}), bf16[256,1024]{1,0:T(8,128)(2,1)}) %reduce-scatter.9.cloned.1.call-update) | async-done | bytes 524304 | tf_op jit(solution)/shard_map/reduce_scatter | solution.py:272
  904.9 5.7 fusion.26
  915.1 46.9 %all-reduce.9.cloned.1.call-done = (bf16[256,2048]{1,0:T(8,128)(2,1)}, bf16[256,2048]{1,0:T(8,128)(2,1)}) async-done(((bf16[256,2048]{1,0:T(8,128)(2,1)}, bf16[256,2048]{1,0:T(8,128)(2,1)}), (bf16[256,2048]{1,0:T(8,128)(2,1)}, bf16[256,2048]{1,0:T(8,128)(2,1)})) %all-reduce.9.cloned.1.call-update) | async-done | bytes 2097168 | tf_op jit(solution)/shard_map/psum | solution.py:204
  967.5 7.2 convolution_convert_fusion.1
  975.6 5.8 convolution_convert_fusion.2
  981.4 51.5 %reduce-scatter.13.cloned.1.call-done = bf16[512,256]{1,0:T(8,128)(2,1)} async-done(((bf16[512,2048]{1,0:T(8,128)(2,1)}), bf16[512,256]{1,0:T(8,128)(2,1)}) %reduce-scatter.13.cloned.1.call-update) | async-done | bytes 262160 | tf_op jit(solution)/shard_map/reduce_scatter | solution.py:305
  1040.4 57.6 %reduce-scatter.19.cloned.1.call-done = bf16[256,4]{1,0:T(8,128)(2,1)} async-done(((bf16[2048,4]{1,0:T(8,128)(2,1)}), bf16[256,4]{1,0:T(8,128)(2,1)}) %reduce-scatter.19.cloned.1.call-update) | async-done | bytes 2064
  1099.6 150.5 %reduce-scatter.15.cloned.1.call-done = bf16[256,2048]{1,0:T(8,128)(2,1)} async-done(((bf16[2048,2048]{1,0:T(8,128)(2,1)}), bf16[256,2048]{1,0:T(8,128)(2,1)}) %reduce-scatter.15.cloned.1.call-update) | async-done | bytes 1048592 | tf_op jit(solution)/shard_map/reduce_scatter | solution.py:308
  1250.1 8.4 fusion.90
  1258.5 113.5 %reduce-scatter.11.cloned.1.call-done = bf16[256,3,512]{2,0,1:T(8,128)(2,1)} async-done(((bf16[2048,3,512]{2,0,1:T(8,128)(2,1)}), bf16[256,3,512]{2,0,1:T(8,128)(2,1)}) %reduce-scatter.11.cloned.1.call-update) | async-done | bytes 786448 | tf_op jit(solution)/shard_map/reduce_scatter | solution.py:302
  1371.9 6.1 fusion.94
  (156 shorter events, 85.5 us)
Async XLA Ops:
  7.2 23.0 %copy-start = (bf16[256,2048]{1,0:T(8,128)(2,1)S(1)}, bf16[256,2048]{1,0:T(8,128)(2,1)}, u32[]{:S(2)}) copy-start(bf16[256,2048]{1,0:T(8,128)(2,1)} %param.19) | copy-start | bytes 3145732
  7.2 101.7 %all-gather.11.cloned.1.call-start = ((), (), s32[]{:S(2)}) async-start(), calls=%async_computation.6 | async-start | bytes 7077888 | tf_op jit(solution)/shard_map/all_gather | solution.py:154
  9.7 153.8 %all-gather.19.cloned.1.call-start = ((), (), s32[]{:S(2)}) async-start(), calls=%async_computation.17 | async-start | bytes 2359296 | tf_op jit(solution)/shard_map/all_gather | solution.py:188
  113.5 16.7 %copy-start.29 = (s32[256]{0:T(256)S(1)}, s32[256]{0:T(256)}, u32[]{:S(2)}) copy-start(s32[256]{0:T(256)} %param.21) | copy-start | bytes 3076
  114.4 99.6 %all-gather.21.cloned.1.call-start = ((), (), s32[]{:S(2)}) async-start(), calls=%async_computation.18 | async-start | bytes 2359296 | tf_op jit(solution)/shard_map/all_gather | solution.py:187
  115.2 149.6 %all-gather.13.cloned.1.call-start = ((), (), s32[]{:S(2)}) async-start(), calls=%async_computation.7 | async-start | bytes 2359296 | tf_op jit(solution)/shard_map/all_gather | solution.py:155
  116.0 188.3 %all-reduce.5.cloned.1.call-start = ((), (), s32[]{:S(2)}) async-start(), calls=%async_computation.8 | async-start | bytes 2097152 | tf_op jit(solution)/shard_map/psum | solution.py:197
  144.4 78.8 %copy-start.11 = (pred[256,2048]{0,1:T(8,128)(4,1)}, pred[256,2048]{0,1:T(8,128)(4,1)S(1)}, u32[]{:S(2)}) copy-start(pred[256,2048]{0,1:T(8,128)(4,1)S(1)} %compare_and_fusion) | copy-start | bytes 1572868
  221.3 3.7 copy-start.2
  221.4 3.7 copy-start.18
  228.0 40.1 %copy-start.23 = (bf16[256,4,128]{0,2,1:T(8,128)(2,1)}, bf16[256,4,128]{0,2,1:T(8,128)(2,1)S(1)}, u32[]{:S(2)}) copy-start(bf16[256,4,128]{0,2,1:T(8,128)(2,1)S(1)} %get-tuple-element.100) | copy-start | bytes 786436
  268.1 162.5 %all-gather.15.cloned.1.call-start = ((), (), s32[]{:S(2)}) async-start(), calls=%async_computation.9 | async-start | bytes 9437184 | tf_op jit(solution)/shard_map/all_gather | solution.py:156
  270.9 321.4 %reduce-scatter.17.cloned.1.call-start = ((), (), s32[]{:S(2)}) async-start(), calls=%async_computation.16 | async-start | bytes 9437184 | tf_op jit(solution)/shard_map/reduce_scatter | solution.py:311
  430.6 7.2 copy-start.13
  443.8 281.5 %all-gather.17.cloned.1.call-start = ((), (), s32[]{:S(2)}) async-start(), calls=%async_computation.10 | async-start | bytes 9437184 | tf_op jit(solution)/shard_map/all_gather | solution.py:157
  601.5 175.1 %all-reduce.7.cloned.1.call-start = ((), (), s32[]{:S(2)}) async-start(), calls=%async_computation.11 | async-start | bytes 2097152 | tf_op jit(solution)/shard_map/psum | solution.py:218
  740.4 162.7 %reduce-scatter.9.cloned.1.call-start = ((), (), s32[]{:S(2)}) async-start(), calls=%async_computation.12 | async-start | bytes 4718592 | tf_op jit(solution)/shard_map/reduce_scatter | solution.py:272
  786.5 7.0 copy-start.12
  786.5 7.0 copy-start.19
  786.5 7.0 copy-start.22
  814.1 147.9 %all-reduce.9.cloned.1.call-start = ((), (), s32[]{:S(2)}) async-start(), calls=%async_computation.20 | async-start | bytes 4194304 | tf_op jit(solution)/shard_map/psum | solution.py:204
  814.4 7.7 copy-start.4
  814.4 7.7 copy-start.5
  910.6 122.3 %reduce-scatter.13.cloned.1.call-start = ((), (), s32[]{:S(2)}) async-start(), calls=%async_computation.14 | async-start | bytes 2359296 | tf_op jit(solution)/shard_map/reduce_scatter | solution.py:305
  914.8 183.2 %reduce-scatter.19.cloned.1.call-start = ((), (), s32[]{:S(2)}) async-start(), calls=%async_computation.19 | async-start | bytes 589824
  967.4 282.6 %reduce-scatter.15.cloned.1.call-start = ((), (), s32[]{:S(2)}) async-start(), calls=%async_computation.15 | async-start | bytes 9437184 | tf_op jit(solution)/shard_map/reduce_scatter | solution.py:308
  974.7 397.3 %reduce-scatter.11.cloned.1.call-start = ((), (), s32[]{:S(2)}) async-start(), calls=%async_computation.13 | async-start | bytes 7077888 | tf_op jit(solution)/shard_map/reduce_scatter | solution.py:302
  1032.9 3.3 copy-start.7
  1032.9 3.3 copy-start.15
  1036.2 62.8 %copy-start.30 = (f32[4,256]{1,0:T(4,128)S(1)}, f32[4,256]{1,0:T(4,128)}, u32[]{:S(2)}) copy-start(f32[4,256]{1,0:T(4,128)} %param.24) | copy-start | bytes 12292
  1036.2 62.8 %copy-start.31 = (f32[4,256]{1,0:T(4,128)S(1)}, f32[4,256]{1,0:T(4,128)}, u32[]{:S(2)}) copy-start(f32[4,256]{1,0:T(4,128)} %param.25) | copy-start | bytes 12292
  1099.6 272.3 %copy-start.10 = (f32[256,3,512]{2,0,1:T(8,128)S(1)}, f32[256,3,512]{2,0,1:T(8,128)}, u32[]{:S(2)}) copy-start(f32[256,3,512]{2,0,1:T(8,128)} %param.26) | copy-start | bytes 4718596
  (17 other events, 28.2 us)
Sparse Core Ops, SparseCore 0:
  10.8 98.0 all-gather.10
  114.5 48.9 all-gather.18
  166.2 47.7 all-gather.20
  216.5 48.1 all-gather.12
  268.2 36.0 all-reduce.4
  307.0 123.5 all-gather.14
  443.9 148.2 reduce-scatter.16
  601.6 123.6 all-gather.16
  740.5 35.9 all-reduce.6
  814.2 88.7 reduce-scatter.8
  910.8 51.1 all-reduce.8
  966.4 66.4 reduce-scatter.12
  1037.2 60.8 reduce-scatter.18
  1101.5 148.4 reduce-scatter.14
  1254.0 117.9 reduce-scatter.10
where the time goes:
time: 1400 us; the launch traced here: 1390 us
  waiting for transfers between devices  1150 us (82%)
  matrix products  86.7 us (6%)
  other arithmetic  57.9 us (4%)
  blocking collectives  47.2 us (3%)
  local copies, waits for them, and re-layouts  31 us (2%)
  between operations  14.8 us (1%)
    reduce_scatter x1, waiting for transfers between devices, local(): lax.psum_scatter(grad_expand.astype(jnp.bfloat16), 'fsdp', scatter_dimens...  150 us
    reduce_scatter x1, waiting for transfers between devices, local(): lax.psum_scatter(grad_reduce.astype(jnp.bfloat16), 'fsdp', scatter_dimens...  148 us
    all_gather x1, waiting for transfers between devices, local(): lax.all_gather(expand_low, 'fsdp', axis=0, tiled=True)  124 us
    all_gather x1, waiting for transfers between devices, local(): lax.all_gather(reduce_low, 'fsdp', axis=1, tiled=True)  124 us
    reduce_scatter x1, waiting for transfers between devices, local(): lax.psum_scatter(grad_input.astype(jnp.bfloat16), 'fsdp', scatter_dimensi...  113 us
    reduce_scatter x1, waiting for transfers between devices, local(): lax.psum_scatter(jnp.concatenate([key_term.reshape(length, local_width),...  79.4 us
    all_gather x1, waiting for transfers between devices, local(): lax.all_gather(input_low, 'fsdp', axis=0, tiled=True)  77.9 us
    unnamed x16, waiting for transfers between devices  58.5 us
  transfers between devices with their start and end apart: 15, of which 15 were waited for; matrix products, arithmetic and copies ran while one was open for 5% of the time, Pallas kernels for 0%

commit v1 on v0

v1 whole, which is shorter than its diff:
```python
from functools import partial

import jax
import jax.numpy as jnp
from jax import lax
from jax.experimental import pallas as pl
from jax.experimental.pallas import tpu as pltpu
from jax.sharding import PartitionSpec as P

HEADS = 16
SPAN = 128
ROW_LEN = 2048
STEP = 7

first_decay = 0.5
second_decay = 0.95
adam_epsilon = 1e-08
norm_epsilon = 1e-05
matrix_shrink = 0.1
input_rate = 0.02
output_rate = 0.45
expand_rate = 0.02
reduce_rate = 0.01
gain_rate = 0.2

F32 = jnp.float32
BF16 = jnp.bfloat16

Z_STEPS = (1, 2, 3)


def swap(value, axis, mask):
    size = lax.axis_size(axis)
    return lax.ppermute(value, axis, [(i, i ^ mask) for i in range(size)])


def over_z(value, step):
    return swap(value, "fsdp", 2 * step)


def over_c(value):
    return swap(value, "mp", 1)


def over_x(value):
    return swap(value, "mp", 2)


def over_y(value):
    return swap(value, "fsdp", 1)


def outer_bits():
    bits, bit = [], 8
    while bit < lax.axis_size("fsdp"):
        bits.append(bit)
        bit *= 2
    return bits


def gather_groups(own):
    half = own.shape[0] // 2
    from_x, from_y = over_x(own), over_y(own)
    corner_one = over_y(from_x[:half])
    corner_two = over_x(from_y[half:])
    pieces = {
        (0, 0): own,
        (1, 0): from_x,
        (0, 1): from_y,
        (1, 1): jnp.concatenate([corner_one, corner_two]),
    }
    for bit in outer_bits():
        for (x, t), piece in list(pieces.items()):
            pieces[x, t + bit // 4] = swap(piece, "fsdp", bit)
    return pieces


def reduce_groups(pieces):
    pieces = dict(pieces)
    for bit in reversed(outer_bits()):
        for (x, t), piece in list(pieces.items()):
            if t & (bit // 4):
                pieces[x, t ^ (bit // 4)] = add(pieces[x, t ^ (bit // 4)], swap(piece, "fsdp", bit))
                del pieces[x, t]
    corner = pieces[1, 1]
    half = corner.shape[0] // 2
    from_y, from_x = over_y(corner[:half]), over_x(corner[half:])
    to_x = jnp.concatenate([add(pieces[1, 0][:half], from_y), pieces[1, 0][half:]])
    to_y = jnp.concatenate([pieces[0, 1][:half], add(pieces[0, 1][half:], from_x)])
    return add(pieces[0, 0], over_x(to_x), over_y(to_y))


def add(*values):
    total = values[0].astype(F32)
    for value in values[1:]:
        total = total + value.astype(F32)
    return total.astype(BF16)


def place_blocks(blocks, axis, at):
    size = blocks[0].shape[axis]
    shape = list(blocks[0].shape)
    shape[axis] *= 4
    whole = jnp.zeros(shape, blocks[0].dtype)
    for step, block in enumerate(blocks):
        whole = lax.dynamic_update_slice_in_dim(whole, block, (at ^ step) * size, axis)
    return whole


def exchange_z(take, axis, at):
    blocks = [take(at)] + [over_z(take(at ^ step), step) for step in Z_STEPS]
    return place_blocks(blocks, axis, at)


def gather_tokens(own):
    mine = jnp.concatenate([own] + [over_z(own, step) for step in Z_STEPS])
    return jnp.concatenate([mine, over_c(mine)])


def scatter_tokens(partial_sums):
    half = partial_sums.shape[0] // 2
    mine = add(partial_sums[:half], over_c(partial_sums[half:]))
    quarter = half // 4
    total = mine[:quarter].astype(F32)
    for step in Z_STEPS:
        total = total + over_z(mine[step * quarter : (step + 1) * quarter], step).astype(F32)
    return total


def normalize(values):
    centre = jnp.mean(values, axis=-1, keepdims=True)
    centred = values - centre
    spread = jnp.mean(centred * centred, axis=-1, keepdims=True)
    scale = lax.rsqrt(spread + norm_epsilon)
    return centred * scale, scale


def norm_back(shape, scale, gain, grad):
    weighted = grad * gain
    back = (
        weighted
        - jnp.mean(weighted, axis=-1, keepdims=True)
        - shape * jnp.mean(weighted * shape, axis=-1, keepdims=True)
    ) * scale
    return back, jnp.sum(grad * shape, axis=0), jnp.sum(grad, axis=0)


def adamw_update(master, moment_one, moment_two, gradient, step_rate, shrink_rate):
    moment_one = first_decay * moment_one + (1.0 - first_decay) * gradient
    moment_two = second_decay * moment_two + (1.0 - second_decay) * gradient * gradient
    mean_part = moment_one / (1.0 - first_decay**STEP)
    square_part = moment_two / (1.0 - second_decay**STEP)
    updated = master - step_rate * (
        mean_part / (jnp.sqrt(square_part) + adam_epsilon) + shrink_rate * master
    )
    return (moment_one, moment_two, updated)


def dot(left, right, dims=((1,), (0,))):
    return lax.dot_general(left, right, (dims, ((), ())), preferred_element_type=F32)


ROWS_BY_ROWS = ((0,), (0,))
COLS_BY_COLS = ((1,), (1,))


def visible(query_marks, key_marks):
    return (query_marks[:, 0:1] == key_marks[0:1, :]) & (key_marks[1:2, :] <= query_marks[:, 1:2])


def attend_kernel(scaling, q_ref, kv_ref, qm_ref, km_ref, out_ref, low_ref, lse_ref):
    head = q_ref.shape[1]
    keys, values = kv_ref[0, :, :head], kv_ref[0, :, head:]
    scores = dot(q_ref[...], keys, COLS_BY_COLS) * scaling
    scores = jnp.where(visible(qm_ref[...], km_ref[...]), scores, -1e30)
    largest = jnp.max(scores, axis=1, keepdims=True)
    weights = jnp.exp(scores - largest)
    totals = jnp.sum(weights, axis=1, keepdims=True)
    probs = (weights * (1.0 / totals)).astype(BF16)
    attended = dot(probs, values)
    out_ref[...] = attended
    low_ref[...] = attended.astype(BF16)
    lse_ref[0] = largest + jnp.log(totals)


def attend_back_kernel(
    scaling, q_ref, kv_ref, qm_ref, km_ref, out_ref, lse_ref, grad_ref, dq_ref, dkv_ref, total_ref
):
    head = q_ref.shape[1]
    keys, values = kv_ref[0, :, :head], kv_ref[0, :, head:]
    grad = grad_ref[...]
    row_dots = jnp.sum(grad.astype(F32) * out_ref[...], axis=1, keepdims=True)
    scores = dot(q_ref[...], keys, COLS_BY_COLS) * scaling
    scores = jnp.where(visible(qm_ref[...], km_ref[...]), scores, -1e30)
    probs = jnp.exp(scores - lse_ref[0])
    prob_grad = dot(grad, values, COLS_BY_COLS)
    score_grad = (probs * (prob_grad - row_dots)).astype(BF16)
    dq_ref[...] = (dot(score_grad, keys) * scaling).astype(BF16)
    key_grad = dot(score_grad, q_ref[...], ROWS_BY_ROWS) * scaling
    value_grad = dot(probs.astype(BF16), grad, ROWS_BY_ROWS)
    both = jnp.concatenate([key_grad, value_grad], axis=1)
    step, last = pl.program_id(1), pl.num_programs(1) - 1

    @pl.when(step == 0)
    def _():
        total_ref[...] = both

    @pl.when(step > 0)
    def _():
        total_ref[...] += both

    @pl.when(step == last)
    def _():
        dkv_ref[0] = total_ref[...].astype(BF16)


BLOCK = 256


def attend(qkv, kv, query_marks, key_marks, scaling):
    heads, length, pair = kv.shape
    head, count = pair // 2, qkv.shape[0]
    return pl.pallas_call(
        partial(attend_kernel, scaling),
        grid=(heads, count // BLOCK),
        in_specs=[
            pl.BlockSpec((BLOCK, head), lambda h, i: (i, 3 * h)),
            pl.BlockSpec((1, length, pair), lambda h, i: (h, 0, 0)),
            pl.BlockSpec((BLOCK, 2), lambda h, i: (i, 0)),
            pl.BlockSpec((2, length), lambda h, i: (0, 0)),
        ],
        out_specs=[
            pl.BlockSpec((BLOCK, head), lambda h, i: (i, h)),
            pl.BlockSpec((BLOCK, head), lambda h, i: (i, h)),
            pl.BlockSpec((1, BLOCK, 1), lambda h, i: (h, i, 0)),
        ],
        out_shape=[
            jax.ShapeDtypeStruct((count, heads * head), F32),
            jax.ShapeDtypeStruct((count, heads * head), BF16),
            jax.ShapeDtypeStruct((heads, count, 1), F32),
        ],
        compiler_params=pltpu.CompilerParams(vmem_limit_bytes=48 << 20),
        name="attend",
    )(qkv, kv, query_marks, key_marks)


def attend_back(qkv, kv, query_marks, key_marks, attended, logsum, grad, scaling):
    heads, length, pair = kv.shape
    head, count = pair // 2, qkv.shape[0]
    block = BLOCK if length <= 2048 else 128
    return pl.pallas_call(
        partial(attend_back_kernel, scaling),
        grid=(heads, count // block),
        in_specs=[
            pl.BlockSpec((block, head), lambda h, i: (i, 3 * h)),
            pl.BlockSpec((1, length, pair), lambda h, i: (h, 0, 0)),
            pl.BlockSpec((block, 2), lambda h, i: (i, 0)),
            pl.BlockSpec((2, length), lambda h, i: (0, 0)),
            pl.BlockSpec((block, head), lambda h, i: (i, h)),
            pl.BlockSpec((1, block, 1), lambda h, i: (h, i, 0)),
            pl.BlockSpec((block, head), lambda h, i: (i, h)),
        ],
        out_specs=[
            pl.BlockSpec((block, head), lambda h, i: (i, h)),
            pl.BlockSpec((1, length, pair), lambda h, i: (h, 0, 0)),
        ],
        out_shape=[
            jax.ShapeDtypeStruct((count, heads * head), BF16),
            jax.ShapeDtypeStruct((heads, length, pair), BF16),
        ],
        scratch_shapes=[pltpu.VMEM((length, pair), F32)],
        compiler_params=pltpu.CompilerParams(vmem_limit_bytes=56 << 20),
        name="attend_back",
    )(qkv, kv, query_marks, key_marks, attended, logsum, grad)


def local(
    tokens,
    cotangent,
    segment_ids,
    span_map,
    norm_params,
    norm_first,
    norm_second,
    attention_input,
    attention_input_first,
    attention_input_second,
    attention_output,
    attention_output_first,
    attention_output_second,
    expand_weight,
    expand_first,
    expand_second,
    reduce_weight,
    reduce_first,
    reduce_second,
):
    width = tokens.shape[1]
    devices, lanes = lax.axis_size("fsdp"), lax.axis_size("mp")
    head = width // HEADS
    scaling = head ** (-0.5)
    shard = width // devices
    strip = 4 * shard
    outer = devices // 8
    groups = 2 * outer
    spot, lane = lax.axis_index("fsdp"), lax.axis_index("mp")
    at = (spot // 2) % 4
    group_at = (spot // 8) * 2 + spot % 2
    piece = tokens.shape[0] // lanes
    units = expand_weight.shape[1] // 4

    def to_relative(value):
        rows = value.shape[0]
        value = value.reshape(rows, outer, 4, 2, shard).transpose(0, 1, 3, 2, 4)
        value = value.reshape(rows, groups, strip)
        return jnp.concatenate(
            [
                lax.dynamic_index_in_dim(value, group_at ^ t, 1, keepdims=False)
                for t in range(groups)
            ],
            axis=1,
        )

    def to_natural(value):
        rows = value.shape[0]
        value = value.reshape(rows, groups, strip)
        value = jnp.stack(
            [
                lax.dynamic_index_in_dim(value, group_at ^ t, 1, keepdims=False)
                for t in range(groups)
            ],
            axis=1,
        )
        value = value.reshape(rows, outer, 2, 4, shard).transpose(0, 1, 3, 2, 4)
        return value.reshape(rows, width)

    def by_group(value):
        return [value[:, t * strip : (t + 1) * strip] for t in range(groups)]

    def own_rows(value):
        return lax.dynamic_slice_in_dim(value, lane * piece, piece, 0)

    def all_lanes(value):
        pair = jnp.stack([value, over_x(value)])
        four = jnp.stack([pair, over_c(pair)], axis=1)
        four = jnp.where(lane >= 2, four[::-1], four)
        four = jnp.where(lane % 2 == 1, four[:, ::-1], four)
        return four.reshape((4 * value.shape[0],) + value.shape[1:])

    input_own = exchange_z(
        lambda i: jnp.concatenate(
            [
                lax.dynamic_slice_in_dim(attention_input[:, kind], i * head, head, 1).astype(BF16)
                for kind in range(3)
            ],
            axis=1,
        ),
        0,
        at,
    )
    input_low = gather_groups(input_own)
    own_tokens = to_relative(own_rows(tokens))
    own_cotangent = to_relative(own_rows(cotangent))
    group_tokens = gather_tokens(own_tokens)
    output_own = exchange_z(
        lambda i: lax.dynamic_slice_in_dim(attention_output, i * head, head, 0).astype(BF16), 1, at
    )
    output_low = gather_groups(output_own)
    expand_own = exchange_z(
        lambda i: lax.dynamic_slice_in_dim(expand_weight, i * units, units, 1).astype(BF16), 0, at
    )
    expand_low = gather_groups(expand_own)
    reduce_own = exchange_z(
        lambda i: lax.dynamic_slice_in_dim(reduce_weight, i * units, units, 0).astype(BF16), 1, at
    )
    reduce_low = gather_groups(reduce_own)
    group_cotangent = gather_tokens(own_cotangent)

    norm_low = norm_params.astype(BF16)[None]
    norm_low = jnp.concatenate([norm_low, over_y(norm_low)])
    for bit in outer_bits():
        norm_low = jnp.concatenate([norm_low, swap(norm_low, "fsdp", bit)])
    norm_low = jnp.stack([norm_low] + [over_z(norm_low, step) for step in Z_STEPS], axis=1)
    norm_low = jnp.where(at % 2 == 1, norm_low[:, jnp.array([1, 0, 3, 2])], norm_low)
    norm_low = jnp.where(at >= 2, norm_low[:, jnp.array([2, 3, 0, 1])], norm_low)
    norm_values = norm_low.transpose(2, 0, 1, 3).reshape(4, width).astype(F32)

    places = (
        span_map[:, None] % (ROW_LEN // SPAN) * SPAN + jnp.arange(SPAN, dtype=jnp.int32)[None, :]
    ).reshape(-1)
    marks = jnp.stack([segment_ids, places]).reshape(2, 1, 2, 2, piece)
    marks = jnp.where(lane >= 2, marks[:, :, ::-1], marks)
    marks = jnp.where(lane % 2 == 1, marks[:, :, :, ::-1], marks)
    marks = jnp.stack([marks, over_y(marks)])
    for bit in outer_bits():
        marks = jnp.concatenate([marks, swap(marks, "fsdp", bit)])
    marks = jnp.concatenate([marks, over_z(marks, 1)], axis=2)
    marks = jnp.concatenate([marks, over_z(marks, 2)], axis=2)
    marks = marks.transpose(1, 0, 3, 4, 2, 5)
    query_marks = marks[:, 0, 0].reshape(2, -1).T
    key_marks = marks.reshape(2, -1)

    features = group_tokens.astype(F32)
    normed_one = (normalize(features)[0] * norm_values[0] + norm_values[1]).astype(BF16)
    input_full = jnp.concatenate(
        [
            jnp.concatenate([input_low[x, t] for x in range(2)], axis=1)
            for t in range(groups)
        ],
        axis=0,
    )
    qkv = dot(normed_one, input_full).astype(BF16)
    count = qkv.shape[0]
    own_kv = jnp.stack(
        [qkv[:, 3 * x * head + head : 3 * x * head + 3 * head] for x in range(2)]
    ).reshape(2 * count, 2 * head)
    kv_low = gather_groups(own_kv)
    order = [(x, t) for t in range(groups) for x in range(2)]
    kv = jnp.stack(
        [
            jnp.concatenate(
                [kv_low[x, t][(h ^ x) * count : ((h ^ x) + 1) * count] for x, t in order]
            )
            for h in range(2)
        ]
    )
    attended, mixed, logsum = attend(qkv, kv, query_marks, key_marks, scaling)
    output_full = jnp.concatenate(
        [
            jnp.concatenate([output_low[x, t] for t in range(groups)], axis=1)
            for x in range(2)
        ],
        axis=0,
    )
    branch = scatter_tokens(dot(mixed, output_full).astype(BF16))
    middle = own_tokens.astype(F32) + branch

    shape_two, scale_two = normalize(middle)
    normed_two = gather_tokens((shape_two * norm_values[2] + norm_values[3]).astype(BF16))
    expand_full = jnp.concatenate(
        [
            jnp.concatenate([expand_low[x, t] for x in range(2)], axis=1)
            for t in range(groups)
        ],
        axis=0,
    )
    reduce_full = jnp.concatenate(
        [
            jnp.concatenate([reduce_low[x, t] for t in range(groups)], axis=1)
            for x in range(2)
        ],
        axis=0,
    )
    hidden = dot(normed_two, expand_full)
    active_wide, gelu_pull = jax.vjp(partial(jax.nn.gelu, approximate=True), hidden)
    active = active_wide.astype(BF16)
    feed = scatter_tokens(dot(active, reduce_full).astype(BF16))
    output = all_lanes(to_natural((middle + feed).astype(BF16)))

    active_grad = dot(group_cotangent, reduce_full, COLS_BY_COLS)
    hidden_grad = gelu_pull(active_grad)[0].astype(BF16)
    second_grad = scatter_tokens(dot(hidden_grad, expand_full, COLS_BY_COLS).astype(BF16))
    middle_part, gain_two, bias_two = norm_back(shape_two, scale_two, norm_values[2], second_grad)
    middle_grad = own_cotangent.astype(F32) + middle_part
    branch_grad = gather_tokens(middle_grad.astype(BF16))

    mixed_grad = dot(branch_grad, output_full, COLS_BY_COLS).astype(BF16)
    query_grad, kv_grad = attend_back(
        qkv, kv, query_marks, key_marks, attended, logsum, mixed_grad, scaling
    )
    kv_pieces = {}
    for i, (x, t) in enumerate(order):
        part = kv_grad[:, i * count : (i + 1) * count]
        kv_pieces[x, t] = jnp.concatenate([part[x], part[1 - x]])
    own_kv_grad = reduce_groups(kv_pieces)
    qkv_grad = jnp.concatenate(
        [
            block
            for x in range(2)
            for block in (
                query_grad[:, x * head : (x + 1) * head],
                own_kv_grad[x * count : (x + 1) * count],
            )
        ],
        axis=1,
    )
    first_grad = scatter_tokens(dot(qkv_grad, input_full, COLS_BY_COLS).astype(BF16))
    shape_one, scale_one = normalize(own_tokens.astype(F32))
    input_part, gain_one, bias_one = norm_back(shape_one, scale_one, norm_values[0], first_grad)
    input_grad = all_lanes(to_natural((middle_grad + input_part).astype(BF16))).astype(F32)

    def matrix_grad(left, right, left_size, left_by_group):
        whole = dot(left, right, ROWS_BY_ROWS).astype(BF16)
        pieces = {}
        for x in range(2):
            for t in range(groups):
                i, j = (t, x) if left_by_group else (x, t)
                rows = whole[i * left_size : (i + 1) * left_size]
                size = rows.shape[1] // (2 if left_by_group else groups)
                pieces[x, t] = rows[:, j * size : (j + 1) * size]
        return reduce_groups(pieces)

    def slice_of(value, axis):
        size = value.shape[axis] // 4
        return lambda i: lax.dynamic_slice_in_dim(value, i * size, size, axis)

    reduce_sum = matrix_grad(active, group_cotangent, units, False)
    share_reduce = exchange_z(slice_of(reduce_sum, 1), 0, at).astype(F32)
    expand_sum = matrix_grad(normed_two, hidden_grad, strip, True)
    share_expand = exchange_z(slice_of(expand_sum, 0), 1, at).astype(F32)
    output_sum = matrix_grad(mixed, branch_grad, head, False)
    share_output = exchange_z(slice_of(output_sum, 1), 0, at).astype(F32)
    input_sum = matrix_grad(normed_one, qkv_grad, strip, True)
    input_blocks = [slice_of(input_sum, 0)(at)] + [
        over_z(slice_of(input_sum, 0)(at ^ step), step) for step in Z_STEPS
    ]
    share_input = place_blocks(
        [block.reshape(shard, 3, head) for block in input_blocks], 2, at
    ).astype(F32)

    norm_sum = jnp.stack([gain_one, bias_one, gain_two, bias_two]).reshape(4, groups, strip)
    own_norm = norm_sum[:, 0]
    for t in range(1, groups):
        mask = (t // 2) * 8 + t % 2
        own_norm = own_norm + swap(norm_sum[:, t], "fsdp", mask)
    share_norm = slice_of(own_norm, 1)(at)
    for step in Z_STEPS:
        share_norm = share_norm + over_z(slice_of(own_norm, 1)(at ^ step), step)
    share_norm = share_norm + over_c(share_norm)
    share_norm = share_norm + over_x(share_norm)

    input_new = adamw_update(
        attention_input,
        attention_input_first,
        attention_input_second,
        share_input,
        input_rate,
        matrix_shrink,
    )
    output_new = adamw_update(
        attention_output,
        attention_output_first,
        attention_output_second,
        share_output,
        output_rate,
        matrix_shrink,
    )
    expand_new = adamw_update(
        expand_weight, expand_first, expand_second, share_expand, expand_rate, matrix_shrink
    )
    reduce_new = adamw_update(
        reduce_weight, reduce_first, reduce_second, share_reduce, reduce_rate, matrix_shrink
    )
    norm_new = adamw_update(norm_params, norm_first, norm_second, share_norm, gain_rate, 0.0)
    return (
        output,
        input_grad,
        *input_new,
        input_new[2].astype(BF16),
        *output_new,
        output_new[2].astype(BF16),
        *expand_new,
        expand_new[2].astype(BF16),
        *reduce_new,
        reduce_new[2].astype(BF16),
        *norm_new,
    )


def solution(mesh):
    rows, vectors, norms = P("fsdp", None), P("fsdp"), P(None, "fsdp")
    cube, across, down = P("fsdp", None, "mp"), P("fsdp", "mp"), P("mp", "fsdp")
    return jax.shard_map(
        local,
        mesh=mesh,
        in_specs=(
            (rows, rows, vectors, vectors)
            + (norms,) * 3
            + (cube,) * 3
            + (down,) * 3
            + (across,) * 3
            + (down,) * 3
        ),
        out_specs=(
            (rows, rows) + (cube,) * 4 + (down,) * 4 + (across,) * 4 + (down,) * 4 + (norms,) * 3
        ),
        check_vma=False,
    )
```

time: 1400 us -> 620 us (0.44)
  waiting for transfers between devices: 1150 us -> 237 us
  starting transfers between devices: 1.72 us -> 186 us
  blocking collectives: 47.2 us -> 0 us
  matrix products: 86.7 us -> 66.6 us
  Pallas kernels: 0 us -> 18.3 us
    reduce_scatter x5 -> x0, waiting for transfers between devices: 543 us -> none  [the longest x1 150 us: local(): lax.psum_scatter(grad_expand.astype(jnp.bfloat16), 'fsdp', scatter_dimens...]
    all_gather x6 -> x0, waiting for transfers between devices: 428 us -> none  [the longest x1 124 us: local(): lax.all_gather(expand_low, 'fsdp', axis=0, tiled=True)]
    ppermute x0 -> x113, waiting for transfers between devices: none -> 237 us  [swap(): return lax.ppermute(value, axis, [(i, i ^ mask) for i in range(size)])]
    ppermute x0 -> x113, starting transfers between devices: none -> 186 us  [swap(): return lax.ppermute(value, axis, [(i, i ^ mask) for i in range(size)])]
    psum x3 -> x0, waiting for transfers between devices: 116 us -> none  [the longest x1 46.9 us: local(): lax.psum(jnp.dot(active, reduce_full, preferred_element_type=jnp.float32)...]
    unnamed x16 -> x0, waiting for transfers between devices: 58.5 us -> none
    all_gather x3 -> x0, blocking collectives: 47.2 us -> none  [the longest x1 20.4 us: local(): lax.all_gather(norm_low, 'fsdp', axis=1, tiled=True)]
    dot_general x18 -> x12, matrix products: 86.7 us -> 66.6 us  [dot(): lax.dot_general(left, right, (dims, ((), ())), preferred_element_type=F32)]
  transfers between devices with their start and end apart: 15 -> 113, of which waited for: 15 -> 48; matrix products, arithmetic and copies ran while one was open for 5% -> 18% of each run, Pallas kernels for 0% -> 3%
where the time goes in v1:
time: 620 us; the launch traced here: 610 us
  waiting for transfers between devices  237 us (38%)
  starting transfers between devices  186 us (30%)
  matrix products  66.6 us (11%)
  other arithmetic  57.9 us (9%)
  local copies, waits for them, and re-layouts  40.7 us (7%)
  Pallas kernels  18.3 us (3%)
    ppermute x113, waiting for transfers between devices, swap(): return lax.ppermute(value, axis, [(i, i ^ mask) for i in range(size)])  237 us
    ppermute x113, starting transfers between devices, swap(): return lax.ppermute(value, axis, [(i, i ^ mask) for i in range(size)])  186 us
    dot_general x12, matrix products, dot(): lax.dot_general(left, right, (dims, ((), ())), preferred_element_type=F32)  66.6 us
  transfers between devices with their start and end apart: 113, of which 48 were waited for; matrix products, arithmetic and copies ran while one was open for 18% of the time, Pallas kernels for 3%

profile of v1, /device:TPU:9, one launch (start us, length us, event | category | flops | bytes accessed | tf_op | source)
XLA Modules:
  0.0 609.5 jit_solution(10011740345212494075)
XLA Ops:
  35.4 4.2 collective-permute-done.8
  45.8 11.2 %collective-permute-start.3 = (bf16[256,2048]{1,0:T(8,128)(2,1)S(1)}, bf16[256,2048]{1,0:T(8,128)(2,1)S(1)}, u32[]{:S(2)}, u32[]{:S(2)}) collective-permute-start(bf16[256,2048]{1,0:T(8,128)(2,1)S(1)} %pad_maximum_fusion.1), channel_id=1, source_target_pairs={{0,1},{1,0},{2,3},{3,2},{4,5},{5,4},{6,7},{7,6},{8,9},{9,8},{10,11... | collective-permute-start | bytes 3145736 | tf_op jit(solution)/shard_map/ppermute | solution.py:34
  64.9 11.1 %collective-permute-done.12 = bf16[1024,384]{1,0:T(8,128)(2,1)S(1)} collective-permute-done((bf16[1024,384]{1,0:T(8,128)(2,1)}, bf16[1024,384]{1,0:T(8,128)(2,1)S(1)}, u32[]{:S(2)}, u32[]{:S(2)}) %collective-permute-start.12) | collective-permute-done | bytes 786464 | tf_op jit(solution)/shard_map/ppermute | solution.py:34
  119.0 6.1 attend.1
  128.5 8.5 %collective-permute-start.29 = (bf16[256,2048]{1,0:T(8,128)(2,1)S(1)}, bf16[256,2048]{1,0:T(8,128)(2,1)S(1)}, u32[]{:S(2)}, u32[]{:S(2)}) collective-permute-start(bf16[256,2048]{1,0:T(8,128)(2,1)S(1)} %slice.471), channel_id=1, source_target_pairs={{0,1},{1,0},{2,3},{3,2},{4,5},{5,4},{6,7},{7,6},{8,9},{9,8},{10,11... | collective-permute-start | bytes 3145736 | tf_op jit(solution)/shard_map/ppermute | solution.py:34
  141.7 5.9 collective-permute-done.44
  147.8 14.4 %collective-permute-done.45 = bf16[512,256]{1,0:T(8,128)(2,1)S(1)} collective-permute-done((bf16[512,256]{1,0:T(8,128)(2,1)S(1)}, bf16[512,256]{1,0:T(8,128)(2,1)S(1)}, u32[]{:S(2)}, u32[]{:S(2)}) %collective-permute-start.45) | collective-permute-done | bytes 262176 | tf_op jit(solution)/shard_map/ppermute | solution.py:34
  164.3 4.9 collective-permute-start.31
  169.2 28.1 %collective-permute-done.46 = bf16[512,256]{1,0:T(8,128)(2,1)S(1)} collective-permute-done((bf16[512,256]{1,0:T(8,128)(2,1)S(1)}, bf16[512,256]{1,0:T(8,128)(2,1)S(1)}, u32[]{:S(2)}, u32[]{:S(2)}) %collective-permute-start.46) | collective-permute-done | bytes 262176 | tf_op jit(solution)/shard_map/ppermute | solution.py:34
  210.6 9.1 %collective-permute-done.41 = bf16[1024,512]{1,0:T(8,128)(2,1)S(1)} collective-permute-done((bf16[1024,512]{1,0:T(8,128)(2,1)S(1)}, bf16[1024,512]{1,0:T(8,128)(2,1)S(1)}, u32[]{:S(2)}, u32[]{:S(2)}) %collective-permute-start.41) | collective-permute-done | bytes 1048608 | tf_op jit(solution)/shard_map/ppermute | solution.py:34
  222.3 19.8 %collective-permute-done.47 = bf16[512,1024]{1,0:T(8,128)(2,1)S(1)} collective-permute-done((bf16[512,1024]{1,0:T(8,128)(2,1)S(1)}, bf16[512,1024]{1,0:T(8,128)(2,1)S(1)}, u32[]{:S(2)}, u32[]{:S(2)}) %collective-permute-start.47) | collective-permute-done | bytes 1048608 | tf_op jit(solution)/shard_map/ppermute | solution.py:34
  246.0 8.1 %collective-permute-done.35 = bf16[64,2048]{1,0:T(8,128)(2,1)S(1)} collective-permute-done((bf16[64,2048]{1,0:T(8,128)(2,1)S(1)}, bf16[64,2048]{1,0:T(8,128)(2,1)S(1)}, u32[]{:S(2)}, u32[]{:S(2)}) %collective-permute-start.35) | collective-permute-done | bytes 262176 | tf_op jit(solution)/shard_map/ppermute | solution.py:34
  268.1 23.5 %fusion.12 = bf16[512,1024]{1,0:T(8,128)(2,1)S(1)} fusion(f32[512,1024]{1,0:T(8,128)S(1)} %fusion.63, bf16[512,2048]{1,0:T(8,128)(2,1)S(1)} %constant_dynamic-update-slice_fusion.10, bf16[256,1024]{1,0:T(8,128)(2,1)S(1)} %collective-permute-done.50, bf16[256,1024]{1,0:T(8,128)(2,1)S(1)} %collective-permute-done.49, ...), kind=kOutput, calls=%fused_computation.34 | convolution fusion | flops 2178940928 | bytes 9437184 | tf_op jit(solution)/shard_map/dot_general | solution.py:160
  294.0 19.9 %convolution_convert_fusion.3 = bf16[512,2048]{1,0:T(8,128)(2,1)S(1)} fusion(bf16[512,1024]{1,0:T(8,128)(2,1)S(1)} %fusion.12, bf16[512,512]{1,0:T(8,128)(2,1)S(1)} %collective-permute-done.43, bf16[512,512]{1,0:T(8,128)(2,1)S(1)} %collective-permute-done.42, bf16[1024,512]{1,0:T(8,128)(2,1)S(1)} %collective-permute-done.41, ...), kind=kOutput, calls=%fused_computation.20 | convolution fusion | flops 2169503744 | bytes 7340032 | tf_op jit(solution)/shard_map/dot_general | solution.py:160
  322.6 7.7 %collective-permute-done.93 = bf16[512,512]{1,0:T(8,128)(2,1)S(1)} collective-permute-done((bf16[512,512]{1,0:T(8,128)(2,1)S(1)}, bf16[512,512]{1,0:T(8,128)(2,1)S(1)}, u32[]{:S(2)}, u32[]{:S(2)}) %collective-permute-start.93) | collective-permute-done | bytes 524320 | tf_op jit(solution)/shard_map/ppermute | solution.py:34
  332.8 8.7 %collective-permute-done.100 = bf16[256,1024]{1,0:T(8,128)(2,1)S(1)} collective-permute-done((bf16[256,1024]{1,0:T(8,128)(2,1)S(1)}, bf16[256,1024]{1,0:T(8,128)(2,1)S(1)}, u32[]{:S(2)}, u32[]{:S(2)}) %collective-permute-start.100) | collective-permute-done | bytes 524320 | tf_op jit(solution)/shard_map/ppermute | solution.py:34
  351.8 9.3 %collective-permute-done.64 = bf16[64,2048]{1,0:T(8,128)(2,1)S(1)} collective-permute-done((bf16[64,2048]{1,0:T(8,128)(2,1)S(1)}, bf16[64,2048]{1,0:T(8,128)(2,1)S(1)}, u32[]{:S(2)}, u32[]{:S(2)}) %collective-permute-start.64) | collective-permute-done | bytes 262176 | tf_op jit(solution)/shard_map/ppermute | solution.py:34
  363.1 13.2 %collective-permute-done.63 = bf16[64,2048]{1,0:T(8,128)(2,1)S(1)} collective-permute-done((bf16[64,2048]{1,0:T(8,128)(2,1)S(1)}, bf16[64,2048]{1,0:T(8,128)(2,1)S(1)}, u32[]{:S(2)}, u32[]{:S(2)}) %collective-permute-start.63) | collective-permute-done | bytes 262176 | tf_op jit(solution)/shard_map/ppermute | solution.py:34
  377.8 6.1 collective-permute-done.54
  403.6 15.6 %collective-permute-done.103 = bf16[512,1024]{1,0:T(8,128)(2,1)} collective-permute-done((bf16[512,1024]{1,0:T(8,128)(2,1)}, bf16[512,1024]{1,0:T(8,128)(2,1)}, u32[]{:S(2)}, u32[]{:S(2)}) %collective-permute-start.103) | collective-permute-done | bytes 1048608 | tf_op jit(solution)/shard_map/ppermute | solution.py:34
  433.7 18.3 %collective-permute-start.56 = (bf16[2,64,2048]{2,1,0:T(8,128)(2,1)S(1)}, bf16[2,64,2048]{2,1,0:T(8,128)(2,1)S(1)}, u32[]{:S(2)}, u32[]{:S(2)}) collective-permute-start(bf16[2,64,2048]{2,1,0:T(8,128)(2,1)S(1)} %get-tuple-element.143), channel_id=1, source_target_pairs={{0,1},{1,0},{2,3},{3,2},{4,5},{5,4},{6,7},{7,6},{8,9},{9,8},{10,11... | collective-permute-start | bytes 1572872 | tf_op jit(solution)/shard_map/ppermute | solution.py:34
  452.0 14.7 %collective-permute-start.68 = (bf16[256,2048]{1,0:T(8,128)(2,1)S(1)}, bf16[256,2048]{1,0:T(8,128)(2,1)S(1)}, u32[]{:S(2)}, u32[]{:S(2)}) collective-permute-start(bf16[256,2048]{1,0:T(8,128)(2,1)S(1)} %pad_maximum_fusion.5), channel_id=1, source_target_pairs={{0,1},{1,0},{2,3},{3,2},{4,5},{5,4},{6,7},{7,6},{8,9},{9,8},{10,11... | collective-permute-start | bytes 3145736 | tf_op jit(solution)/shard_map/ppermute | solution.py:34
  466.9 5.4 fusion.69
  472.4 5.2 fusion.67
  483.8 12.2 %attend_back.1 = (bf16[512,256]{1,0:T(8,128)(2,1)}, bf16[2,2048,256]{2,1,0:T(8,128)(2,1)}) custom-call(bf16[512,768]{1,0:T(8,128)(2,1)} %copy-done.1, bf16[2,2048,256]{2,1,0:T(8,128)(2,1)} %copy-done, s32[512,2]{1,0:T(8,128)} %bitcast.152, s32[2,2048]{1,0:T(2,128)} %copy-done.5, f32[512,256]{1,0:T(8,128)} %copy-done.3, f32[2,512,1]{2,1,0:T(8,128)} %copy-done.4, ...), custom_call_target="tpu_custom_call" | custom-call | tf_op jit(solution)/shard_map/attend_back/pallas_call | solution.py:251
  514.0 5.1 collective-permute-done.72
  525.1 4.3 collective-permute-start.73
  532.6 7.7 %collective-permute-done.79 = bf16[512,384]{0,1:T(8,128)(2,1)S(1)} collective-permute-done((bf16[512,384]{0,1:T(8,128)(2,1)S(1)}, bf16[512,384]{0,1:T(8,128)(2,1)S(1)}, u32[]{:S(2)}, u32[]{:S(2)}) %collective-permute-start.79) | collective-permute-done | bytes 393248 | tf_op jit(solution)/shard_map/ppermute | solution.py:34
  547.0 12.0 %collective-permute-done.82 = bf16[1024,384]{0,1:T(8,128)(2,1)S(1)} collective-permute-done((bf16[1024,384]{0,1:T(8,128)(2,1)S(1)}, bf16[1024,384]{0,1:T(8,128)(2,1)S(1)}, u32[]{:S(2)}, u32[]{:S(2)}) %collective-permute-start.82) | collective-permute-done | bytes 786464 | tf_op jit(solution)/shard_map/ppermute | solution.py:34
  564.2 5.9 collective-permute-done.75
  576.8 5.3 collective-permute-start.109
  601.7 5.4 fusion.73
  (591 shorter events, 269.3 us)
Async XLA Ops:
  3.1 40.2 %collective-permute-start = (bf16[64,2048]{1,0:T(8,128)(2,1)}, bf16[64,2048]{1,0:T(8,128)(2,1)}, u32[]{:S(2)}, u32[]{:S(2)}) collective-permute-start(bf16[64,2048]{1,0:T(8,128)(2,1)} %get-tuple-element.167), channel_id=1, source_target_pairs={{0,8},{4,12},{8,0},{12,4},{16,24},{20,28},{24,16},{28,20},{1,9},{5... | collective-permute-start | bytes 786440 | tf_op jit(solution)/shard_map/ppermute | solution.py:34
  3.1 41.6 %collective-permute-start.1 = (bf16[64,2048]{1,0:T(8,128)(2,1)}, bf16[64,2048]{1,0:T(8,128)(2,1)}, u32[]{:S(2)}, u32[]{:S(2)}) collective-permute-start(bf16[64,2048]{1,0:T(8,128)(2,1)} %get-tuple-element.167), channel_id=1, source_target_pairs={{0,16},{4,20},{8,24},{12,28},{16,0},{20,4},{24,8},{28,12},{1,17},{... | collective-permute-start | bytes 786440 | tf_op jit(solution)/shard_map/ppermute | solution.py:34
  43.3 50.9 %collective-permute-start.22 = (bf16[128,256]{1,0:T(8,128)(2,1)}, bf16[128,256]{1,0:T(8,128)(2,1)S(1)}, u32[]{:S(2)}, u32[]{:S(2)}) collective-permute-start(bf16[128,256]{1,0:T(8,128)(2,1)} %get-tuple-element.146), channel_id=1, source_target_pairs={{0,8},{4,12},{8,0},{12,4},{16,24},{20,28},{24,16},{28,20},{1,9},{5... | collective-permute-start | bytes 196616 | tf_op jit(solution)/shard_map/ppermute | solution.py:34
  44.7 51.5 %collective-permute-start.23 = (bf16[128,256]{1,0:T(8,128)(2,1)}, bf16[128,256]{1,0:T(8,128)(2,1)S(1)}, u32[]{:S(2)}, u32[]{:S(2)}) collective-permute-start(bf16[128,256]{1,0:T(8,128)(2,1)} %get-tuple-element.145), channel_id=1, source_target_pairs={{0,16},{4,20},{8,24},{12,28},{16,0},{20,4},{24,8},{28,12},{1,17},{... | collective-permute-start | bytes 196616 | tf_op jit(solution)/shard_map/ppermute | solution.py:34
  45.8 34.8 %collective-permute-start.3 = (bf16[256,2048]{1,0:T(8,128)(2,1)S(1)}, bf16[256,2048]{1,0:T(8,128)(2,1)S(1)}, u32[]{:S(2)}, u32[]{:S(2)}) collective-permute-start(bf16[256,2048]{1,0:T(8,128)(2,1)S(1)} %pad_maximum_fusion.1), channel_id=1, source_target_pairs={{0,1},{1,0},{2,3},{3,2},{4,5},{5,4},{6,7},{7,6},{8,9},{9,8},{10,11... | collective-permute-start | bytes 3145736 | tf_op jit(solution)/shard_map/ppermute | solution.py:34
  93.8 43.2 %collective-permute-start.37 = (bf16[256,512]{1,0:T(8,128)(2,1)}, bf16[256,512]{1,0:T(8,128)(2,1)}, u32[]{:S(2)}, u32[]{:S(2)}) collective-permute-start(bf16[256,512]{1,0:T(8,128)(2,1)} %get-tuple-element.93), channel_id=1, source_target_pairs={{0,8},{4,12},{8,0},{12,4},{16,24},{20,28},{24,16},{28,20},{1,9},{5... | collective-permute-start | bytes 786440 | tf_op jit(solution)/shard_map/ppermute | solution.py:34
  108.4 30.7 %collective-permute-start.38 = (bf16[256,512]{1,0:T(8,128)(2,1)}, bf16[256,512]{1,0:T(8,128)(2,1)S(1)}, u32[]{:S(2)}, u32[]{:S(2)}) collective-permute-start(bf16[256,512]{1,0:T(8,128)(2,1)} %get-tuple-element.92), channel_id=1, source_target_pairs={{0,16},{4,20},{8,24},{12,28},{16,0},{20,4},{24,8},{28,12},{1,17},{... | collective-permute-start | bytes 786440 | tf_op jit(solution)/shard_map/ppermute | solution.py:34
  109.9 30.1 %collective-permute-start.39 = (bf16[256,512]{1,0:T(8,128)(2,1)}, bf16[256,512]{1,0:T(8,128)(2,1)S(1)}, u32[]{:S(2)}, u32[]{:S(2)}) collective-permute-start(bf16[256,512]{1,0:T(8,128)(2,1)} %get-tuple-element.91), channel_id=1, source_target_pairs={{0,24},{4,28},{8,16},{12,20},{16,8},{20,12},{24,0},{28,4},{1,25},{... | collective-permute-start | bytes 786440 | tf_op jit(solution)/shard_map/ppermute | solution.py:34
  125.2 37.7 %collective-permute-start.57 = (bf16[64,2048]{1,0:T(8,128)(2,1)S(1)}, bf16[64,2048]{1,0:T(8,128)(2,1)S(1)}, u32[]{:S(2)}, u32[]{:S(2)}) collective-permute-start(bf16[64,2048]{1,0:T(8,128)(2,1)S(1)} %copy-done.32), channel_id=1, source_target_pairs={{0,8},{4,12},{8,0},{12,4},{16,24},{20,28},{24,16},{28,20},{1,9},{5... | collective-permute-start | bytes 786440 | tf_op jit(solution)/shard_map/ppermute | solution.py:34
  128.5 34.5 %collective-permute-start.29 = (bf16[256,2048]{1,0:T(8,128)(2,1)S(1)}, bf16[256,2048]{1,0:T(8,128)(2,1)S(1)}, u32[]{:S(2)}, u32[]{:S(2)}) collective-permute-start(bf16[256,2048]{1,0:T(8,128)(2,1)S(1)} %slice.471), channel_id=1, source_target_pairs={{0,1},{1,0},{2,3},{3,2},{4,5},{5,4},{6,7},{7,6},{8,9},{9,8},{10,11... | collective-permute-start | bytes 3145736 | tf_op jit(solution)/shard_map/ppermute | solution.py:34
  140.0 57.4 %collective-permute-start.58 = (bf16[64,2048]{1,0:T(8,128)(2,1)S(1)}, bf16[64,2048]{1,0:T(8,128)(2,1)S(1)}, u32[]{:S(2)}, u32[]{:S(2)}) collective-permute-start(bf16[64,2048]{1,0:T(8,128)(2,1)S(1)} %copy-done.32), channel_id=1, source_target_pairs={{0,16},{4,20},{8,24},{12,28},{16,0},{20,4},{24,8},{28,12},{1,17},{... | collective-permute-start | bytes 786440 | tf_op jit(solution)/shard_map/ppermute | solution.py:34
  147.5 50.8 %collective-permute-start.59 = (bf16[64,2048]{1,0:T(8,128)(2,1)S(1)}, bf16[64,2048]{1,0:T(8,128)(2,1)S(1)}, u32[]{:S(2)}, u32[]{:S(2)}) collective-permute-start(bf16[64,2048]{1,0:T(8,128)(2,1)S(1)} %copy-done.32), channel_id=1, source_target_pairs={{0,24},{4,28},{8,16},{12,20},{16,8},{20,12},{24,0},{28,4},{1,25},{... | collective-permute-start | bytes 786440 | tf_op jit(solution)/shard_map/ppermute | solution.py:34
  162.2 35.1 %collective-permute-start.46 = (bf16[512,256]{1,0:T(8,128)(2,1)S(1)}, bf16[512,256]{1,0:T(8,128)(2,1)S(1)}, u32[]{:S(2)}, u32[]{:S(2)}) collective-permute-start(bf16[512,256]{1,0:T(8,128)(2,1)S(1)} %copy-done.35), channel_id=1, source_target_pairs={{0,24},{4,28},{8,16},{12,20},{16,8},{20,12},{24,0},{28,4},{1,25},{... | collective-permute-start | bytes 786440 | tf_op jit(solution)/shard_map/ppermute | solution.py:34
  163.4 39.5 %collective-permute-start.32 = (bf16[64,2048]{1,0:T(8,128)(2,1)S(1)}, bf16[64,2048]{1,0:T(8,128)(2,1)S(1)}, u32[]{:S(2)}, u32[]{:S(2)}) collective-permute-start(bf16[64,2048]{1,0:T(8,128)(2,1)S(1)} %get-tuple-element.126), channel_id=1, source_target_pairs={{0,24},{4,28},{8,16},{12,20},{16,8},{20,12},{24,0},{28,4},{1,25},{... | collective-permute-start | bytes 786440 | tf_op jit(solution)/shard_map/ppermute | solution.py:34
  164.3 42.9 %collective-permute-start.31 = (bf16[64,2048]{1,0:T(8,128)(2,1)S(1)}, bf16[64,2048]{1,0:T(8,128)(2,1)S(1)}, u32[]{:S(2)}, u32[]{:S(2)}) collective-permute-start(bf16[64,2048]{1,0:T(8,128)(2,1)S(1)} %get-tuple-element.127), channel_id=1, source_target_pairs={{0,16},{4,20},{8,24},{12,28},{16,0},{20,4},{24,8},{28,12},{1,17},{... | collective-permute-start | bytes 786440 | tf_op jit(solution)/shard_map/ppermute | solution.py:34
  202.9 39.2 %collective-permute-start.47 = (bf16[512,1024]{1,0:T(8,128)(2,1)S(1)}, bf16[512,1024]{1,0:T(8,128)(2,1)S(1)}, u32[]{:S(2)}, u32[]{:S(2)}) collective-permute-start(bf16[512,1024]{1,0:T(8,128)(2,1)S(1)} %constant_dynamic-update-slice_fusion.33), channel_id=1, source_target_pairs={{0,4},{4,0},{8,12},{12,8},{16,20},{20,16},{24,28},{28,24},{1,5},{5... | collective-permute-start | bytes 3145736 | tf_op jit(solution)/shard_map/ppermute | solution.py:34
  207.2 36.5 %collective-permute-start.48 = (bf16[512,1024]{1,0:T(8,128)(2,1)S(1)}, bf16[512,1024]{1,0:T(8,128)(2,1)S(1)}, u32[]{:S(2)}, u32[]{:S(2)}) collective-permute-start(bf16[512,1024]{1,0:T(8,128)(2,1)S(1)} %constant_dynamic-update-slice_fusion.33), channel_id=1, source_target_pairs={{0,2},{1,3},{2,0},{3,1},{4,6},{5,7},{6,4},{7,5},{8,10},{9,11},{10,... | collective-permute-start | bytes 3145736 | tf_op jit(solution)/shard_map/ppermute | solution.py:34
  208.3 47.3 %collective-permute-start.60 = (bf16[256,2048]{1,0:T(8,128)(2,1)S(1)}, bf16[256,2048]{1,0:T(8,128)(2,1)S(1)}, u32[]{:S(2)}, u32[]{:S(2)}) collective-permute-start(bf16[256,2048]{1,0:T(8,128)(2,1)S(1)} %pad_maximum_fusion.4), channel_id=1, source_target_pairs={{0,1},{1,0},{2,3},{3,2},{4,5},{5,4},{6,7},{7,6},{8,9},{9,8},{10,11... | collective-permute-start | bytes 3145736 | tf_op jit(solution)/shard_map/ppermute | solution.py:34
  344.8 31.6 %collective-permute-start.63 = (bf16[64,2048]{1,0:T(8,128)(2,1)S(1)}, bf16[64,2048]{1,0:T(8,128)(2,1)S(1)}, u32[]{:S(2)}, u32[]{:S(2)}) collective-permute-start(bf16[64,2048]{1,0:T(8,128)(2,1)S(1)} %get-tuple-element.121), channel_id=1, source_target_pairs={{0,16},{4,20},{8,24},{12,28},{16,0},{20,4},{24,8},{28,12},{1,17},{... | collective-permute-start | bytes 786440 | tf_op jit(solution)/shard_map/ppermute | solution.py:34
  348.2 35.7 %collective-permute-start.54 = (bf16[64,2048]{1,0:T(8,128)(2,1)S(1)}, bf16[64,2048]{1,0:T(8,128)(2,1)S(1)}, u32[]{:S(2)}, u32[]{:S(2)}) collective-permute-start(bf16[64,2048]{1,0:T(8,128)(2,1)S(1)} %get-tuple-element.123), channel_id=1, source_target_pairs={{0,24},{4,28},{8,16},{12,20},{16,8},{20,12},{24,0},{28,4},{1,25},{... | collective-permute-start | bytes 786440 | tf_op jit(solution)/shard_map/ppermute | solution.py:34
  349.4 39.1 %collective-permute-start.53 = (bf16[64,2048]{1,0:T(8,128)(2,1)S(1)}, bf16[64,2048]{1,0:T(8,128)(2,1)S(1)}, u32[]{:S(2)}, u32[]{:S(2)}) collective-permute-start(bf16[64,2048]{1,0:T(8,128)(2,1)S(1)} %get-tuple-element.124), channel_id=1, source_target_pairs={{0,16},{4,20},{8,24},{12,28},{16,0},{20,4},{24,8},{28,12},{1,17},{... | collective-permute-start | bytes 786440 | tf_op jit(solution)/shard_map/ppermute | solution.py:34
  383.9 35.3 %collective-permute-start.103 = (bf16[512,1024]{1,0:T(8,128)(2,1)}, bf16[512,1024]{1,0:T(8,128)(2,1)}, u32[]{:S(2)}, u32[]{:S(2)}) collective-permute-start(bf16[512,1024]{1,0:T(8,128)(2,1)} %pad_maximum_fusion.10), channel_id=1, source_target_pairs={{0,4},{4,0},{8,12},{12,8},{16,20},{20,16},{24,28},{28,24},{1,5},{5... | collective-permute-start | bytes 3145736 | tf_op jit(solution)/shard_map/ppermute | solution.py:34
  388.6 31.0 %collective-permute-start.101 = (bf16[512,1024]{1,0:T(8,128)(2,1)}, bf16[512,1024]{1,0:T(8,128)(2,1)}, u32[]{:S(2)}, u32[]{:S(2)}) collective-permute-start(bf16[512,1024]{1,0:T(8,128)(2,1)} %pad_maximum_fusion.9), channel_id=1, source_target_pairs={{0,2},{1,3},{2,0},{3,1},{4,6},{5,7},{6,4},{7,5},{8,10},{9,11},{10,... | collective-permute-start | bytes 3145736 | tf_op jit(solution)/shard_map/ppermute | solution.py:34
  392.4 33.6 %collective-permute-start.65 = (bf16[64,2048]{1,0:T(8,128)(2,1)S(1)}, bf16[64,2048]{1,0:T(8,128)(2,1)S(1)}, u32[]{:S(2)}, u32[]{:S(2)}) collective-permute-start(bf16[64,2048]{1,0:T(8,128)(2,1)S(1)} %get-tuple-element.55), channel_id=1, source_target_pairs={{0,8},{4,12},{8,0},{12,4},{16,24},{20,28},{24,16},{28,20},{1,9},{5... | collective-permute-start | bytes 786440 | tf_op jit(solution)/shard_map/ppermute | solution.py:34
  396.7 31.3 %collective-permute-start.66 = (bf16[64,2048]{1,0:T(8,128)(2,1)S(1)}, bf16[64,2048]{1,0:T(8,128)(2,1)S(1)}, u32[]{:S(2)}, u32[]{:S(2)}) collective-permute-start(bf16[64,2048]{1,0:T(8,128)(2,1)S(1)} %get-tuple-element.55), channel_id=1, source_target_pairs={{0,16},{4,20},{8,24},{12,28},{16,0},{20,4},{24,8},{28,12},{1,17},{... | collective-permute-start | bytes 786440 | tf_op jit(solution)/shard_map/ppermute | solution.py:34
  400.8 31.3 %collective-permute-start.67 = (bf16[64,2048]{1,0:T(8,128)(2,1)S(1)}, bf16[64,2048]{1,0:T(8,128)(2,1)S(1)}, u32[]{:S(2)}, u32[]{:S(2)}) collective-permute-start(bf16[64,2048]{1,0:T(8,128)(2,1)S(1)} %get-tuple-element.55), channel_id=1, source_target_pairs={{0,24},{4,28},{8,16},{12,20},{16,8},{20,12},{24,0},{28,4},{1,25},{... | collective-permute-start | bytes 786440 | tf_op jit(solution)/shard_map/ppermute | solution.py:34
  428.0 44.2 %collective-permute-start.104 = (bf16[512,256]{1,0:T(8,128)(2,1)S(1)}, bf16[512,256]{1,0:T(8,128)(2,1)S(1)}, u32[]{:S(2)}, u32[]{:S(2)}) collective-permute-start(bf16[512,256]{1,0:T(8,128)(2,1)S(1)} %get-tuple-element.104), channel_id=1, source_target_pairs={{0,8},{4,12},{8,0},{12,4},{16,24},{20,28},{24,16},{28,20},{1,9},{5... | collective-permute-start | bytes 786440 | tf_op jit(solution)/shard_map/ppermute | solution.py:34
  432.1 40.2 %collective-permute-start.105 = (bf16[512,256]{1,0:T(8,128)(2,1)S(1)}, bf16[512,256]{1,0:T(8,128)(2,1)S(1)}, u32[]{:S(2)}, u32[]{:S(2)}) collective-permute-start(bf16[512,256]{1,0:T(8,128)(2,1)S(1)} %get-tuple-element.103), channel_id=1, source_target_pairs={{0,16},{4,20},{8,24},{12,28},{16,0},{20,4},{24,8},{28,12},{1,17},{... | collective-permute-start | bytes 786440 | tf_op jit(solution)/shard_map/ppermute | solution.py:34
  433.3 39.0 %collective-permute-start.106 = (bf16[512,256]{1,0:T(8,128)(2,1)S(1)}, bf16[512,256]{1,0:T(8,128)(2,1)S(1)}, u32[]{:S(2)}, u32[]{:S(2)}) collective-permute-start(bf16[512,256]{1,0:T(8,128)(2,1)S(1)} %get-tuple-element.102), channel_id=1, source_target_pairs={{0,24},{4,28},{8,16},{12,20},{16,8},{20,12},{24,0},{28,4},{1,25},{... | collective-permute-start | bytes 786440 | tf_op jit(solution)/shard_map/ppermute | solution.py:34
  433.7 43.9 %collective-permute-start.56 = (bf16[2,64,2048]{2,1,0:T(8,128)(2,1)S(1)}, bf16[2,64,2048]{2,1,0:T(8,128)(2,1)S(1)}, u32[]{:S(2)}, u32[]{:S(2)}) collective-permute-start(bf16[2,64,2048]{2,1,0:T(8,128)(2,1)S(1)} %get-tuple-element.143), channel_id=1, source_target_pairs={{0,1},{1,0},{2,3},{3,2},{4,5},{5,4},{6,7},{7,6},{8,9},{9,8},{10,11... | collective-permute-start | bytes 1572872 | tf_op jit(solution)/shard_map/ppermute | solution.py:34
  561.1 31.3 %collective-permute-start.83 = (bf16[256,384]{0,1:T(8,128)(2,1)}, bf16[256,384]{0,1:T(8,128)(2,1)}, u32[]{:S(2)}, u32[]{:S(2)}) collective-permute-start(bf16[256,384]{0,1:T(8,128)(2,1)} %get-tuple-element.131), channel_id=1, source_target_pairs={{0,8},{4,12},{8,0},{12,4},{16,24},{20,28},{24,16},{28,20},{1,9},{5... | collective-permute-start | bytes 589832 | tf_op jit(solution)/shard_map/ppermute | solution.py:34
  561.6 32.2 %collective-permute-start.84 = (bf16[256,384]{0,1:T(8,128)(2,1)}, bf16[256,384]{0,1:T(8,128)(2,1)}, u32[]{:S(2)}, u32[]{:S(2)}) collective-permute-start(bf16[256,384]{0,1:T(8,128)(2,1)} %get-tuple-element.130), channel_id=1, source_target_pairs={{0,16},{4,20},{8,24},{12,28},{16,0},{20,4},{24,8},{28,12},{1,17},{... | collective-permute-start | bytes 589832 | tf_op jit(solution)/shard_map/ppermute | solution.py:34
  (163 other events, 2484.7 us)

commit v2 on v1

v2 whole, which is shorter than its diff:
```python
from functools import partial

import jax
import jax.numpy as jnp
from jax import lax
from jax.experimental import pallas as pl
from jax.experimental.pallas import tpu as pltpu
from jax.sharding import PartitionSpec as P

HEADS = 16
SPAN = 128
ROW_LEN = 2048
STEP = 7

first_decay = 0.5
second_decay = 0.95
adam_epsilon = 1e-08
norm_epsilon = 1e-05
matrix_shrink = 0.1
input_rate = 0.02
output_rate = 0.45
expand_rate = 0.02
reduce_rate = 0.01
gain_rate = 0.2

F32 = jnp.float32
BF16 = jnp.bfloat16
PARAMS = pltpu.CompilerParams(vmem_limit_bytes=60 << 20)
SMALL = pl.CostEstimate(flops=1, bytes_accessed=1, transcendentals=0)

Z_STEPS = (1, 2, 3)
AUX = 16


def swap(value, axis, mask):
    size = lax.axis_size(axis)
    return lax.ppermute(value, axis, [(i, i ^ mask) for i in range(size)])


def over_z(value, step):
    return swap(value, "fsdp", 2 * step)


def over_c(value):
    return swap(value, "mp", 1)


def over_x(value):
    return swap(value, "mp", 2)


def over_y(value):
    return swap(value, "fsdp", 1)


def after(value, *others):
    return lax.optimization_barrier((value,) + others)[0] if others else value


def outer_bits():
    bits, bit = [], 8
    while bit < lax.axis_size("fsdp"):
        bits.append(bit)
        bit *= 2
    return bits


def gather_groups(own, ready=()):
    if ready:
        own = after(own, *ready)
    half = own.shape[0] // 2
    from_x, from_y = over_x(own), over_y(own)
    pieces = {
        (0, 0): (own,),
        (1, 0): (from_x,),
        (0, 1): (from_y,),
        (1, 1): (over_y(from_x[:half]), over_x(from_y[half:])),
    }
    for bit in outer_bits():
        for (x, t), piece in list(pieces.items()):
            pieces[x, t + bit // 4] = tuple(swap(part, "fsdp", bit) for part in piece)
    return pieces


def first_level(pieces):
    return pieces[1, 0][0], pieces[0, 1][0]


def reduce_groups(pieces, first_after=(), sum_after=(), second_after=()):
    pieces = dict(pieces)
    for bit in reversed(outer_bits()):
        for (x, t), piece in list(pieces.items()):
            if t & (bit // 4):
                pieces[x, t ^ (bit // 4)] = add(pieces[x, t ^ (bit // 4)], swap(piece, "fsdp", bit))
                del pieces[x, t]
    corner = after(pieces[1, 1], *first_after)
    half = corner.shape[0] // 2
    first = from_y, from_x = over_y(corner[:half]), over_x(corner[half:])
    to_x = after(pieces[1, 0], *sum_after)
    to_y = after(pieces[0, 1], *sum_after)
    to_x = jnp.concatenate([add(to_x[:half], from_y), to_x[half:]])
    to_y = jnp.concatenate([to_y[:half], add(to_y[half:], from_x)])
    sent = (after(to_x, *second_after), after(to_y, *second_after))
    second = over_x(sent[0]), over_y(sent[1])
    return add(pieces[0, 0], *second), first, second, sent


def add(*values):
    total = values[0].astype(F32)
    for value in values[1:]:
        total = total + value.astype(F32)
    return total.astype(BF16)


def copies_kernel(plan, inputs, at_ref, *refs):
    sems = refs[-1]
    copies = [
        pltpu.make_async_copy(source, target, sems.at[i])
        for i, (source, target) in enumerate(plan(at_ref[0], refs[:inputs], refs[inputs:-1]))
    ]
    for copy in copies:
        copy.start()
    for copy in copies:
        copy.wait()


def copies(plan, count, at, arrays, shapes, name):
    return pl.pallas_call(
        partial(copies_kernel, plan, len(arrays)),
        in_specs=[pl.BlockSpec(memory_space=pltpu.SMEM)]
        + [pl.BlockSpec(memory_space=pl.ANY)] * len(arrays),
        out_specs=[pl.BlockSpec(memory_space=pltpu.VMEM)] * len(shapes),
        out_shape=[jax.ShapeDtypeStruct(shape, BF16) for shape in shapes],
        scratch_shapes=[pltpu.SemaphoreType.DMA((count,))],
        compiler_params=PARAMS,
        cost_estimate=SMALL,
        name=name,
    )(at, *arrays)


def assemble(at, parts, count=1):
    rows, units = parts[0].shape[0], parts[0].shape[1] // count

    def plan(spot, ins, outs):
        for i, part in enumerate(ins):
            for j, out in enumerate(outs):
                yield part.at[:, pl.ds(j * units, units)], out.at[spot ^ i]

    return copies(plan, 4 * count, at, parts, [(4, rows, units)] * count, "assemble")


def along_z(parts, ready=None):
    if ready is not None:
        parts = [after(part, came) for part, came in zip(parts, ready)]
    return [over_z(part, step) for part, step in zip(parts, Z_STEPS)]


def token_groups():
    groups = []
    for outer in range(lax.axis_size("fsdp") // 8):
        for y in range(2):
            for x in range(2):
                groups.append(
                    [
                        ((outer * 4 + z) * 2 + y) * 4 + x * 2 + c
                        for z in range(4)
                        for c in range(2)
                    ]
                )
    return groups


def gather_tokens(own):
    return lax.all_gather(
        own, ("fsdp", "mp"), axis_index_groups=token_groups(), axis=0, tiled=True
    )


def scatter_tokens(partial_sums):
    return lax.psum_scatter(
        partial_sums,
        ("fsdp", "mp"),
        axis_index_groups=token_groups(),
        scatter_dimension=0,
        tiled=True,
    )


def normalize(values):
    centre = jnp.mean(values, axis=-1, keepdims=True)
    centred = values - centre
    spread = jnp.mean(centred * centred, axis=-1, keepdims=True)
    scale = lax.rsqrt(spread + norm_epsilon)
    return centred * scale, scale


def norm_back(shape, scale, gain, grad):
    weighted = grad * gain
    back = (
        weighted
        - jnp.mean(weighted, axis=-1, keepdims=True)
        - shape * jnp.mean(weighted * shape, axis=-1, keepdims=True)
    ) * scale
    return back, jnp.sum(grad * shape, axis=0), jnp.sum(grad, axis=0)


def adamw_update(master, moment_one, moment_two, gradient, step_rate, shrink_rate):
    moment_one = first_decay * moment_one + (1.0 - first_decay) * gradient
    moment_two = second_decay * moment_two + (1.0 - second_decay) * gradient * gradient
    mean_part = moment_one / (1.0 - first_decay**STEP)
    square_part = moment_two / (1.0 - second_decay**STEP)
    updated = master - step_rate * (
        mean_part / (jnp.sqrt(square_part) + adam_epsilon) + shrink_rate * master
    )
    return (moment_one, moment_two, updated)


def dot(left, right, dims=((1,), (0,))):
    return lax.dot_general(left, right, (dims, ((), ())), preferred_element_type=F32)


ROWS_BY_ROWS = ((0,), (0,))
COLS_BY_COLS = ((1,), (1,))


def at_steps(body):
    for step in range(4):
        pl.when(pl.program_id(0) == step)(partial(body, step))


def pack_attention_kernel(at_ref, weight_ref, turned_ref, norm_ref, marks_ref, *refs):
    outs, aux = refs[:4], refs[4]
    rows, head = weight_ref.shape[1:]

    def body(step):
        for kind in range(3):
            outs[step][:rows, kind * head : (kind + 1) * head] = weight_ref[kind].astype(BF16)
        outs[step][:rows, 3 * head :] = turned_ref[...].T.astype(BF16)
        aux[...] = jnp.zeros_like(aux)
        aux[:4, : norm_ref.shape[1]] = norm_ref[...]
        aux[8:10, : marks_ref.shape[1]] = marks_ref[...].astype(F32)
        outs[step][rows:, :] = aux[...].astype(BF16)

    at_steps(body)


def pack_attention(at, weight, turned, norms, marks):
    _, rows, width = weight.shape
    head = width // 4
    shape = (rows + AUX, 4 * head)
    return pl.pallas_call(
        pack_attention_kernel,
        grid_spec=pltpu.PrefetchScalarGridSpec(
            num_scalar_prefetch=1,
            grid=(4,),
            in_specs=[
                pl.BlockSpec((3, rows, head), lambda i, at: (0, 0, at[0] ^ i)),
                pl.BlockSpec((head, rows), lambda i, at: (at[0] ^ i, 0)),
                pl.BlockSpec(norms.shape, lambda i, at: (0, 0)),
                pl.BlockSpec(marks.shape, lambda i, at: (0, 0)),
            ],
            out_specs=[pl.BlockSpec(shape, lambda i, at: (0, 0))] * 4,
            scratch_shapes=[pltpu.VMEM((AUX, 4 * head), F32)],
        ),
        out_shape=[jax.ShapeDtypeStruct(shape, BF16)] * 4,
        compiler_params=PARAMS,
        cost_estimate=SMALL,
        name="pack_attention",
    )(at, weight, turned, norms, marks)


def pack_kernel(at_ref, plain_ref, turned_ref, *outs):
    def body(step):
        units = plain_ref.shape[1]
        outs[step][:, :units] = plain_ref[...].astype(BF16)
        outs[step][:, units:] = turned_ref[...].T.astype(BF16)

    at_steps(body)


def pack(at, plain, turned):
    rows, cols = plain.shape
    shape = (rows, cols // 2)
    return pl.pallas_call(
        pack_kernel,
        grid_spec=pltpu.PrefetchScalarGridSpec(
            num_scalar_prefetch=1,
            grid=(4,),
            in_specs=[
                pl.BlockSpec((rows, cols // 4), lambda i, at: (0, at[0] ^ i)),
                pl.BlockSpec((cols // 4, rows), lambda i, at: (at[0] ^ i, 0)),
            ],
            out_specs=[pl.BlockSpec(shape, lambda i, at: (0, 0))] * 4,
        ),
        out_shape=[jax.ShapeDtypeStruct(shape, BF16)] * 4,
        compiler_params=PARAMS,
        cost_estimate=SMALL,
        name="pack",
    )(at, plain, turned)


def flatten(pieces, rows, columns):
    arrays, specs, layout = [], [], []
    size, index = columns
    for key in sorted(pieces):
        for array in pieces[key]:
            arrays.append(array)
            specs.append(
                pl.BlockSpec((array.shape[0], rows, size), lambda *_, j=index: (0, 0, j))
            )
        layout.append((key, len(pieces[key])))
    return arrays, specs, layout


def half_block(refs, layout, key, half):
    start = 0
    for other, count in layout:
        if other == key:
            break
        start += count
    if count == 2:
        value = refs[start + half][...]
    else:
        value = refs[start][2 * half : 2 * half + 2]
    return value.reshape(value.shape[0] * value.shape[1], value.shape[2])


def groups_of(layout):
    return len(layout) // 2


def times_units(value, refs, layout, x):
    groups = groups_of(layout)
    size = value.shape[1] // (2 * groups)
    total = None
    for t in range(groups):
        for half in range(2):
            i = 2 * t + half
            term = dot(value[:, i * size : (i + 1) * size], half_block(refs, layout, (x, t), half))
            total = term if total is None else total + term
    return total


def times_features(value, refs, layout, store):
    units = value.shape[1] // 2
    for t in range(groups_of(layout)):
        for half in range(2):
            term = dot(value[:, :units], half_block(refs, layout, (0, t), half), COLS_BY_COLS)
            term = term + dot(
                value[:, units:], half_block(refs, layout, (1, t), half), COLS_BY_COLS
            )
            store(2 * t + half, term)


def whole(array):
    zeros = (0,) * array.ndim
    return pl.BlockSpec(array.shape, lambda *_: zeros)


def rows_spec(array):
    return pl.BlockSpec((array.shape[0] // 2, array.shape[1]), lambda i: (i, 0))


def project_kernel(layout, head, tokens_ref, norms, *refs):
    pieces, (low_ref, q_ref, kv_ref) = refs[:-3], refs[-3:]
    low = (normalize(tokens_ref[...].astype(F32))[0] * norms[0:1] + norms[1:2]).astype(BF16)
    low_ref[...] = low
    for x in range(2):
        out = times_units(low, pieces, layout, x).astype(BF16)
        q_ref[:, x * head : (x + 1) * head] = out[:, :head]
        kv_ref[x] = out[:, head:]


def project(tokens, norms, pieces, shard, head):
    arrays, specs, layout = flatten(pieces, shard, (3 * head, 0))
    count = tokens.shape[0]
    queries = jax.ShapeDtypeStruct((count, 2 * head), BF16)
    return pl.pallas_call(
        partial(project_kernel, layout, head),
        grid=(2,),
        in_specs=[rows_spec(tokens), whole(norms)] + specs,
        out_specs=[
            rows_spec(tokens),
            rows_spec(queries),
            pl.BlockSpec((2, count // 2, 2 * head), lambda i: (0, i, 0)),
        ],
        out_shape=[
            jax.ShapeDtypeStruct(tokens.shape, BF16),
            queries,
            jax.ShapeDtypeStruct((2, count, 2 * head), BF16),
        ],
        compiler_params=PARAMS,
        cost_estimate=SMALL,
        name="project",
    )(tokens, norms, *arrays)


def to_units_kernel(layout, value_ref, *refs):
    pieces, out = refs[:-1], refs[-1]
    units = out.shape[1] // 2
    for x in range(2):
        term = times_units(value_ref[...], pieces, layout, x)
        out[:, x * units : (x + 1) * units] = term.astype(out.dtype)


def to_units(value, pieces, shard, columns, kind):
    arrays, specs, layout = flatten(pieces, shard, columns)
    out = jax.ShapeDtypeStruct((value.shape[0], 2 * columns[0]), kind)
    return pl.pallas_call(
        partial(to_units_kernel, layout),
        grid=(2,),
        in_specs=[rows_spec(value)] + specs,
        out_specs=rows_spec(out),
        out_shape=out,
        compiler_params=PARAMS,
        cost_estimate=SMALL,
        name="to_units",
    )(value, *arrays)


def to_features_kernel(layout, value_ref, *refs):
    pieces, out = refs[:-1], refs[-1]

    def store(i, term):
        size = term.shape[1]
        out[:, i * size : (i + 1) * size] = term.astype(BF16)

    times_features(value_ref[...], pieces, layout, store)


def to_features(value, pieces, shard, columns, width):
    arrays, specs, layout = flatten(pieces, shard, columns)
    out = jax.ShapeDtypeStruct((value.shape[0], width), BF16)
    return pl.pallas_call(
        partial(to_features_kernel, layout),
        grid=(2,),
        in_specs=[rows_spec(value)] + specs,
        out_specs=rows_spec(out),
        out_shape=out,
        compiler_params=PARAMS,
        cost_estimate=SMALL,
        name="to_features",
    )(value, *arrays)


def feed_kernel(layout, value_ref, pull_ref, *refs):
    pieces, (active_ref, grad_ref, out_ref) = refs[:-3], refs[-3:]
    units = active_ref.shape[1] // 2
    scale = 0.7978845608028654
    for x in range(2):
        columns = slice(x * units, (x + 1) * units)
        hidden = times_units(value_ref[...], pieces, layout, x)
        square = hidden * hidden
        curve = jnp.tanh(scale * (hidden + 0.044715 * hidden * square))
        rise = 0.5 * (1.0 + curve)
        active_ref[:, columns] = (hidden * rise).astype(BF16)
        slope = rise + 0.5 * hidden * (1.0 - curve * curve) * scale * (
            1.0 + 3.0 * 0.044715 * square
        )
        grad_ref[:, columns] = (pull_ref[:, columns] * slope).astype(BF16)

    def store(i, term):
        size = term.shape[1]
        out_ref[:, i * size : (i + 1) * size] = term.astype(BF16)

    times_features(grad_ref[...], pieces, layout, store)


def feed_forward(value, pull, pieces, shard, units):
    arrays, specs, layout = flatten(pieces, shard, (units, 0))
    low = jax.ShapeDtypeStruct((value.shape[0], 2 * units), BF16)
    return pl.pallas_call(
        partial(feed_kernel, layout),
        grid=(2,),
        in_specs=[rows_spec(value), rows_spec(pull)] + specs,
        out_specs=[rows_spec(low), rows_spec(low), rows_spec(value)],
        out_shape=[low, low, jax.ShapeDtypeStruct(value.shape, BF16)],
        compiler_params=PARAMS,
        cost_estimate=SMALL,
        name="feed_forward",
    )(value, pull, *arrays)


def project_back_kernel(layout, head, query_ref, pair_ref, tokens_ref, *refs):
    pieces, (out, sums) = refs[:-2], refs[-2:]
    shape = normalize(tokens_ref[...].astype(F32))[0]
    value = jnp.concatenate(
        [query_ref[:, :head], pair_ref[0], query_ref[:, head:], pair_ref[1]], axis=1
    )

    @pl.when(pl.program_id(0) == 0)
    def _():
        sums[...] = jnp.zeros_like(sums)

    def store(i, term):
        size = term.shape[1]
        columns = slice(i * size, (i + 1) * size)
        out[:, columns] = term.astype(BF16)
        sums[0:1, columns] += jnp.sum(term * shape[:, columns], axis=0, keepdims=True)
        sums[1:2, columns] += jnp.sum(term, axis=0, keepdims=True)

    times_features(value, pieces, layout, store)


def project_back(query_grad, pair_grad, tokens, pieces, shard, head):
    arrays, specs, layout = flatten(pieces, shard, (3 * head, 0))
    count, width = tokens.shape
    sums = jax.ShapeDtypeStruct((2, width), F32)
    return pl.pallas_call(
        partial(project_back_kernel, layout, head),
        grid=(2,),
        in_specs=[
            rows_spec(query_grad),
            pl.BlockSpec((2, count // 2, 2 * head), lambda i: (0, i, 0)),
            rows_spec(tokens),
        ]
        + specs,
        out_specs=[rows_spec(tokens), whole(sums)],
        out_shape=[jax.ShapeDtypeStruct(tokens.shape, BF16), sums],
        compiler_params=PARAMS,
        cost_estimate=SMALL,
        name="project_back",
    )(query_grad, pair_grad, tokens, *arrays)


def grads_kernel(groups, pairs, extra, *refs):
    lefts, rights = refs[:pairs], refs[pairs : 2 * pairs]
    rest = refs[2 * pairs :]
    if extra:
        sums, outs, aux = rest[0], rest[1:-1], rest[-1]
    else:
        outs = rest

    def body(t):
        for x in range(2):
            out, start = outs[t * 2 + x], 0
            for left, right in zip(lefts, rights):
                if len(right.shape) == 3:
                    value = right[x]
                else:
                    units = right.shape[1] // 2
                    value = right[:, x * units : (x + 1) * units]
                term = dot(left[...], value, ROWS_BY_ROWS)
                shard, units = term.shape[0] // 4, term.shape[1]
                out[:, :shard, start : start + units] = term.astype(BF16).reshape(4, shard, units)
                start += units
            if extra:
                for z in range(4):
                    aux[...] = jnp.zeros_like(aux)
                    if x == 0:
                        aux[:4, :shard] = sums[:, z * shard : (z + 1) * shard]
                    out[z, shard:, :] = aux[...].astype(BF16)

    for t in range(groups):
        pl.when(pl.program_id(0) == t)(partial(body, t))


def weight_grads(pairs, groups, sums=None):
    count, width = pairs[0][0].shape
    strip = width // groups
    units = sum(right.shape[2] if right.ndim == 3 else right.shape[1] // 2 for _, right in pairs)
    extra = sums is not None
    shape = (4, strip // 4 + (AUX if extra else 0), units)
    outs = pl.pallas_call(
        partial(grads_kernel, groups, len(pairs), extra),
        grid=(groups,),
        in_specs=[pl.BlockSpec((count, strip), lambda t: (0, t))] * len(pairs)
        + [whole(right) for _, right in pairs]
        + ([pl.BlockSpec((4, strip), lambda t: (0, t))] if extra else []),
        out_specs=[pl.BlockSpec(shape, lambda t: (0, 0, 0))] * (2 * groups),
        out_shape=[jax.ShapeDtypeStruct(shape, BF16)] * (2 * groups),
        scratch_shapes=[pltpu.VMEM((AUX, units), F32)] if extra else [],
        compiler_params=PARAMS,
        cost_estimate=SMALL,
        name="weight_grads",
    )(*[left for left, _ in pairs], *[right for _, right in pairs], *([sums] if extra else []))
    return {(i % 2, i // 2): out for i, out in enumerate(outs)}


def visible(query_marks, key_marks):
    return (query_marks[:, 0:1] == key_marks[0:1, :]) & (key_marks[1:2, :] <= query_marks[:, 1:2])


def collect(layout, refs, kv_ref):
    flipped = pl.program_id(0) == 0
    count = refs[0].shape[1]
    i = 0
    for at, (_, parts) in enumerate(layout):
        value = refs[i][0] if parts == 1 else jnp.where(flipped, refs[i + 1][0], refs[i][0])
        kv_ref[at * count : (at + 1) * count] = value
        i += parts


def attend_kernel(scaling, layout, q_ref, qm_ref, km_ref, *refs):
    members, (out_ref, low_ref, lse_ref, kv_ref) = refs[:-4], refs[-4:]
    pl.when(pl.program_id(1) == 0)(lambda: collect(layout, members, kv_ref))
    head = q_ref.shape[1]
    keys, values = kv_ref[:, :head], kv_ref[:, head:]
    scores = dot(q_ref[...], keys, COLS_BY_COLS) * scaling
    scores = jnp.where(visible(qm_ref[...], km_ref[...]), scores, -1e30)
    largest = jnp.max(scores, axis=1, keepdims=True)
    weights = jnp.exp(scores - largest)
    totals = jnp.sum(weights, axis=1, keepdims=True)
    probs = (weights * (1.0 / totals)).astype(BF16)
    attended = dot(probs, values)
    out_ref[...] = attended
    low_ref[...] = attended.astype(BF16)
    lse_ref[0] = largest + jnp.log(totals)


def attend_back_kernel(
    scaling, layout, q_ref, qm_ref, km_ref, out_ref, lse_ref, grad_ref, *refs
):
    outs = len(layout)
    members, dq_ref = refs[: -outs - 3], refs[-outs - 3]
    dkv_refs, total_ref, kv_ref = refs[-outs - 2 : -2], refs[-2], refs[-1]
    step, last = pl.program_id(1), pl.num_programs(1) - 1
    pl.when(step == 0)(lambda: collect(layout, members, kv_ref))
    head = q_ref.shape[1]
    keys, values = kv_ref[:, :head], kv_ref[:, head:]
    grad = grad_ref[...]
    row_dots = jnp.sum(grad.astype(F32) * out_ref[...], axis=1, keepdims=True)
    scores = dot(q_ref[...], keys, COLS_BY_COLS) * scaling
    scores = jnp.where(visible(qm_ref[...], km_ref[...]), scores, -1e30)
    probs = jnp.exp(scores - lse_ref[0])
    prob_grad = dot(grad, values, COLS_BY_COLS)
    score_grad = (probs * (prob_grad - row_dots)).astype(BF16)
    dq_ref[...] = (dot(score_grad, keys) * scaling).astype(BF16)
    key_grad = dot(score_grad, q_ref[...], ROWS_BY_ROWS) * scaling
    value_grad = dot(probs.astype(BF16), grad, ROWS_BY_ROWS)
    both = jnp.concatenate([key_grad, value_grad], axis=1)

    @pl.when(step == 0)
    def _():
        total_ref[...] = both

    @pl.when(step > 0)
    def _():
        total_ref[...] += both

    @pl.when(step == last)
    def _():
        count = dkv_refs[0].shape[1]
        for i, ref in enumerate(dkv_refs):
            ref[0] = total_ref[i * count : (i + 1) * count].astype(BF16)


BLOCK = 256


def member_specs(members):
    arrays, specs, layout = [], [], []
    for key in sorted(members):
        parts = members[key]
        for array in parts:
            block = (1,) + array.shape[1:]
            if len(parts) == 1:
                specs.append(pl.BlockSpec(block, lambda h, i, x=key[0]: (h ^ x, 0, 0)))
            else:
                specs.append(pl.BlockSpec(block, lambda h, i: (0, 0, 0)))
            arrays.append(array)
        layout.append((key, len(parts)))
    return arrays, specs, layout


def attend(queries, members, query_marks, key_marks, scaling):
    arrays, specs, layout = member_specs(members)
    count, head = queries.shape[0], queries.shape[1] // 2
    length = key_marks.shape[1]
    return pl.pallas_call(
        partial(attend_kernel, scaling, layout),
        grid=(2, count // BLOCK),
        in_specs=[
            pl.BlockSpec((BLOCK, head), lambda h, i: (i, h)),
            pl.BlockSpec((BLOCK, 2), lambda h, i: (i, 0)),
            pl.BlockSpec((2, length), lambda h, i: (0, 0)),
        ]
        + specs,
        out_specs=[
            pl.BlockSpec((BLOCK, head), lambda h, i: (i, h)),
            pl.BlockSpec((BLOCK, head), lambda h, i: (i, h)),
            pl.BlockSpec((1, BLOCK, 1), lambda h, i: (h, i, 0)),
        ],
        out_shape=[
            jax.ShapeDtypeStruct((count, 2 * head), F32),
            jax.ShapeDtypeStruct((count, 2 * head), BF16),
            jax.ShapeDtypeStruct((2, count, 1), F32),
        ],
        scratch_shapes=[pltpu.VMEM((length, 2 * head), BF16)],
        compiler_params=PARAMS,
        cost_estimate=SMALL,
        name="attend",
    )(queries, query_marks, key_marks, *arrays)


def attend_back(queries, members, query_marks, key_marks, attended, logsum, grad, scaling):
    arrays, specs, layout = member_specs(members)
    count, head = queries.shape[0], queries.shape[1] // 2
    length = key_marks.shape[1]
    block = BLOCK if length <= 2048 else 128
    rows = pl.BlockSpec((block, head), lambda h, i: (i, h))
    outs = pl.pallas_call(
        partial(attend_back_kernel, scaling, layout),
        grid=(2, count // block),
        in_specs=[
            rows,
            pl.BlockSpec((block, 2), lambda h, i: (i, 0)),
            pl.BlockSpec((2, length), lambda h, i: (0, 0)),
            rows,
            pl.BlockSpec((1, block, 1), lambda h, i: (h, i, 0)),
            rows,
        ]
        + specs,
        out_specs=[rows]
        + [
            pl.BlockSpec((1, count, 2 * head), lambda h, i, x=key[0]: (h ^ x, 0, 0))
            for key, _ in layout
        ],
        out_shape=[jax.ShapeDtypeStruct((count, 2 * head), BF16)]
        + [jax.ShapeDtypeStruct((2, count, 2 * head), BF16)] * len(layout),
        scratch_shapes=[
            pltpu.VMEM((length, 2 * head), F32),
            pltpu.VMEM((length, 2 * head), BF16),
        ],
        compiler_params=PARAMS,
        cost_estimate=SMALL,
        name="attend_back",
    )(queries, query_marks, key_marks, attended, logsum, grad, *arrays)
    return outs[0], {key: out for (key, _), out in zip(layout, outs[1:])}


def adam_kernel(rate, shape, sources, at_ref, *refs):
    count = 4 * len(sources)
    parts, (master_ref, first_ref, second_ref), outs, chosen = (
        refs[:count],
        refs[count : count + 3],
        refs[count + 3 : count + 7],
        refs[count + 7],
    )

    def body(step):
        column = 0
        for i, (start, stop) in enumerate(sources):
            value = parts[4 * i + step][: chosen.shape[0], start:stop]
            chosen[:, column : column + stop - start] = value
            column += stop - start

    at_steps(body)
    grad = chosen[...].astype(F32)
    if shape == "turned":
        grad = grad.T
    if shape == "cube":
        head = grad.shape[1] // 3
        grad = jnp.stack([grad[:, k * head : (k + 1) * head] for k in range(3)])
    first, second, master = adamw_update(
        master_ref[...], first_ref[...], second_ref[...], grad, rate, matrix_shrink
    )
    outs[0][...] = first
    outs[1][...] = second
    outs[2][...] = master
    outs[3][...] = master.astype(BF16)


def adam(at, matrix, rate, shape, sources):
    master = matrix[0]
    if shape == "cube":
        three, rows, cols = master.shape
        spec = pl.BlockSpec((three, rows, cols // 4), lambda i, at: (0, 0, at[0] ^ i))
    elif shape == "turned":
        rows, cols = master.shape[1], master.shape[0]
        spec = pl.BlockSpec((cols // 4, rows), lambda i, at: (at[0] ^ i, 0))
    else:
        rows, cols = master.shape
        spec = pl.BlockSpec((rows, cols // 4), lambda i, at: (0, at[0] ^ i))
    columns = [(start, stop) for _, start, stop in sources]
    units = sum(stop - start for start, stop in columns)
    return pl.pallas_call(
        partial(adam_kernel, rate, shape, columns),
        grid_spec=pltpu.PrefetchScalarGridSpec(
            num_scalar_prefetch=1,
            grid=(4,),
            in_specs=[
                pl.BlockSpec(part.shape, lambda i, at: (0, 0))
                for parts, _, _ in sources
                for part in parts
            ]
            + [spec] * 3,
            out_specs=[spec] * 4,
            scratch_shapes=[pltpu.VMEM((rows, units), BF16)],
        ),
        out_shape=[jax.ShapeDtypeStruct(master.shape, kind) for kind in (F32, F32, F32, BF16)],
        compiler_params=PARAMS,
        cost_estimate=SMALL,
        name="adam",
    )(at, *[part for parts, _, _ in sources for part in parts], *matrix)


def local(
    tokens,
    cotangent,
    segment_ids,
    span_map,
    norm_params,
    norm_first,
    norm_second,
    attention_input,
    attention_input_first,
    attention_input_second,
    attention_output,
    attention_output_first,
    attention_output_second,
    expand_weight,
    expand_first_moment,
    expand_second,
    reduce_weight,
    reduce_first_moment,
    reduce_second,
):
    width = tokens.shape[1]
    devices, lanes = lax.axis_size("fsdp"), lax.axis_size("mp")
    head = width // HEADS
    scaling = head ** (-0.5)
    shard = width // devices
    strip = 4 * shard
    outer = devices // 8
    groups = 2 * outer
    spot, lane = lax.axis_index("fsdp"), lax.axis_index("mp")
    at = (spot // 2) % 4
    at_word = at.reshape(1)
    group_at = (spot // 8) * 2 + spot % 2
    piece = tokens.shape[0] // lanes
    units = expand_weight.shape[1] // 4

    def to_relative(value):
        rows = value.shape[0]
        value = value.reshape(rows, outer, 4, 2, shard).transpose(0, 1, 3, 2, 4)
        value = value.reshape(rows, groups, strip)
        return jnp.concatenate(
            [
                lax.dynamic_index_in_dim(value, group_at ^ t, 1, keepdims=False)
                for t in range(groups)
            ],
            axis=1,
        )

    def to_natural(value):
        rows = value.shape[0]
        value = value.reshape(rows, groups, strip)
        value = jnp.stack(
            [
                lax.dynamic_index_in_dim(value, group_at ^ t, 1, keepdims=False)
                for t in range(groups)
            ],
            axis=1,
        )
        value = value.reshape(rows, outer, 2, 4, shard).transpose(0, 1, 3, 2, 4)
        return value.reshape(rows, width)

    def own_rows(value):
        return lax.dynamic_slice_in_dim(value, lane * piece, piece, 0)

    def all_lanes(value):
        pair = jnp.stack([value, over_x(value)])
        four = jnp.stack([pair, over_c(pair)], axis=1)
        four = jnp.where(lane >= 2, four[::-1], four)
        four = jnp.where(lane % 2 == 1, four[:, ::-1], four)
        return four.reshape((4 * value.shape[0],) + value.shape[1:])

    def exchange(parts, ready=None):
        return [parts[0]] + along_z(parts[1:], ready)

    def shares(total, ready=None):
        return exchange(
            [lax.dynamic_index_in_dim(total, at ^ step, 0, keepdims=False) for step in range(4)],
            ready,
        )

    span_places = jnp.repeat(span_map % (ROW_LEN // SPAN), SPAN)
    input_cube = attention_input.transpose(1, 0, 2)
    first_packed = pack_attention(
        at_word,
        input_cube,
        attention_output,
        norm_params,
        jnp.stack([segment_ids, span_places]),
    )
    first_parts = exchange(first_packed)
    own_tokens = to_relative(after(own_rows(tokens), first_packed[0]))
    second_packed = pack(after(at_word, own_tokens), expand_weight, reduce_weight)
    group_tokens = gather_tokens(after(own_tokens, second_packed[0], *first_parts[1:]))
    second_parts = exchange(second_packed, first_parts[1:])
    own_cotangent = to_relative(after(own_rows(cotangent), second_packed[0]))
    (first_own,) = assemble(at_word, [after(first_parts[0], own_cotangent)] + first_parts[1:])
    low = gather_groups(first_own)
    group_cotangent = gather_tokens(after(own_cotangent, first_own))

    aux = jnp.stack([low[0, t][0][:, shard:] for t in range(groups)])
    norm_values = aux[:, :, :4, :shard].transpose(2, 0, 1, 3).reshape(4, width).astype(F32)

    marks = aux[:, :, 8:10, : 4 * piece].astype(jnp.int32)
    inside = jnp.arange(4 * piece, dtype=jnp.int32) % SPAN
    marks = jnp.stack([marks[:, :, 0], marks[:, :, 1] * SPAN + inside])
    marks = marks.reshape(2, groups, 4, 2, 2, piece)
    marks = jnp.where(lane >= 2, marks[:, :, :, ::-1], marks)
    marks = marks.transpose(0, 3, 1, 2, 4, 5)
    query_marks = marks[:, 0, 0].reshape(2, -1).T
    key_marks = marks.reshape(2, -1)

    normed_one, queries, own_kv = project(
        after(group_tokens, key_marks, *second_parts[1:]), norm_values, low, shard, head
    )
    kv_low = gather_groups(own_kv)
    expand_own, reduce_own = assemble(
        at_word, [after(second_parts[0], own_kv)] + second_parts[1:], 2
    )
    expand_low = gather_groups(expand_own, kv_low[1, 1])
    reduce_low = gather_groups(reduce_own, expand_low[1, 1])
    attended, mixed, logsum = attend(
        after(queries, expand_own, group_cotangent), kv_low, query_marks, key_marks, scaling
    )
    branch = scatter_tokens(to_features(mixed, low, shard, (head, 3), width))
    middle = own_tokens.astype(F32) + branch.astype(F32)

    shape_two, scale_two = normalize(after(middle, *first_level(reduce_low)))
    normed_two = gather_tokens((shape_two * norm_values[2] + norm_values[3]).astype(BF16))
    active_grad = to_units(group_cotangent, reduce_low, shard, (units, 0), F32)
    active, hidden_grad, second_terms = feed_forward(
        normed_two, active_grad, expand_low, shard, units
    )
    second_grad = scatter_tokens(second_terms)
    reduce_pieces = weight_grads([(group_cotangent, active)], groups)
    reduce_sum, reduce_first, reduce_came, reduce_sent = reduce_groups(reduce_pieces)
    expand_pieces = weight_grads([(normed_two, after(hidden_grad, reduce_pieces[0, 0]))], groups)
    feed_terms = to_features(
        after(active, expand_pieces[0, 0]), reduce_low, shard, (units, 0), width
    )
    middle_part, gain_two, bias_two = norm_back(
        shape_two, scale_two, norm_values[2], after(second_grad, feed_terms, *reduce_sent).astype(F32)
    )
    middle_grad = own_cotangent.astype(F32) + middle_part
    branch_grad = gather_tokens(middle_grad.astype(BF16))
    expand_sum, _, expand_came, expand_sent = reduce_groups(expand_pieces, reduce_came)
    feed = scatter_tokens(after(feed_terms, branch_grad))

    mixed_grad = to_units(
        after(branch_grad, reduce_sum, *expand_sent), low, shard, (head, 3), BF16
    )
    reduce_shares = shares(reduce_sum)
    query_grad, kv_pieces = attend_back(
        queries, kv_low, query_marks, key_marks, attended, logsum, mixed_grad, scaling
    )
    expand_shares = shares(expand_sum, reduce_shares[1:])
    own_kv_grad, _, kv_came, _ = reduce_groups(
        kv_pieces, expand_came + tuple(reduce_shares[1:]), (), expand_shares[1:]
    )
    query_pieces = weight_grads(
        [(branch_grad, after(mixed, kv_pieces[1, 1])), (normed_one, query_grad)], groups
    )
    query_sum, _, query_came, _ = reduce_groups(query_pieces, kv_came)
    output = lax.all_gather(
        to_natural((middle + feed.astype(F32)).astype(BF16)), "mp", axis=0, tiled=True
    )
    first_terms, norm_sums = project_back(
        after(query_grad, output, query_pieces[0, 0]), own_kv_grad, group_tokens, low, shard, head
    )
    first_grad = scatter_tokens(first_terms)
    all_sums = jnp.concatenate([norm_sums, gain_two[None], bias_two[None]])
    shape_one, scale_one = normalize(own_tokens.astype(F32))
    pair_pieces = weight_grads(
        [(normed_one, own_kv_grad)], groups, all_sums
    )
    pair_sum, _, _, pair_sent = reduce_groups(pair_pieces, query_came)
    query_shares = shares(after(query_sum, *pair_sent))
    pair_shares = shares(pair_sum)
    share_norm = sum(part[shard : shard + 4, :shard].astype(F32) for part in pair_shares)
    share_norm = share_norm + over_c(share_norm)
    share_norm = share_norm + over_x(share_norm)

    reduce_new = adam(
        at_word,
        (reduce_weight, reduce_first_moment, reduce_second),
        reduce_rate,
        "turned",
        [(reduce_shares, 0, units)],
    )
    output_new = adam(
        at_word,
        (attention_output, attention_output_first, attention_output_second),
        output_rate,
        "turned",
        [(query_shares, 0, head)],
    )
    expand_new = adam(
        at_word,
        (expand_weight, expand_first_moment, expand_second),
        expand_rate,
        "plain",
        [(expand_shares, 0, units)],
    )
    input_part, _, _ = norm_back(
        shape_one, scale_one, norm_values[0], after(first_grad, reduce_new[0], expand_new[0]).astype(F32)
    )
    input_grad = all_lanes(to_natural((middle_grad + input_part).astype(BF16))).astype(F32)
    input_new = adam(
        at_word,
        (
            input_cube,
            attention_input_first.transpose(1, 0, 2),
            attention_input_second.transpose(1, 0, 2),
        ),
        input_rate,
        "cube",
        [(query_shares, head, 2 * head), (pair_shares, 0, 2 * head)],
    )
    norm_new = adamw_update(norm_params, norm_first, norm_second, share_norm, gain_rate, 0.0)
    return (
        output,
        input_grad,
        *[array.transpose(1, 0, 2) for array in input_new],
        *output_new,
        *expand_new,
        *reduce_new,
        *norm_new,
    )


def solution(mesh):
    rows, vectors, norms = P("fsdp", None), P("fsdp"), P(None, "fsdp")
    cube, across, down = P("fsdp", None, "mp"), P("fsdp", "mp"), P("mp", "fsdp")
    return jax.shard_map(
        local,
        mesh=mesh,
        in_specs=(
            (rows, rows, vectors, vectors)
            + (norms,) * 3
            + (cube,) * 3
            + (down,) * 3
            + (across,) * 3
            + (down,) * 3
        ),
        out_specs=(
            (rows, rows) + (cube,) * 4 + (down,) * 4 + (across,) * 4 + (down,) * 4 + (norms,) * 3
        ),
        check_vma=False,
    )
```

time: 620 us -> 547 us (0.88)
  starting transfers between devices: 186 us -> 74.6 us
  Pallas kernels: 18.3 us -> 125 us
  matrix products: 66.6 us -> 0 us
  other arithmetic: 57.9 us -> 37.3 us
  waiting for transfers between devices: 237 us -> 252 us
  between operations: 3.25 us -> 15.2 us
  local copies, waits for them, and re-layouts: 40.7 us -> 32.8 us
    ppermute x113 -> x58, starting transfers between devices: 186 us -> 73.5 us  [swap(): return lax.ppermute(value, axis, [(i, i ^ mask) for i in range(size)])]
    pallas_call x2 -> x21, Pallas kernels: 18.3 us -> 125 us  [the longest x4 25.5 us: adam(): pl.pallas_call(partial(adam_kernel, rate, shape, columns), grid_spec=pltp...]
    dot_general x12 -> x0, matrix products: 66.6 us -> none  [dot(): lax.dot_general(left, right, (dims, ((), ())), preferred_element_type=F32)]
    all_gather x0 -> x5, waiting for transfers between devices: none -> 47.5 us  [the longest x4 47.5 us: gather_tokens(): lax.all_gather(own, ('fsdp', 'mp'), axis_index_groups=token_groups(), axi...]
    ppermute x113 -> x58, waiting for transfers between devices: 237 us -> 202 us  [swap(): return lax.ppermute(value, axis, [(i, i ^ mask) for i in range(size)])]
    convert_element_type x5 -> x6, other arithmetic: 17.7 us -> 5.42 us  [the longest x1 2.01 us: local(): branch_grad = gather_tokens(middle_grad.astype(BF16))]
    dynamic_update_slice x25 -> x0, local copies, waits for them, and re-layouts: 6.38 us -> none  [place_blocks(): lax.dynamic_update_slice_in_dim(whole, block, (at ^ step) * size, axis)]
  transfers between devices with their start and end apart: 113 -> 67, of which waited for: 48 -> 33; matrix products, arithmetic and copies ran while one was open for 18% -> 9% of each run, Pallas kernels for 3% -> 17%
where the time goes in v2:
time: 547 us; the launch traced here: 537 us
  waiting for transfers between devices  252 us (46%)
  Pallas kernels  125 us (23%)
  starting transfers between devices  74.6 us (14%)
  other arithmetic  37.3 us (7%)
  local copies, waits for them, and re-layouts  32.8 us (6%)
  between operations  15.2 us (3%)
    ppermute x58, waiting for transfers between devices, swap(): return lax.ppermute(value, axis, [(i, i ^ mask) for i in range(size)])  202 us
    ppermute x58, starting transfers between devices, swap(): return lax.ppermute(value, axis, [(i, i ^ mask) for i in range(size)])  73.5 us
    all_gather x4, waiting for transfers between devices, gather_tokens(): lax.all_gather(own, ('fsdp', 'mp'), axis_index_groups=token_groups(), axi...  47.5 us
    pallas_call x4, Pallas kernels, adam(): pl.pallas_call(partial(adam_kernel, rate, shape, columns), grid_spec=pltp...  25.5 us
    pallas_call x4, Pallas kernels, weight_grads(): pl.pallas_call(partial(grads_kernel, groups, len(pairs), extra), grid=(gr...  22.5 us
    pallas_call x1, Pallas kernels, attend_back(): pl.pallas_call(partial(attend_back_kernel, scaling, layout), grid=(2, cou...  12.4 us
  transfers between devices with their start and end apart: 67, of which 33 were waited for; matrix products, arithmetic and copies ran while one was open for 9% of the time, Pallas kernels for 17%

profile of v2, /device:TPU:9, one launch (start us, length us, event | category | flops | bytes accessed | tf_op | source)
XLA Modules:
  0.0 536.7 jit_solution(17901110044825282740)
XLA Ops:
  18.4 4.4 pack.1
  27.6 11.8 %collective-permute-done.2.refs_3_ = bf16[272,512]{1,0:T(8,128)(2,1)S(1)} collective-permute-done((bf16[272,512]{1,0:T(8,128)(2,1)}, bf16[272,512]{1,0:T(8,128)(2,1)S(1)}, u32[]{:S(2)}, u32[]{:S(2)}) %collective-permute-start.2) | collective-permute-done | bytes 278560 | tf_op jit(solution)/shard_map/ppermute | solution.py:37
  50.3 18.0 %collective-permute-done.3.refs_1_ = bf16[4,272,512]{2,1,0:T(8,128)(2,1)S(1)} collective-permute-done((bf16[4,272,512]{2,1,0:T(8,128)(2,1)}, bf16[4,272,512]{2,1,0:T(8,128)(2,1)S(1)}, u32[]{:S(2)}, u32[]{:S(2)}) %collective-permute-start.3) | collective-permute-done | bytes 1114144 | tf_op jit(solution)/shard_map/ppermute | solution.py:37
  81.7 5.6 %collective-permute-done.5.refs_2_ = bf16[256,1024]{1,0:T(8,128)(2,1)} collective-permute-done((bf16[256,1024]{1,0:T(8,128)(2,1)}, bf16[256,1024]{1,0:T(8,128)(2,1)}, u32[]{:S(2)}, u32[]{:S(2)}) %collective-permute-start.5) | collective-permute-done | bytes 524320 | tf_op jit(solution)/shard_map/ppermute | solution.py:37
  87.2 24.5 %collective-permute-done.6.refs_3_ = bf16[256,1024]{1,0:T(8,128)(2,1)} collective-permute-done((bf16[256,1024]{1,0:T(8,128)(2,1)}, bf16[256,1024]{1,0:T(8,128)(2,1)}, u32[]{:S(2)}, u32[]{:S(2)}) %collective-permute-start.6) | collective-permute-done | bytes 524320 | tf_op jit(solution)/shard_map/ppermute | solution.py:37
  112.8 6.7 %project.1 = (bf16[512,2048]{1,0:T(8,128)(2,1)}, bf16[512,256]{1,0:T(8,128)(2,1)}, bf16[2,512,256]{2,1,0:T(8,128)(2,1)}) custom-call(bf16[512,2048]{1,0:T(8,128)(2,1)} %all-gather.6.cloned.1.call-done.tokens_ref, f32[4,2048]{1,0:T(4,128)} %bitcast.112, bf16[4,272,512]{2,1,0:T(8,128)(2,1)} %assemble.2.refs_0_, bf16[4,272,512]{2,1,0:T(8,128)(2,1)} %copy-done, ...), custom_call_target="tpu_custom_call" | custom-call | flops 1 | bytes 1 | tf_op jit(solution)/shard_map/project/pallas_call | solution.py:378
  119.5 12.0 %collective-permute-done.11.refs_2_ = bf16[2,512,256]{2,1,0:T(8,128)(2,1)S(1)} collective-permute-done((bf16[2,512,256]{2,1,0:T(8,128)(2,1)}, bf16[2,512,256]{2,1,0:T(8,128)(2,1)S(1)}, u32[]{:S(2)}, u32[]{:S(2)}) %collective-permute-start.11) | collective-permute-done | bytes 524320 | tf_op jit(solution)/shard_map/ppermute | solution.py:37
  138.2 8.3 %attend.1 = (f32[512,256]{1,0:T(8,128)}, bf16[512,256]{1,0:T(8,128)(2,1)}, f32[2,512,1]{2,1,0:T(8,128)}) custom-call(bf16[512,256]{1,0:T(8,128)(2,1)} %get-tuple-element.134.q_ref, s32[512,2]{1,0:T(8,128)} %bitcast.100, s32[2,2048]{1,0:T(2,128)} %reshape.168.km_ref, bf16[2,512,256]{2,1,0:T(8,128)(2,1)} %get-tuple-element.130.refs_0_, ...), custom_call_target="tpu_custom_call" | custom-call | flops 1 | bytes 1 | tf_op jit(solution)/shard_map/attend/pallas_call | solution.py:670
  153.2 18.9 %collective-permute-done.14.refs_2_ = bf16[4,256,512]{2,1,0:T(8,128)(2,1)S(1)} collective-permute-done((bf16[4,256,512]{2,1,0:T(8,128)(2,1)S(1)}, bf16[4,256,512]{2,1,0:T(8,128)(2,1)S(1)}, u32[]{:S(2)}, u32[]{:S(2)}) %collective-permute-start.14) | collective-permute-done | bytes 1048608 | tf_op jit(solution)/shard_map/ppermute | solution.py:37
  174.5 11.3 %collective-permute-done.15.refs_3_ = bf16[2,256,512]{2,1,0:T(8,128)(2,1)S(1)} collective-permute-done((bf16[2,256,512]{2,1,0:T(8,128)(2,1)S(1)}, bf16[2,256,512]{2,1,0:T(8,128)(2,1)S(1)}, u32[]{:S(2)}, u32[]{:S(2)}) %collective-permute-start.15) | collective-permute-done | bytes 524320 | tf_op jit(solution)/shard_map/ppermute | solution.py:37
  189.6 18.2 %collective-permute-done.18.refs_2_ = bf16[4,256,512]{2,1,0:T(8,128)(2,1)S(1)} collective-permute-done((bf16[4,256,512]{2,1,0:T(8,128)(2,1)}, bf16[4,256,512]{2,1,0:T(8,128)(2,1)S(1)}, u32[]{:S(2)}, u32[]{:S(2)}) %collective-permute-start.18) | collective-permute-done | bytes 1048608 | tf_op jit(solution)/shard_map/ppermute | solution.py:37
  211.1 7.1 %collective-permute-done.20.refs_3_ = bf16[2,256,512]{2,1,0:T(8,128)(2,1)S(1)} collective-permute-done((bf16[2,256,512]{2,1,0:T(8,128)(2,1)S(1)}, bf16[2,256,512]{2,1,0:T(8,128)(2,1)S(1)}, u32[]{:S(2)}, u32[]{:S(2)}) %collective-permute-start.20) | collective-permute-done | bytes 524320 | tf_op jit(solution)/shard_map/ppermute | solution.py:37
  219.8 6.2 %to_units.2.pull_ref = f32[512,1024]{1,0:T(8,128)} custom-call(bf16[512,2048]{1,0:T(8,128)(2,1)} %all-gather.8.cloned.1.call-done.value_ref.refs_0_, bf16[4,256,512]{2,1,0:T(8,128)(2,1)} %get-tuple-element.138.refs_0_, bf16[4,256,512]{2,1,0:T(8,128)(2,1)} %copy-done.5, bf16[4,256,512]{2,1,0:T(8,128)(2,1)} %copy-done.4, bf16[2,256,512]{2,1,0:T(8,128)(2,1)} %copy-done.12, ...), custom_call_target="tpu_custom_call" | custom-call | flops 1 | bytes 1 | tf_op jit(solution)/shard_map/to_units/pallas_call | solution.py:409
  226.1 16.4 %all-gather.10.cloned.1.call-done.value_ref.refs_0_ = bf16[512,2048]{1,0:T(8,128)(2,1)} async-done(((bf16[64,2048]{1,0:T(8,128)(2,1)}), bf16[512,2048]{1,0:T(8,128)(2,1)}) %all-gather.10.cloned.1.call-update) | async-done | bytes 2097168 | tf_op jit(solution)/shard_map/all_gather | solution.py:174
  242.4 9.7 %feed_forward.1 = (bf16[512,1024]{1,0:T(8,128)(2,1)}, bf16[512,1024]{1,0:T(8,128)(2,1)}, bf16[512,2048]{1,0:T(8,128)(2,1)}) custom-call(bf16[512,2048]{1,0:T(8,128)(2,1)} %all-gather.10.cloned.1.call-done.value_ref.refs_0_, f32[512,1024]{1,0:T(8,128)} %to_units.2.pull_ref, bf16[4,256,512]{2,1,0:T(8,128)(2,1)} %get-tuple-element.137.refs_0_, ...), custom_call_target="tpu_custom_call" | custom-call | flops 1 | bytes 1 | tf_op jit(solution)/shard_map/feed_forward/pallas_call | solution.py:472
  252.2 6.2 %weight_grads.4 = (bf16[4,256,512]{2,1,0:T(8,128)(2,1)}, bf16[4,256,512]{2,1,0:T(8,128)(2,1)}, bf16[4,256,512]{2,1,0:T(8,128)(2,1)}, bf16[4,256,512]{2,1,0:T(8,128)(2,1)}) custom-call(bf16[512,2048]{1,0:T(8,128)(2,1)} %all-gather.8.cloned.1.call-done.value_ref.refs_0_, bf16[512,1024]{1,0:T(8,128)(2,1)} %get-tuple-element.145.refs_1_.value_ref), custom_call_target="tpu_custom_call" | custom-call | flops 1 | bytes 1 | tf_op jit(solution)/shard_map/weight_grads/pallas_call | solution.py:564
  263.1 6.2 %weight_grads.5 = (bf16[4,256,512]{2,1,0:T(8,128)(2,1)}, bf16[4,256,512]{2,1,0:T(8,128)(2,1)}, bf16[4,256,512]{2,1,0:T(8,128)(2,1)}, bf16[4,256,512]{2,1,0:T(8,128)(2,1)}) custom-call(bf16[512,2048]{1,0:T(8,128)(2,1)} %all-gather.10.cloned.1.call-done.value_ref.refs_0_, bf16[512,1024]{1,0:T(8,128)(2,1)} %get-tuple-element.143.refs_1_), custom_call_target="tpu_custom_call" | custom-call | flops 1 | bytes 1 | tf_op jit(solution)/shard_map/weight_grads/pallas_call | solution.py:564
  269.3 6.1 %to_features.3 = bf16[512,2048]{1,0:T(8,128)(2,1)} custom-call(bf16[512,1024]{1,0:T(8,128)(2,1)} %get-tuple-element.145.refs_1_.value_ref, bf16[4,256,512]{2,1,0:T(8,128)(2,1)} %get-tuple-element.138.refs_0_, bf16[4,256,512]{2,1,0:T(8,128)(2,1)} %copy-done.5, bf16[4,256,512]{2,1,0:T(8,128)(2,1)} %copy-done.4, bf16[2,256,512]{2,1,0:T(8,128)(2,1)} %copy-done.12, ...), custom_call_target="tpu_custom_call" | custom-call | flops 1 | bytes 1 | tf_op jit(solution)/shard_map/to_features/pallas_call | solution.py:434
  287.8 31.1 %all-gather.12.cloned.1.call-done.value_ref.refs_0_ = bf16[512,2048]{1,0:T(8,128)(2,1)} async-done(((bf16[64,2048]{1,0:T(8,128)(2,1)}), bf16[512,2048]{1,0:T(8,128)(2,1)}) %all-gather.12.cloned.1.call-update) | async-done | bytes 2097168 | tf_op jit(solution)/shard_map/all_gather | solution.py:174
  323.3 10.8 %collective-permute-done.26 = bf16[2,256,512]{2,1,0:T(8,128)(2,1)S(1)} collective-permute-done((bf16[2,256,512]{2,1,0:T(8,128)(2,1)S(1)}, bf16[2,256,512]{2,1,0:T(8,128)(2,1)S(1)}, u32[]{:S(2)}, u32[]{:S(2)}) %collective-permute-start.26) | collective-permute-done | bytes 524320 | tf_op jit(solution)/shard_map/ppermute | solution.py:37
  343.8 15.3 %collective-permute-done.28 = bf16[4,256,512]{2,1,0:T(8,128)(2,1)} collective-permute-done((bf16[4,256,512]{2,1,0:T(8,128)(2,1)}, bf16[4,256,512]{2,1,0:T(8,128)(2,1)}, u32[]{:S(2)}, u32[]{:S(2)}) %collective-permute-start.28) | collective-permute-done | bytes 1048608 | tf_op jit(solution)/shard_map/ppermute | solution.py:37
  365.5 12.4 %attend_back.1 = (bf16[512,256]{1,0:T(8,128)(2,1)}, bf16[2,512,256]{2,1,0:T(8,128)(2,1)}, bf16[2,512,256]{2,1,0:T(8,128)(2,1)}, bf16[2,512,256]{2,1,0:T(8,128)(2,1)}, bf16[2,512,256]{2,1,0:T(8,128)(2,1)}) custom-call(bf16[512,256]{1,0:T(8,128)(2,1)} %get-tuple-element.134.q_ref, s32[512,2]{1,0:T(8,128)} %bitcast.101, s32[2,2048]{1,0:T(2,128)} %reshape.168.km_ref, ...), custom_call_target="tpu_custom_call" | custom-call | flops 1 | bytes 1 | tf_op jit(solution)/shard_map/attend_back/pallas_call | solution.py:702
  395.5 12.8 %collective-permute-done.36.refs_3_ = bf16[256,512]{1,0:T(8,128)(2,1)S(1)} collective-permute-done((bf16[256,512]{1,0:T(8,128)(2,1)S(1)}, bf16[256,512]{1,0:T(8,128)(2,1)S(1)}, u32[]{:S(2)}, u32[]{:S(2)}) %collective-permute-start.36) | collective-permute-done | bytes 262176 | tf_op jit(solution)/shard_map/ppermute | solution.py:37
  410.9 5.8 %weight_grads.6 = (bf16[4,256,256]{2,1,0:T(8,128)(2,1)}, bf16[4,256,256]{2,1,0:T(8,128)(2,1)}, bf16[4,256,256]{2,1,0:T(8,128)(2,1)}, bf16[4,256,256]{2,1,0:T(8,128)(2,1)}) custom-call(bf16[512,2048]{1,0:T(8,128)(2,1)} %all-gather.12.cloned.1.call-done.value_ref.refs_0_, bf16[512,2048]{1,0:T(8,128)(2,1)} %get-tuple-element.160.refs_1_.refs_0_, ...), custom_call_target="tpu_custom_call" | custom-call | flops 1 | bytes 1 | tf_op jit(solution)/shard_map/weight_grads/pallas_call | solution.py:564
  420.9 7.3 %project_back.1 = (bf16[512,2048]{1,0:T(8,128)(2,1)}, f32[2,2048]{1,0:T(2,128)}) custom-call(bf16[512,256]{1,0:T(8,128)(2,1)} %get-tuple-element.164.refs_3_.query_ref, bf16[2,512,256]{2,1,0:T(8,128)(2,1)} %add_convert_fusion.4.pair_ref.refs_1_, bf16[512,2048]{1,0:T(8,128)(2,1)} %all-gather.6.cloned.1.call-done.tokens_ref, ...), custom_call_target="tpu_custom_call" | custom-call | flops 1 | bytes 1 | tf_op jit(solution)/shard_map/project_back/pallas_call | solution.py:509
  437.8 4.3 weight_grads.7
  442.1 5.8 %collective-permute-done.45 = bf16[4,256,256]{2,1,0:T(8,128)(2,1)S(1)} collective-permute-done((bf16[4,256,256]{2,1,0:T(8,128)(2,1)S(1)}, bf16[4,256,256]{2,1,0:T(8,128)(2,1)S(1)}, u32[]{:S(2)}, u32[]{:S(2)}) %collective-permute-start.45) | collective-permute-done | bytes 524320 | tf_op jit(solution)/shard_map/ppermute | solution.py:37
  449.9 7.4 %adam.4 = (f32[2048,256]{1,0:T(8,128)}, f32[2048,256]{1,0:T(8,128)}, f32[2048,256]{1,0:T(8,128)}, bf16[2048,256]{1,0:T(8,128)(2,1)}) custom-call(s32[1]{0:T(128)} %bitcast.at_ref, bf16[256,512]{1,0:T(8,128)(2,1)} %get-tuple-element.219.refs_0_, bf16[256,512]{1,0:T(8,128)(2,1)} %collective-permute-done.30.refs_1_, ...), custom_call_target="tpu_custom_call" | custom-call | flops 1 | bytes 1 | tf_op jit(solution)/shard_map/adam/pallas_call | solution.py:777
  457.3 7.7 %adam.5 = (f32[256,2048]{1,0:T(8,128)}, f32[256,2048]{1,0:T(8,128)}, f32[256,2048]{1,0:T(8,128)}, bf16[256,2048]{1,0:T(8,128)(2,1)}) custom-call(s32[1]{0:T(128)} %bitcast.at_ref, bf16[256,512]{1,0:T(8,128)(2,1)} %get-tuple-element.215.refs_0_, bf16[256,512]{1,0:T(8,128)(2,1)} %copy-done.49, bf16[256,512]{1,0:T(8,128)(2,1)} %copy-done.50, ...), custom_call_target="tpu_custom_call" | custom-call | flops 1 | bytes 1 | tf_op jit(solution)/shard_map/adam/pallas_call | solution.py:777
  487.3 11.5 %collective-permute-start.41 = (bf16[2,64,2048]{2,1,0:T(8,128)(2,1)S(1)}, bf16[2,64,2048]{2,1,0:T(8,128)(2,1)S(1)}, u32[]{:S(2)}, u32[]{:S(2)}) collective-permute-start(bf16[2,64,2048]{2,1,0:T(8,128)(2,1)S(1)} %get-tuple-element.240), channel_id=1, source_target_pairs={{0,1},{1,0},{2,3},{3,2},{4,5},{5,4},{6,7},{7,6},{8,9},{9,8},{10,11... | collective-permute-start | bytes 1572872 | tf_op jit(solution)/shard_map/ppermute | solution.py:37
  502.9 9.8 %collective-permute-start.56 = (f32[4,256]{1,0:T(4,128)S(1)}, f32[4,256]{1,0:T(4,128)S(1)}, u32[]{:S(2)}, u32[]{:S(2)}) collective-permute-start(f32[4,256]{1,0:T(4,128)S(1)} %fusion.24), channel_id=1, source_target_pairs={{0,1},{1,0},{2,3},{3,2},{4,5},{5,4},{6,7},{7,6},{8,9},{9,8},{10,11... | collective-permute-start | bytes 12296 | tf_op jit(solution)/shard_map/ppermute | solution.py:37
  519.9 6.1 %adam.6 = (f32[3,256,512]{2,1,0:T(8,128)}, f32[3,256,512]{2,1,0:T(8,128)}, f32[3,256,512]{2,1,0:T(8,128)}, bf16[3,256,512]{2,1,0:T(8,128)(2,1)}) custom-call(s32[1]{0:T(128)} %bitcast.at_ref, bf16[256,256]{1,0:T(8,128)(2,1)} %get-tuple-element.236.refs_0_, bf16[256,256]{1,0:T(8,128)(2,1)} %copy-done.35, bf16[256,256]{1,0:T(8,128)(2,1)} %copy-done.36, ...), custom_call_target="tpu_custom_call" | custom-call | flops 1 | bytes 1 | tf_op jit(solution)/shard_map/adam/pallas_call | solution.py:777
  (374 shorter events, 175.8 us)
Async XLA Ops:
  7.2 104.6 %all-gather.6.cloned.1.call-start = ((), (), s32[]{:S(2)}) async-start(), calls=%async_computation.4 | async-start | bytes 2359296 | tf_op jit(solution)/shard_map/all_gather | solution.py:174
  15.3 24.1 %collective-permute-start.2 = (bf16[272,512]{1,0:T(8,128)(2,1)}, bf16[272,512]{1,0:T(8,128)(2,1)S(1)}, u32[]{:S(2)}, u32[]{:S(2)}) collective-permute-start(bf16[272,512]{1,0:T(8,128)(2,1)} %get-tuple-element.118), channel_id=1, source_target_pairs={{0,24},{4,28},{8,16},{12,20},{16,8},{20,12},{24,0},{28,4},{1,25},{... | collective-permute-start | bytes 835592 | tf_op jit(solution)/shard_map/ppermute | solution.py:37
  39.4 97.9 %all-gather.8.cloned.1.call-start = ((), (), s32[]{:S(2)}) async-start(), calls=%async_computation.5 | async-start | bytes 2359296 | tf_op jit(solution)/shard_map/all_gather | solution.py:174
  43.7 144.7 %reduce-scatter.5.cloned.1.call-start = ((), (), s32[]{:S(2)}) async-start(), calls=%async_computation.6 | async-start | bytes 2359296 | tf_op jit(solution)/shard_map/reduce_scatter | solution.py:180
  43.7 24.6 %collective-permute-start.3 = (bf16[4,272,512]{2,1,0:T(8,128)(2,1)}, bf16[4,272,512]{2,1,0:T(8,128)(2,1)S(1)}, u32[]{:S(2)}, u32[]{:S(2)}) collective-permute-start(bf16[4,272,512]{2,1,0:T(8,128)(2,1)} %assemble.2.refs_0_), channel_id=1, source_target_pairs={{0,4},{4,0},{8,12},{12,8},{16,20},{20,16},{24,28},{28,24},{1,5},{5... | collective-permute-start | bytes 3342344 | tf_op jit(solution)/shard_map/ppermute | solution.py:37
  45.1 24.3 %collective-permute-start.7 = (bf16[4,272,512]{2,1,0:T(8,128)(2,1)}, bf16[4,272,512]{2,1,0:T(8,128)(2,1)S(1)}, u32[]{:S(2)}, u32[]{:S(2)}) collective-permute-start(bf16[4,272,512]{2,1,0:T(8,128)(2,1)} %assemble.2.refs_0_), channel_id=1, source_target_pairs={{0,2},{1,3},{2,0},{3,1},{4,6},{5,7},{6,4},{7,5},{8,10},{9,11},{10,... | collective-permute-start | bytes 3342344 | tf_op jit(solution)/shard_map/ppermute | solution.py:37
  46.9 34.8 %collective-permute-start.4 = (bf16[256,1024]{1,0:T(8,128)(2,1)}, bf16[256,1024]{1,0:T(8,128)(2,1)}, u32[]{:S(2)}, u32[]{:S(2)}) collective-permute-start(bf16[256,1024]{1,0:T(8,128)(2,1)} %get-tuple-element.123), channel_id=1, source_target_pairs={{0,8},{4,12},{8,0},{12,4},{16,24},{20,28},{24,16},{28,20},{1,9},{5... | collective-permute-start | bytes 1572872 | tf_op jit(solution)/shard_map/ppermute | solution.py:37
  46.9 40.4 %collective-permute-start.5 = (bf16[256,1024]{1,0:T(8,128)(2,1)}, bf16[256,1024]{1,0:T(8,128)(2,1)}, u32[]{:S(2)}, u32[]{:S(2)}) collective-permute-start(bf16[256,1024]{1,0:T(8,128)(2,1)} %get-tuple-element.125), channel_id=1, source_target_pairs={{0,16},{4,20},{8,24},{12,28},{16,0},{20,4},{24,8},{28,12},{1,17},{... | collective-permute-start | bytes 1572872 | tf_op jit(solution)/shard_map/ppermute | solution.py:37
  49.3 62.4 %collective-permute-start.6 = (bf16[256,1024]{1,0:T(8,128)(2,1)}, bf16[256,1024]{1,0:T(8,128)(2,1)}, u32[]{:S(2)}, u32[]{:S(2)}) collective-permute-start(bf16[256,1024]{1,0:T(8,128)(2,1)} %get-tuple-element.127), channel_id=1, source_target_pairs={{0,24},{4,28},{8,16},{12,20},{16,8},{20,12},{24,0},{28,4},{1,25},{... | collective-permute-start | bytes 1572872 | tf_op jit(solution)/shard_map/ppermute | solution.py:37
  70.2 41.6 %collective-permute-start.8 = (bf16[2,272,512]{2,1,0:T(8,128)(2,1)}, bf16[2,272,512]{2,1,0:T(8,128)(2,1)S(1)}, u32[]{:S(2)}, u32[]{:S(2)}) collective-permute-start(bf16[2,272,512]{2,1,0:T(8,128)(2,1)} %slice.217), channel_id=1, source_target_pairs={{0,4},{4,0},{8,12},{12,8},{16,20},{20,16},{24,28},{28,24},{1,5},{5... | collective-permute-start | bytes 1671176 | tf_op jit(solution)/shard_map/ppermute | solution.py:37
  72.2 39.5 %collective-permute-start.9 = (bf16[2,272,512]{2,1,0:T(8,128)(2,1)}, bf16[2,272,512]{2,1,0:T(8,128)(2,1)S(1)}, u32[]{:S(2)}, u32[]{:S(2)}) collective-permute-start(bf16[2,272,512]{2,1,0:T(8,128)(2,1)} %slice.218), channel_id=1, source_target_pairs={{0,2},{1,3},{2,0},{3,1},{4,6},{5,7},{6,4},{7,5},{8,10},{9,11},{10,... | collective-permute-start | bytes 1671176 | tf_op jit(solution)/shard_map/ppermute | solution.py:37
  150.2 92.2 %all-gather.10.cloned.1.call-start = ((), (), s32[]{:S(2)}) async-start(), calls=%async_computation.7 | async-start | bytes 2359296 | tf_op jit(solution)/shard_map/all_gather | solution.py:174
  151.4 20.8 %collective-permute-start.14 = (bf16[4,256,512]{2,1,0:T(8,128)(2,1)S(1)}, bf16[4,256,512]{2,1,0:T(8,128)(2,1)S(1)}, u32[]{:S(2)}, u32[]{:S(2)}) collective-permute-start(bf16[4,256,512]{2,1,0:T(8,128)(2,1)S(1)} %copy-done.27), channel_id=1, source_target_pairs={{0,2},{1,3},{2,0},{3,1},{4,6},{5,7},{6,4},{7,5},{8,10},{9,11},{10,... | collective-permute-start | bytes 3145736 | tf_op jit(solution)/shard_map/ppermute | solution.py:37
  152.5 21.4 %collective-permute-start.16 = (bf16[4,256,512]{2,1,0:T(8,128)(2,1)S(1)}, bf16[4,256,512]{2,1,0:T(8,128)(2,1)S(1)}, u32[]{:S(2)}, u32[]{:S(2)}) collective-permute-start(bf16[4,256,512]{2,1,0:T(8,128)(2,1)S(1)} %copy-done.27), channel_id=1, source_target_pairs={{0,4},{4,0},{8,12},{12,8},{16,20},{20,16},{24,28},{28,24},{1,5},{5... | collective-permute-start | bytes 3145736 | tf_op jit(solution)/shard_map/ppermute | solution.py:37
  186.8 21.0 %collective-permute-start.18 = (bf16[4,256,512]{2,1,0:T(8,128)(2,1)}, bf16[4,256,512]{2,1,0:T(8,128)(2,1)S(1)}, u32[]{:S(2)}, u32[]{:S(2)}) collective-permute-start(bf16[4,256,512]{2,1,0:T(8,128)(2,1)} %get-tuple-element.138.refs_0_), channel_id=1, source_target_pairs={{0,2},{1,3},{2,0},{3,1},{4,6},{5,7},{6,4},{7,5},{8,10},{9,11},{10,... | collective-permute-start | bytes 3145736 | tf_op jit(solution)/shard_map/ppermute | solution.py:37
  186.8 21.0 %collective-permute-start.19 = (bf16[4,256,512]{2,1,0:T(8,128)(2,1)}, bf16[4,256,512]{2,1,0:T(8,128)(2,1)S(1)}, u32[]{:S(2)}, u32[]{:S(2)}) collective-permute-start(bf16[4,256,512]{2,1,0:T(8,128)(2,1)} %get-tuple-element.138.refs_0_), channel_id=1, source_target_pairs={{0,4},{4,0},{8,12},{12,8},{16,20},{20,16},{24,28},{28,24},{1,5},{5... | collective-permute-start | bytes 3145736 | tf_op jit(solution)/shard_map/ppermute | solution.py:37
  209.2 72.7 %reduce-scatter.7.cloned.1.call-start = ((), (), s32[]{:S(2)}) async-start(), calls=%async_computation.8 | async-start | bytes 2359296 | tf_op jit(solution)/shard_map/reduce_scatter | solution.py:180
  252.2 66.7 %all-gather.12.cloned.1.call-start = ((), (), s32[]{:S(2)}) async-start(), calls=%async_computation.9 | async-start | bytes 2359296 | tf_op jit(solution)/shard_map/all_gather | solution.py:174
  285.3 94.7 %reduce-scatter.9.cloned.1.call-start = ((), (), s32[]{:S(2)}) async-start(), calls=%async_computation.10 | async-start | bytes 2359296 | tf_op jit(solution)/shard_map/reduce_scatter | solution.py:180
  285.4 34.0 %collective-permute-start.25 = (bf16[4,256,512]{2,1,0:T(8,128)(2,1)}, bf16[4,256,512]{2,1,0:T(8,128)(2,1)}, u32[]{:S(2)}, u32[]{:S(2)}) collective-permute-start(bf16[4,256,512]{2,1,0:T(8,128)(2,1)} %pad_maximum_fusion.1), channel_id=1, source_target_pairs={{0,4},{4,0},{8,12},{12,8},{16,20},{20,16},{24,28},{28,24},{1,5},{5... | collective-permute-start | bytes 3145736 | tf_op jit(solution)/shard_map/ppermute | solution.py:37
  286.5 33.0 %collective-permute-start.24 = (bf16[4,256,512]{2,1,0:T(8,128)(2,1)}, bf16[4,256,512]{2,1,0:T(8,128)(2,1)}, u32[]{:S(2)}, u32[]{:S(2)}) collective-permute-start(bf16[4,256,512]{2,1,0:T(8,128)(2,1)} %pad_maximum_fusion), channel_id=1, source_target_pairs={{0,2},{1,3},{2,0},{3,1},{4,6},{5,7},{6,4},{7,5},{8,10},{9,11},{10,... | collective-permute-start | bytes 3145736 | tf_op jit(solution)/shard_map/ppermute | solution.py:37
  319.0 101.9 %all-gather.14.cloned.1.call-start = ((), (), s32[]{:S(2)}) async-start(), calls=%async_computation.11 | async-start | bytes 1310720 | tf_op jit(solution)/shard_map/all_gather | solution.py:960
  335.2 23.9 %collective-permute-start.28 = (bf16[4,256,512]{2,1,0:T(8,128)(2,1)}, bf16[4,256,512]{2,1,0:T(8,128)(2,1)}, u32[]{:S(2)}, u32[]{:S(2)}) collective-permute-start(bf16[4,256,512]{2,1,0:T(8,128)(2,1)} %pad_maximum_fusion.2), channel_id=1, source_target_pairs={{0,2},{1,3},{2,0},{3,1},{4,6},{5,7},{6,4},{7,5},{8,10},{9,11},{10,... | collective-permute-start | bytes 3145736 | tf_op jit(solution)/shard_map/ppermute | solution.py:37
  336.7 23.5 %collective-permute-start.29 = (bf16[4,256,512]{2,1,0:T(8,128)(2,1)S(1)}, bf16[4,256,512]{2,1,0:T(8,128)(2,1)S(1)}, u32[]{:S(2)}, u32[]{:S(2)}) collective-permute-start(bf16[4,256,512]{2,1,0:T(8,128)(2,1)S(1)} %pad_maximum_fusion.3), channel_id=1, source_target_pairs={{0,4},{4,0},{8,12},{12,8},{16,20},{20,16},{24,28},{28,24},{1,5},{5... | collective-permute-start | bytes 3145736 | tf_op jit(solution)/shard_map/ppermute | solution.py:37
  341.1 36.7 %collective-permute-start.30 = (bf16[256,512]{1,0:T(8,128)(2,1)}, bf16[256,512]{1,0:T(8,128)(2,1)}, u32[]{:S(2)}, u32[]{:S(2)}) collective-permute-start(bf16[256,512]{1,0:T(8,128)(2,1)} %get-tuple-element.222), channel_id=1, source_target_pairs={{0,8},{4,12},{8,0},{12,4},{16,24},{20,28},{24,16},{28,20},{1,9},{5... | collective-permute-start | bytes 786440 | tf_op jit(solution)/shard_map/ppermute | solution.py:37
  341.5 36.4 %collective-permute-start.31 = (bf16[256,512]{1,0:T(8,128)(2,1)S(1)}, bf16[256,512]{1,0:T(8,128)(2,1)}, u32[]{:S(2)}, u32[]{:S(2)}) collective-permute-start(bf16[256,512]{1,0:T(8,128)(2,1)S(1)} %get-tuple-element.221), channel_id=1, source_target_pairs={{0,16},{4,20},{8,24},{12,28},{16,0},{20,4},{24,8},{28,12},{1,17},{... | collective-permute-start | bytes 786440 | tf_op jit(solution)/shard_map/ppermute | solution.py:37
  343.0 34.8 %collective-permute-start.32 = (bf16[256,512]{1,0:T(8,128)(2,1)S(1)}, bf16[256,512]{1,0:T(8,128)(2,1)}, u32[]{:S(2)}, u32[]{:S(2)}) collective-permute-start(bf16[256,512]{1,0:T(8,128)(2,1)S(1)} %get-tuple-element.220), channel_id=1, source_target_pairs={{0,24},{4,28},{8,16},{12,20},{16,8},{20,12},{24,0},{28,4},{1,25},{... | collective-permute-start | bytes 786440 | tf_op jit(solution)/shard_map/ppermute | solution.py:37
  383.3 89.8 %reduce-scatter.11.cloned.1.call-start = ((), (), s32[]{:S(2)}) async-start(), calls=%async_computation.12 | async-start | bytes 2359296 | tf_op jit(solution)/shard_map/reduce_scatter | solution.py:180
  386.2 22.0 %collective-permute-start.36 = (bf16[256,512]{1,0:T(8,128)(2,1)S(1)}, bf16[256,512]{1,0:T(8,128)(2,1)S(1)}, u32[]{:S(2)}, u32[]{:S(2)}) collective-permute-start(bf16[256,512]{1,0:T(8,128)(2,1)S(1)} %get-tuple-element.170), channel_id=1, source_target_pairs={{0,24},{4,28},{8,16},{12,20},{16,8},{20,12},{24,0},{28,4},{1,25},{... | collective-permute-start | bytes 786440 | tf_op jit(solution)/shard_map/ppermute | solution.py:37
  387.1 22.3 %collective-permute-start.33 = (bf16[1,512,256]{2,1,0:T(8,128)(2,1)S(1)}, bf16[1,512,256]{2,1,0:T(8,128)(2,1)S(1)}, u32[]{:S(2)}, u32[]{:S(2)}) collective-permute-start(bf16[1,512,256]{2,1,0:T(8,128)(2,1)S(1)} %copy-done.48), channel_id=1, source_target_pairs={{0,4},{4,0},{8,12},{12,8},{16,20},{20,16},{24,28},{28,24},{1,5},{5... | collective-permute-start | bytes 786440 | tf_op jit(solution)/shard_map/ppermute | solution.py:37
  483.5 17.9 %collective-permute-start.54 = (bf16[272,256]{1,0:T(8,128)(2,1)}, bf16[272,256]{1,0:T(8,128)(2,1)S(1)}, u32[]{:S(2)}, u32[]{:S(2)}) collective-permute-start(bf16[272,256]{1,0:T(8,128)(2,1)} %get-tuple-element.228), channel_id=1, source_target_pairs={{0,16},{4,20},{8,24},{12,28},{16,0},{20,4},{24,8},{28,12},{1,17},{... | collective-permute-start | bytes 417800 | tf_op jit(solution)/shard_map/ppermute | solution.py:37
  487.3 39.4 %collective-permute-start.41 = (bf16[2,64,2048]{2,1,0:T(8,128)(2,1)S(1)}, bf16[2,64,2048]{2,1,0:T(8,128)(2,1)S(1)}, u32[]{:S(2)}, u32[]{:S(2)}) collective-permute-start(bf16[2,64,2048]{2,1,0:T(8,128)(2,1)S(1)} %get-tuple-element.240), channel_id=1, source_target_pairs={{0,1},{1,0},{2,3},{3,2},{4,5},{5,4},{6,7},{7,6},{8,9},{9,8},{10,11... | collective-permute-start | bytes 1572872 | tf_op jit(solution)/shard_map/ppermute | solution.py:37
  (95 other events, 901.5 us)
Sparse Core Ops, SparseCore 0:
  39.6 50.1 all-gather.5
  91.9 40.6 all-gather.7
  150.3 33.2 reduce-scatter.4
  209.3 33.0 all-gather.9
  252.3 29.5 reduce-scatter.6
  285.4 33.4 all-gather.11
  321.8 35.2 reduce-scatter.8
  383.5 18.4 all-gather.13
  428.3 33.4 reduce-scatter.10

commit v3 on v2

--- a/solution.py
+++ b/solution.py
@@ -28,6 +28,11 @@
 PARAMS = pltpu.CompilerParams(vmem_limit_bytes=60 << 20)
 SMALL = pl.CostEstimate(flops=1, bytes_accessed=1, transcendentals=0)
 
+
+def cost(microseconds):
+    return pl.CostEstimate(flops=int(microseconds * 1.15e9), bytes_accessed=1, transcendentals=0)
+
+
 Z_STEPS = (1, 2, 3)
 AUX = 16
 
@@ -65,7 +70,7 @@
     return bits
 
 
-def gather_groups(own, ready=()):
+def gather_groups(own, ready=(), second_ready=()):
     if ready:
         own = after(own, *ready)
     half = own.shape[0] // 2
@@ -74,7 +79,10 @@
         (0, 0): (own,),
         (1, 0): (from_x,),
         (0, 1): (from_y,),
-        (1, 1): (over_y(from_x[:half]), over_x(from_y[half:])),
+        (1, 1): (
+            over_y(after(from_x[:half], *second_ready)),
+            over_x(after(from_y[half:], *second_ready)),
+        ),
     }
     for bit in outer_bits():
         for (x, t), piece in list(pieces.items()):
@@ -91,18 +99,21 @@
     for bit in reversed(outer_bits()):
         for (x, t), piece in list(pieces.items()):
             if t & (bit // 4):
-                pieces[x, t ^ (bit // 4)] = add(pieces[x, t ^ (bit // 4)], swap(piece, "fsdp", bit))
+                pieces[x, t ^ (bit // 4)] = tuple(
+                    add(here, swap(part, "fsdp", bit))
+                    for here, part in zip(pieces[x, t ^ (bit // 4)], piece)
+                )
                 del pieces[x, t]
-    corner = after(pieces[1, 1], *first_after)
-    half = corner.shape[0] // 2
-    first = from_y, from_x = over_y(corner[:half]), over_x(corner[half:])
-    to_x = after(pieces[1, 0], *sum_after)
-    to_y = after(pieces[0, 1], *sum_after)
+    one, two = (after(part, *first_after) for part in pieces[1, 1])
+    first = from_y, from_x = over_y(one), over_x(two)
+    half = one.shape[0]
+    to_x = after(pieces[1, 0][0], *sum_after)
+    to_y = after(pieces[0, 1][0], *sum_after)
     to_x = jnp.concatenate([add(to_x[:half], from_y), to_x[half:]])
     to_y = jnp.concatenate([to_y[:half], add(to_y[half:], from_x)])
     sent = (after(to_x, *second_after), after(to_y, *second_after))
     second = over_x(sent[0]), over_y(sent[1])
-    return add(pieces[0, 0], *second), first, second, sent
+    return add(pieces[0, 0][0], *second), first, second, sent
 
 
 def add(*values):
@@ -269,34 +280,41 @@
     )(at, weight, turned, norms, marks)
 
 
-def pack_kernel(at_ref, plain_ref, turned_ref, *outs):
+def pack_kernel(turns, at_ref, *refs):
+    weights, outs = refs[: len(turns)], refs[len(turns) :]
+
     def body(step):
-        units = plain_ref.shape[1]
-        outs[step][:, :units] = plain_ref[...].astype(BF16)
-        outs[step][:, units:] = turned_ref[...].T.astype(BF16)
+        for i, turn in enumerate(turns):
+            value = weights[i][...].T if turn else weights[i][...]
+            outs[4 * i + step][...] = value.astype(BF16)
 
     at_steps(body)
 
 
-def pack(at, plain, turned):
-    rows, cols = plain.shape
-    shape = (rows, cols // 2)
-    return pl.pallas_call(
-        pack_kernel,
+def pack(at, weights, turns):
+    specs, shapes = [], []
+    for weight, turn in zip(weights, turns):
+        rows, cols = weight.shape
+        if turn:
+            specs.append(pl.BlockSpec((rows // 4, cols), lambda i, at: (at[0] ^ i, 0)))
+            shapes.append((cols, rows // 4))
+        else:
+            specs.append(pl.BlockSpec((rows, cols // 4), lambda i, at: (0, at[0] ^ i)))
+            shapes.append((rows, cols // 4))
+    outs = pl.pallas_call(
+        partial(pack_kernel, turns),
         grid_spec=pltpu.PrefetchScalarGridSpec(
             num_scalar_prefetch=1,
             grid=(4,),
-            in_specs=[
-                pl.BlockSpec((rows, cols // 4), lambda i, at: (0, at[0] ^ i)),
-                pl.BlockSpec((cols // 4, rows), lambda i, at: (at[0] ^ i, 0)),
-            ],
-            out_specs=[pl.BlockSpec(shape, lambda i, at: (0, 0))] * 4,
+            in_specs=specs,
+            out_specs=[pl.BlockSpec(shape, lambda i, at: (0, 0)) for shape in shapes for _ in range(4)],
         ),
-        out_shape=[jax.ShapeDtypeStruct(shape, BF16)] * 4,
+        out_shape=[jax.ShapeDtypeStruct(shape, BF16) for shape in shapes for _ in range(4)],
         compiler_params=PARAMS,
         cost_estimate=SMALL,
         name="pack",
-    )(at, plain, turned)
+    )(at, *weights)
+    return [outs[4 * i : 4 * i + 4] for i in range(len(weights))]
 
 
 def flatten(pieces, rows, columns):
@@ -403,7 +421,7 @@
         out[:, x * units : (x + 1) * units] = term.astype(out.dtype)
 
 
-def to_units(value, pieces, shard, columns, kind):
+def to_units(value, pieces, shard, columns, kind, estimate=SMALL):
     arrays, specs, layout = flatten(pieces, shard, columns)
     out = jax.ShapeDtypeStruct((value.shape[0], 2 * columns[0]), kind)
     return pl.pallas_call(
@@ -413,7 +431,7 @@
         out_specs=rows_spec(out),
         out_shape=out,
         compiler_params=PARAMS,
-        cost_estimate=SMALL,
+        cost_estimate=estimate,
         name="to_units",
     )(value, *arrays)
 
@@ -428,7 +446,7 @@
     times_features(value_ref[...], pieces, layout, store)
 
 
-def to_features(value, pieces, shard, columns, width):
+def to_features(value, pieces, shard, columns, width, estimate=SMALL):
     arrays, specs, layout = flatten(pieces, shard, columns)
     out = jax.ShapeDtypeStruct((value.shape[0], width), BF16)
     return pl.pallas_call(
@@ -438,7 +456,7 @@
         out_specs=rows_spec(out),
         out_shape=out,
         compiler_params=PARAMS,
-        cost_estimate=SMALL,
+        cost_estimate=estimate,
         name="to_features",
     )(value, *arrays)
 
@@ -533,26 +551,38 @@
 
     def body(t):
         for x in range(2):
-            out, start = outs[t * 2 + x], 0
+            halves = outs[first_out(x, t) : first_out(x, t) + count_out(x, t)]
+            start = 0
             for left, right in zip(lefts, rights):
                 if len(right.shape) == 3:
                     value = right[x]
                 else:
                     units = right.shape[1] // 2
                     value = right[:, x * units : (x + 1) * units]
-                term = dot(left[...], value, ROWS_BY_ROWS)
+                term = dot(left[...], value, ROWS_BY_ROWS).astype(BF16)
                 shard, units = term.shape[0] // 4, term.shape[1]
-                out[:, :shard, start : start + units] = term.astype(BF16).reshape(4, shard, units)
+                deep = 4 // len(halves)
+                for i, out in enumerate(halves):
+                    rows = term[i * deep * shard : (i + 1) * deep * shard]
+                    out[:, :shard, start : start + units] = rows.reshape(deep, shard, units)
                 start += units
             if extra:
                 for z in range(4):
                     aux[...] = jnp.zeros_like(aux)
                     if x == 0:
                         aux[:4, :shard] = sums[:, z * shard : (z + 1) * shard]
-                    out[z, shard:, :] = aux[...].astype(BF16)
+                    halves[z // deep][z % deep, shard:, :] = aux[...].astype(BF16)
 
     for t in range(groups):
         pl.when(pl.program_id(0) == t)(partial(body, t))
+
+
+def count_out(x, t):
+    return 2 if x and t % 2 else 1
+
+
+def first_out(x, t):
+    return sum(count_out(i % 2, i // 2) for i in range(2 * t + x))
 
 
 def weight_grads(pairs, groups, sums=None):
@@ -560,21 +590,31 @@
     strip = width // groups
     units = sum(right.shape[2] if right.ndim == 3 else right.shape[1] // 2 for _, right in pairs)
     extra = sums is not None
-    shape = (4, strip // 4 + (AUX if extra else 0), units)
+    rows = strip // 4 + (AUX if extra else 0)
+    shapes = [
+        (4 // count_out(x, t), rows, units)
+        for t in range(groups)
+        for x in range(2)
+        for _ in range(count_out(x, t))
+    ]
     outs = pl.pallas_call(
         partial(grads_kernel, groups, len(pairs), extra),
         grid=(groups,),
         in_specs=[pl.BlockSpec((count, strip), lambda t: (0, t))] * len(pairs)
         + [whole(right) for _, right in pairs]
         + ([pl.BlockSpec((4, strip), lambda t: (0, t))] if extra else []),
-        out_specs=[pl.BlockSpec(shape, lambda t: (0, 0, 0))] * (2 * groups),
-        out_shape=[jax.ShapeDtypeStruct(shape, BF16)] * (2 * groups),
+        out_specs=[pl.BlockSpec(shape, lambda t: (0, 0, 0)) for shape in shapes],
+        out_shape=[jax.ShapeDtypeStruct(shape, BF16) for shape in shapes],
         scratch_shapes=[pltpu.VMEM((AUX, units), F32)] if extra else [],
         compiler_params=PARAMS,
-        cost_estimate=SMALL,
+        cost_estimate=cost(6),
         name="weight_grads",
     )(*[left for left, _ in pairs], *[right for _, right in pairs], *([sums] if extra else []))
-    return {(i % 2, i // 2): out for i, out in enumerate(outs)}
+    return {
+        (x, t): tuple(outs[first_out(x, t) : first_out(x, t) + count_out(x, t)])
+        for t in range(groups)
+        for x in range(2)
+    }
 
 
 def visible(query_marks, key_marks):
@@ -611,7 +651,7 @@
 def attend_back_kernel(
     scaling, layout, q_ref, qm_ref, km_ref, out_ref, lse_ref, grad_ref, *refs
 ):
-    outs = len(layout)
+    outs = sum(count_out(*key) for key, _ in layout)
     members, dq_ref = refs[: -outs - 3], refs[-outs - 3]
     dkv_refs, total_ref, kv_ref = refs[-outs - 2 : -2], refs[-2], refs[-1]
     step, last = pl.program_id(1), pl.num_programs(1) - 1
@@ -640,9 +680,19 @@
 
     @pl.when(step == last)
     def _():
-        count = dkv_refs[0].shape[1]
-        for i, ref in enumerate(dkv_refs):
-            ref[0] = total_ref[i * count : (i + 1) * count].astype(BF16)
+        count, at = dkv_refs[0].shape[1], 0
+        for i, (key, _) in enumerate(layout):
+            value = total_ref[i * count : (i + 1) * count].astype(BF16)
+            if count_out(*key) == 1:
+                dkv_refs[at][0] = value
+            else:
+                for half in range(2):
+
+                    @pl.when(pl.program_id(0) == (half ^ key[0]))
+                    def _(half=half):
+                        dkv_refs[at + half][0] = value
+
+            at += count_out(*key)
 
 
 BLOCK = 256
@@ -714,10 +764,17 @@
         out_specs=[rows]
         + [
             pl.BlockSpec((1, count, 2 * head), lambda h, i, x=key[0]: (h ^ x, 0, 0))
+            if count_out(*key) == 1
+            else pl.BlockSpec((1, count, 2 * head), lambda h, i: (0, 0, 0))
             for key, _ in layout
+            for _ in range(count_out(*key))
         ],
         out_shape=[jax.ShapeDtypeStruct((count, 2 * head), BF16)]
-        + [jax.ShapeDtypeStruct((2, count, 2 * head), BF16)] * len(layout),
+        + [
+            jax.ShapeDtypeStruct((2 // count_out(*key), count, 2 * head), BF16)
+            for key, _ in layout
+            for _ in range(count_out(*key))
+        ],
         scratch_shapes=[
             pltpu.VMEM((length, 2 * head), F32),
             pltpu.VMEM((length, 2 * head), BF16),
@@ -726,7 +783,11 @@
         cost_estimate=SMALL,
         name="attend_back",
     )(queries, query_marks, key_marks, attended, logsum, grad, *arrays)
-    return outs[0], {key: out for (key, _), out in zip(layout, outs[1:])}
+    pieces, at = {}, 1
+    for key, _ in layout:
+        pieces[key] = tuple(outs[at : at + count_out(*key)])
+        at += count_out(*key)
+    return outs[0], pieces
 
 
 def adam_kernel(rate, shape, sources, at_ref, *refs):
@@ -790,7 +851,7 @@
         ),
         out_shape=[jax.ShapeDtypeStruct(master.shape, kind) for kind in (F32, F32, F32, BF16)],
         compiler_params=PARAMS,
-        cost_estimate=SMALL,
+        cost_estimate=cost(7),
         name="adam",
     )(at, *[part for parts, _, _ in sources for part in parts], *matrix)
 
@@ -869,11 +930,11 @@
     def exchange(parts, ready=None):
         return [parts[0]] + along_z(parts[1:], ready)
 
+    def blocks_of(total):
+        return [lax.dynamic_index_in_dim(total, at ^ step, 0, keepdims=False) for step in range(4)]
+
     def shares(total, ready=None):
-        return exchange(
-            [lax.dynamic_index_in_dim(total, at ^ step, 0, keepdims=False) for step in range(4)],
-            ready,
-        )
+        return exchange(blocks_of(total), ready)
 
     span_places = jnp.repeat(span_map % (ROW_LEN // SPAN), SPAN)
     input_cube = attention_input.transpose(1, 0, 2)
@@ -886,10 +947,13 @@
     )
     first_parts = exchange(first_packed)
     own_tokens = to_relative(after(own_rows(tokens), first_packed[0]))
-    second_packed = pack(after(at_word, own_tokens), expand_weight, reduce_weight)
-    group_tokens = gather_tokens(after(own_tokens, second_packed[0], *first_parts[1:]))
-    second_parts = exchange(second_packed, first_parts[1:])
-    own_cotangent = to_relative(after(own_rows(cotangent), second_packed[0]))
+    expand_packed, reduce_packed = pack(
+        after(at_word, own_tokens), [expand_weight, reduce_weight], (False, True)
+    )
+    own_cotangent = to_relative(after(own_rows(cotangent), expand_packed[0]))
+    group_tokens = gather_tokens(after(own_tokens, own_cotangent, *first_parts[1:]))
+    expand_parts = exchange(expand_packed, first_parts[1:])
+    reduce_parts = exchange(reduce_packed, expand_parts[1:])
     (first_own,) = assemble(at_word, [after(first_parts[0], own_cotangent)] + first_parts[1:])
     low = gather_groups(first_own)
     group_cotangent = gather_tokens(after(own_cotangent, first_own))
@@ -907,61 +971,69 @@
     key_marks = marks.reshape(2, -1)
 
     normed_one, queries, own_kv = project(
-        after(group_tokens, key_marks, *second_parts[1:]), norm_values, low, shard, head
+        after(group_tokens, key_marks, *expand_parts[1:]), norm_values, low, shard, head
     )
     kv_low = gather_groups(own_kv)
-    expand_own, reduce_own = assemble(
-        at_word, [after(second_parts[0], own_kv)] + second_parts[1:], 2
-    )
+    (expand_own,) = assemble(at_word, expand_parts)
     expand_low = gather_groups(expand_own, kv_low[1, 1])
+    attended, mixed, logsum = attend(
+        after(queries, expand_own, reduce_parts[1]),
+        kv_low,
+        query_marks,
+        key_marks,
+        scaling,
+    )
+    (reduce_own,) = assemble(at_word, [after(reduce_parts[0], mixed)] + reduce_parts[1:])
     reduce_low = gather_groups(reduce_own, expand_low[1, 1])
-    attended, mixed, logsum = attend(
-        after(queries, expand_own, group_cotangent), kv_low, query_marks, key_marks, scaling
-    )
-    branch = scatter_tokens(to_features(mixed, low, shard, (head, 3), width))
+    branch = scatter_tokens(to_features(after(mixed, group_cotangent, *reduce_parts[2:]), low, shard, (head, 3), width))
     middle = own_tokens.astype(F32) + branch.astype(F32)
 
-    shape_two, scale_two = normalize(after(middle, *first_level(reduce_low)))
+    shape_two, scale_two = normalize(after(middle, *expand_low[1, 1]))
     normed_two = gather_tokens((shape_two * norm_values[2] + norm_values[3]).astype(BF16))
-    active_grad = to_units(group_cotangent, reduce_low, shard, (units, 0), F32)
+    active_grad = to_units(group_cotangent, reduce_low, shard, (units, 0), F32, cost(25))
     active, hidden_grad, second_terms = feed_forward(
         normed_two, active_grad, expand_low, shard, units
     )
     second_grad = scatter_tokens(second_terms)
     reduce_pieces = weight_grads([(group_cotangent, active)], groups)
     reduce_sum, reduce_first, reduce_came, reduce_sent = reduce_groups(reduce_pieces)
-    expand_pieces = weight_grads([(normed_two, after(hidden_grad, reduce_pieces[0, 0]))], groups)
+    expand_pieces = weight_grads([(normed_two, after(hidden_grad, reduce_pieces[0, 0][0]))], groups)
     feed_terms = to_features(
-        after(active, expand_pieces[0, 0]), reduce_low, shard, (units, 0), width
+        after(active, expand_pieces[0, 0][0]), reduce_low, shard, (units, 0), width, cost(6)
     )
     middle_part, gain_two, bias_two = norm_back(
         shape_two, scale_two, norm_values[2], after(second_grad, feed_terms, *reduce_sent).astype(F32)
     )
     middle_grad = own_cotangent.astype(F32) + middle_part
-    branch_grad = gather_tokens(middle_grad.astype(BF16))
-    expand_sum, _, expand_came, expand_sent = reduce_groups(expand_pieces, reduce_came)
-    feed = scatter_tokens(after(feed_terms, branch_grad))
+    middle_low = middle_grad.astype(BF16)
+    branch_grad = gather_tokens(middle_low)
+    feed = scatter_tokens(after(feed_terms, middle_low))
 
     mixed_grad = to_units(
-        after(branch_grad, reduce_sum, *expand_sent), low, shard, (head, 3), BF16
-    )
-    reduce_shares = shares(reduce_sum)
+        branch_grad, low, shard, (head, 3), BF16
+    )
+    expand_sum, _, expand_came, _ = reduce_groups(expand_pieces, reduce_came, (mixed_grad,))
     query_grad, kv_pieces = attend_back(
         queries, kv_low, query_marks, key_marks, attended, logsum, mixed_grad, scaling
     )
-    expand_shares = shares(expand_sum, reduce_shares[1:])
-    own_kv_grad, _, kv_came, _ = reduce_groups(
-        kv_pieces, expand_came + tuple(reduce_shares[1:]), (), expand_shares[1:]
-    )
+    own_kv_grad, kv_first, kv_came, _ = reduce_groups(kv_pieces, expand_came)
+    reduce_shares = shares(after(reduce_sum, query_grad))
+    expand_shares = shares(after(expand_sum, query_grad))
     query_pieces = weight_grads(
-        [(branch_grad, after(mixed, kv_pieces[1, 1])), (normed_one, query_grad)], groups
+        [(branch_grad, after(mixed, kv_pieces[1, 1][0])), (normed_one, query_grad)], groups
     )
     query_sum, _, query_came, _ = reduce_groups(query_pieces, kv_came)
-    output = lax.all_gather(
-        to_natural((middle + feed.astype(F32)).astype(BF16)), "mp", axis=0, tiled=True
-    )
+    natural_output = to_natural(
+        (middle + after(feed, *kv_first).astype(F32)).astype(BF16)
+    )
+    output = lax.all_gather(natural_output, "mp", axis=0, tiled=True)
     first_terms, norm_sums = project_back(
-        after(query_grad, output, query_pieces[0, 0]), own_kv_grad, group_tokens, low, shard, head
+        after(query_grad, natural_output, query_pieces[0, 0][0], *reduce_shares[1:]),
+        own_kv_grad,
+        group_tokens,
+        low,
+        shard,
+        head,
     )
     first_grad = scatter_tokens(first_terms)
     all_sums = jnp.concatenate([norm_sums, gain_two[None], bias_two[None]])
@@ -969,20 +1041,27 @@
     pair_pieces = weight_grads(
         [(normed_one, own_kv_grad)], groups, all_sums
     )
-    pair_sum, _, _, pair_sent = reduce_groups(pair_pieces, query_came)
-    query_shares = shares(after(query_sum, *pair_sent))
-    pair_shares = shares(pair_sum)
-    share_norm = sum(part[shard : shard + 4, :shard].astype(F32) for part in pair_shares)
-    share_norm = share_norm + over_c(share_norm)
-    share_norm = share_norm + over_x(share_norm)
-
     reduce_new = adam(
         at_word,
         (reduce_weight, reduce_first_moment, reduce_second),
         reduce_rate,
         "turned",
-        [(reduce_shares, 0, units)],
-    )
+        [([after(reduce_shares[0], pair_pieces[0, 0][0])] + reduce_shares[1:], 0, units)],
+    )
+    pair_sum, _, pair_came, pair_sent = reduce_groups(pair_pieces, (), (reduce_new[0],))
+    expand_new = adam(
+        at_word,
+        (expand_weight, expand_first_moment, expand_second),
+        expand_rate,
+        "plain",
+        [([after(expand_shares[0], *pair_sent)] + expand_shares[1:], 0, units)],
+    )
+    query_shares = shares(query_sum)
+    pair_shares = shares(after(pair_sum, expand_new[0]))
+    share_norm = sum(part[shard : shard + 4, :shard].astype(F32) for part in pair_shares)
+    share_norm = share_norm + over_c(share_norm)
+    share_norm = share_norm + over_x(share_norm)
+
     output_new = adam(
         at_word,
         (attention_output, attention_output_first, attention_output_second),
@@ -990,15 +1069,8 @@
         "turned",
         [(query_shares, 0, head)],
     )
-    expand_new = adam(
-        at_word,
-        (expand_weight, expand_first_moment, expand_second),
-        expand_rate,
-        "plain",
-        [(expand_shares, 0, units)],
-    )
     input_part, _, _ = norm_back(
-        shape_one, scale_one, norm_values[0], after(first_grad, reduce_new[0], expand_new[0]).astype(F32)
+        shape_one, scale_one, norm_values[0], first_grad.astype(F32)
     )
     input_grad = all_lanes(to_natural((middle_grad + input_part).astype(BF16))).astype(F32)
     input_new = adam(
@@ -1010,7 +1082,10 @@
         ),
         input_rate,
         "cube",
-        [(query_shares, head, 2 * head), (pair_shares, 0, 2 * head)],
+        [
+            ([after(query_shares[0], output_new[0])] + query_shares[1:], head, 2 * head),
+            (pair_shares, 0, 2 * head),
+        ],
     )
     norm_new = adamw_update(norm_params, norm_first, norm_second, share_norm, gain_rate, 0.0)
     return (

time: 547 us -> 496 us (0.907)
  waiting for transfers between devices: 252 us -> 187 us
  starting transfers between devices: 74.6 us -> 82.8 us
    all_gather x4, waiting for transfers between devices: 47.5 us -> 8.63 us  [gather_tokens(): lax.all_gather(own, ('fsdp', 'mp'), axis_index_groups=token_groups(), axi...]
    ppermute x58 -> x61, waiting for transfers between devices: 202 us -> 171 us  [swap(): return lax.ppermute(value, axis, [(i, i ^ mask) for i in range(size)])]
    ppermute x58 -> x61, starting transfers between devices: 73.5 us -> 82 us  [swap(): return lax.ppermute(value, axis, [(i, i ^ mask) for i in range(size)])]
    slice x5 -> x0, local copies, waits for them, and re-layouts: 6.48 us -> none  [reduce_groups(): first = from_y, from_x = (over_y(corner[:half]), over_x(corner[half:]))]
    convert_element_type x15, other arithmetic: 9.48 us -> 15.7 us  [add(): return total.astype(BF16)]
    unnamed x121 -> x133, local copies, waits for them, and re-layouts: 10.3 us -> 14.9 us
  transfers between devices with their start and end apart: 67 -> 70, of which waited for: 33 -> 26; matrix products, arithmetic and copies ran while one was open for 9% -> 10% of each run, Pallas kernels for 17% -> 21%
where the time goes in v3:
time: 496 us; the launch traced here: 487 us
  waiting for transfers between devices  187 us (38%)
  Pallas kernels  127 us (26%)
  starting transfers between devices  82.8 us (17%)
  other arithmetic  42.5 us (9%)
  local copies, waits for them, and re-layouts  32.1 us (6%)
  between operations  15.4 us (3%)
    ppermute x61, waiting for transfers between devices, swap(): return lax.ppermute(value, axis, [(i, i ^ mask) for i in range(size)])  171 us
    ppermute x61, starting transfers between devices, swap(): return lax.ppermute(value, axis, [(i, i ^ mask) for i in range(size)])  82 us
    pallas_call x4, Pallas kernels, adam(): pl.pallas_call(partial(adam_kernel, rate, shape, columns), grid_spec=pltp...  25.1 us
    pallas_call x4, Pallas kernels, weight_grads(): pl.pallas_call(partial(grads_kernel, groups, len(pairs), extra), grid=(gr...  22.7 us
    convert_element_type x15, other arithmetic, add(): return total.astype(BF16)  15.7 us
    unnamed x133, local copies, waits for them, and re-layouts  14.9 us
    pallas_call x1, Pallas kernels, attend_back(): pl.pallas_call(partial(attend_back_kernel, scaling, layout), grid=(2, cou...  12.5 us
  transfers between devices with their start and end apart: 70, of which 26 were waited for; matrix products, arithmetic and copies ran while one was open for 10% of the time, Pallas kernels for 21%

profile of v3, /device:TPU:9, one launch (start us, length us, event | category | flops | bytes accessed | tf_op | source)
XLA Modules:
  0.0 486.7 jit_solution(4155375073541631646)
XLA Ops:
  27.6 11.8 %collective-permute-done.2.refs_3_ = bf16[272,512]{1,0:T(8,128)(2,1)S(1)} collective-permute-done((bf16[272,512]{1,0:T(8,128)(2,1)}, bf16[272,512]{1,0:T(8,128)(2,1)S(1)}, u32[]{:S(2)}, u32[]{:S(2)}) %collective-permute-start.2) | collective-permute-done | bytes 278560 | tf_op jit(solution)/shard_map/ppermute | solution.py:42
  49.1 18.0 %collective-permute-done.3.refs_1_ = bf16[4,272,512]{2,1,0:T(8,128)(2,1)S(1)} collective-permute-done((bf16[4,272,512]{2,1,0:T(8,128)(2,1)}, bf16[4,272,512]{2,1,0:T(8,128)(2,1)S(1)}, u32[]{:S(2)}, u32[]{:S(2)}) %collective-permute-start.3) | collective-permute-done | bytes 1114144 | tf_op jit(solution)/shard_map/ppermute | solution.py:42
  78.3 8.6 %collective-permute-done.6.refs_3_ = bf16[256,512]{1,0:T(8,128)(2,1)} collective-permute-done((bf16[256,512]{1,0:T(8,128)(2,1)}, bf16[256,512]{1,0:T(8,128)(2,1)}, u32[]{:S(2)}, u32[]{:S(2)}) %collective-permute-start.6) | collective-permute-done | bytes 262176 | tf_op jit(solution)/shard_map/ppermute | solution.py:42
  87.9 6.7 %project.1 = (bf16[512,2048]{1,0:T(8,128)(2,1)}, bf16[512,256]{1,0:T(8,128)(2,1)}, bf16[2,512,256]{2,1,0:T(8,128)(2,1)}) custom-call(bf16[512,2048]{1,0:T(8,128)(2,1)} %all-gather.6.cloned.1.call-done.tokens_ref, f32[4,2048]{1,0:T(4,128)} %bitcast.111, bf16[4,272,512]{2,1,0:T(8,128)(2,1)} %assemble.3.refs_0_, bf16[4,272,512]{2,1,0:T(8,128)(2,1)} %copy-done, ...), custom_call_target="tpu_custom_call" | custom-call | flops 1 | bytes 1 | tf_op jit(solution)/shard_map/project/pallas_call | solution.py:396
  99.6 6.3 %collective-permute-done.12.refs_2_ = bf16[2,512,256]{2,1,0:T(8,128)(2,1)S(1)} collective-permute-done((bf16[2,512,256]{2,1,0:T(8,128)(2,1)}, bf16[2,512,256]{2,1,0:T(8,128)(2,1)S(1)}, u32[]{:S(2)}, u32[]{:S(2)}) %collective-permute-start.12) | collective-permute-done | bytes 524320 | tf_op jit(solution)/shard_map/ppermute | solution.py:42
  113.8 6.6 %collective-permute-done.10.refs_1_ = bf16[256,512]{1,0:T(8,128)(2,1)S(1)} collective-permute-done((bf16[256,512]{1,0:T(8,128)(2,1)}, bf16[256,512]{1,0:T(8,128)(2,1)S(1)}, u32[]{:S(2)}, u32[]{:S(2)}) %collective-permute-start.10) | collective-permute-done | bytes 262176 | tf_op jit(solution)/shard_map/ppermute | solution.py:42
  121.3 8.3 %attend.1 = (f32[512,256]{1,0:T(8,128)}, bf16[512,256]{1,0:T(8,128)(2,1)}, f32[2,512,1]{2,1,0:T(8,128)}) custom-call(bf16[512,256]{1,0:T(8,128)(2,1)} %get-tuple-element.148.q_ref, s32[512,2]{1,0:T(8,128)} %bitcast.98, s32[2,2048]{1,0:T(2,128)} %reshape.168.km_ref, bf16[2,512,256]{2,1,0:T(8,128)(2,1)} %get-tuple-element.149.refs_0_, ...), custom_call_target="tpu_custom_call" | custom-call | flops 1 | bytes 1 | tf_op jit(solution)/shard_map/attend/pallas_call | solution.py:720
  129.5 10.2 %collective-permute-done.16.refs_3_ = bf16[256,512]{1,0:T(8,128)(2,1)S(1)} collective-permute-done((bf16[256,512]{1,0:T(8,128)(2,1)}, bf16[256,512]{1,0:T(8,128)(2,1)S(1)}, u32[]{:S(2)}, u32[]{:S(2)}) %collective-permute-start.16) | collective-permute-done | bytes 262176 | tf_op jit(solution)/shard_map/ppermute | solution.py:42
  147.9 21.5 %collective-permute-done.17.refs_2_ = bf16[4,256,512]{2,1,0:T(8,128)(2,1)S(1)} collective-permute-done((bf16[4,256,512]{2,1,0:T(8,128)(2,1)S(1)}, bf16[4,256,512]{2,1,0:T(8,128)(2,1)S(1)}, u32[]{:S(2)}, u32[]{:S(2)}) %collective-permute-start.17) | collective-permute-done | bytes 1048608 | tf_op jit(solution)/shard_map/ppermute | solution.py:42
  175.1 6.2 %collective-permute-done.18.refs_3_ = bf16[2,256,512]{2,1,0:T(8,128)(2,1)S(1)} collective-permute-done((bf16[2,256,512]{2,1,0:T(8,128)(2,1)S(1)}, bf16[2,256,512]{2,1,0:T(8,128)(2,1)S(1)}, u32[]{:S(2)}, u32[]{:S(2)}) %collective-permute-start.18) | collective-permute-done | bytes 524320 | tf_op jit(solution)/shard_map/ppermute | solution.py:42
  187.4 17.9 %collective-permute-done.22.refs_2_ = bf16[4,256,512]{2,1,0:T(8,128)(2,1)S(1)} collective-permute-done((bf16[4,256,512]{2,1,0:T(8,128)(2,1)}, bf16[4,256,512]{2,1,0:T(8,128)(2,1)S(1)}, u32[]{:S(2)}, u32[]{:S(2)}) %collective-permute-start.22) | collective-permute-done | bytes 1048608 | tf_op jit(solution)/shard_map/ppermute | solution.py:42
  208.1 10.2 %collective-permute-done.23.refs_3_ = bf16[2,256,512]{2,1,0:T(8,128)(2,1)S(1)} collective-permute-done((bf16[2,256,512]{2,1,0:T(8,128)(2,1)S(1)}, bf16[2,256,512]{2,1,0:T(8,128)(2,1)S(1)}, u32[]{:S(2)}, u32[]{:S(2)}) %collective-permute-start.23) | collective-permute-done | bytes 524320 | tf_op jit(solution)/shard_map/ppermute | solution.py:42
  219.9 5.9 %to_units.2.pull_ref = f32[512,1024]{1,0:T(8,128)} custom-call(bf16[512,2048]{1,0:T(8,128)(2,1)} %all-gather.8.cloned.1.call-done.value_ref.refs_0_, bf16[4,256,512]{2,1,0:T(8,128)(2,1)} %assemble.5.refs_0_, bf16[4,256,512]{2,1,0:T(8,128)(2,1)} %collective-permute-done.21.refs_1_, bf16[4,256,512]{2,1,0:T(8,128)(2,1)} %copy-done.50, ...), custom_call_target="tpu_custom_call" | custom-call | flops 28750000128 | bytes 1 | tf_op jit(solution)/shard_map/to_units/pallas_call | solution.py:427
  225.9 9.8 %feed_forward.1 = (bf16[512,1024]{1,0:T(8,128)(2,1)}, bf16[512,1024]{1,0:T(8,128)(2,1)}, bf16[512,2048]{1,0:T(8,128)(2,1)}) custom-call(bf16[512,2048]{1,0:T(8,128)(2,1)} %all-gather.10.cloned.1.call-done.value_ref.refs_0_, f32[512,1024]{1,0:T(8,128)} %to_units.2.pull_ref, bf16[4,256,512]{2,1,0:T(8,128)(2,1)} %assemble.4.refs_0_, ...), custom_call_target="tpu_custom_call" | custom-call | flops 1 | bytes 1 | tf_op jit(solution)/shard_map/feed_forward/pallas_call | solution.py:490
  235.7 6.2 %weight_grads.4 = (bf16[4,256,512]{2,1,0:T(8,128)(2,1)}, bf16[4,256,512]{2,1,0:T(8,128)(2,1)}, bf16[4,256,512]{2,1,0:T(8,128)(2,1)}, bf16[2,256,512]{2,1,0:T(8,128)(2,1)}, bf16[2,256,512]{2,1,0:T(8,128)(2,1)}) custom-call(bf16[512,2048]{1,0:T(8,128)(2,1)} %all-gather.8.cloned.1.call-done.value_ref.refs_0_, bf16[512,1024]{1,0:T(8,128)(2,1)} %get-tuple-element.167.refs_1_.value_ref), custom_call_target="tpu_custom_call" | custom-call | flops 6899999744 | bytes 1 | tf_op jit(solution)/shard_map/weight_grads/pallas_call | solution.py:600
  242.4 6.3 %weight_grads.5 = (bf16[4,256,512]{2,1,0:T(8,128)(2,1)}, bf16[4,256,512]{2,1,0:T(8,128)(2,1)}, bf16[4,256,512]{2,1,0:T(8,128)(2,1)}, bf16[2,256,512]{2,1,0:T(8,128)(2,1)}, bf16[2,256,512]{2,1,0:T(8,128)(2,1)}) custom-call(bf16[512,2048]{1,0:T(8,128)(2,1)} %all-gather.10.cloned.1.call-done.value_ref.refs_0_, bf16[512,1024]{1,0:T(8,128)(2,1)} %get-tuple-element.165.refs_1_), custom_call_target="tpu_custom_call" | custom-call | flops 6899999744 | bytes 1 | tf_op jit(solution)/shard_map/weight_grads/pallas_call | solution.py:600
  248.7 6.1 %to_features.3 = bf16[512,2048]{1,0:T(8,128)(2,1)} custom-call(bf16[512,1024]{1,0:T(8,128)(2,1)} %get-tuple-element.167.refs_1_.value_ref, bf16[4,256,512]{2,1,0:T(8,128)(2,1)} %assemble.5.refs_0_, bf16[4,256,512]{2,1,0:T(8,128)(2,1)} %collective-permute-done.21.refs_1_, bf16[4,256,512]{2,1,0:T(8,128)(2,1)} %copy-done.50, bf16[2,256,512]{2,1,0:T(8,128)(2,1)} %copy-done.60, ...), custom_call_target="tpu_custom_call" | custom-call | flops 6899999744 | bytes 1 | tf_op jit(solution)/shard_map/to_features/pallas_call | solution.py:452
  260.5 7.3 %reduce-scatter.7.cloned.1.call-done = bf16[64,2048]{1,0:T(8,128)(2,1)} async-done(((bf16[512,2048]{1,0:T(8,128)(2,1)}), bf16[64,2048]{1,0:T(8,128)(2,1)}) %reduce-scatter.7.cloned.1.call-update) | async-done | bytes 262160 | tf_op jit(solution)/shard_map/reduce_scatter | solution.py:191
  273.4 20.9 %collective-permute-done.28 = bf16[4,256,512]{2,1,0:T(8,128)(2,1)S(1)} collective-permute-done((bf16[4,256,512]{2,1,0:T(8,128)(2,1)S(1)}, bf16[4,256,512]{2,1,0:T(8,128)(2,1)S(1)}, u32[]{:S(2)}, u32[]{:S(2)}) %collective-permute-start.28) | collective-permute-done | bytes 1048608 | tf_op jit(solution)/shard_map/ppermute | solution.py:42
  295.9 8.6 %all-gather.12.cloned.1.call-done.value_ref.refs_0_ = bf16[512,2048]{1,0:T(8,128)(2,1)} async-done(((bf16[64,2048]{1,0:T(8,128)(2,1)}), bf16[512,2048]{1,0:T(8,128)(2,1)}) %all-gather.12.cloned.1.call-update) | async-done | bytes 2097168 | tf_op jit(solution)/shard_map/all_gather | solution.py:185
  316.0 12.5 %attend_back.1 = (bf16[512,256]{1,0:T(8,128)(2,1)}, bf16[2,512,256]{2,1,0:T(8,128)(2,1)}, bf16[2,512,256]{2,1,0:T(8,128)(2,1)}, bf16[2,512,256]{2,1,0:T(8,128)(2...) custom-call(bf16[512,256]{1,0:T(8,128)(2,1)} %get-tuple-element.148.q_ref, s32[512,2]{1,0:T(8,128)} %bitcast.99, ...), custom_call_target="tpu_custom_call" | custom-call | flops 1 | bytes 1 | tf_op jit(solution)/shard_map/attend_back/pallas_call | solution.py:752
  329.8 7.1 %collective-permute-start.36 = (bf16[256,512]{1,0:T(8,128)(2,1)}, bf16[256,512]{1,0:T(8,128)(2,1)}, u32[]{:S(2)}, u32[]{:S(2)}) collective-permute-start(bf16[256,512]{1,0:T(8,128)(2,1)} %get-tuple-element.253), channel_id=1, source_target_pairs={{0,16},{4,20},{8,24},{12,28},{16,0},{20,4},{24,8},{28,12},{1,17},{... | collective-permute-start | bytes 786440 | tf_op jit(solution)/shard_map/ppermute | solution.py:42
  338.5 5.8 %weight_grads.6 = (bf16[4,256,256]{2,1,0:T(8,128)(2,1)}, bf16[4,256,256]{2,1,0:T(8,128)(2,1)}, bf16[4,256,256]{2,1,0:T(8,128)(2,1)}, bf16[2,256,256]{2,1,0:T(8,128)(2,1)}, bf16[2,256,256]{2,1,0:T(8,128)(2,1)}) custom-call(bf16[512,2048]{1,0:T(8,128)(2,1)} %all-gather.12.cloned.1.call-done.value_ref.refs_0_, ...), custom_call_target="tpu_custom_call" | custom-call | flops 6899999744 | bytes 1 | tf_op jit(solution)/shard_map/weight_grads/pallas_call | solution.py:600
  346.1 4.6 collective-permute-done.34
  355.1 6.3 %collective-permute-done.37.refs_3_ = bf16[256,512]{1,0:T(8,128)(2,1)} collective-permute-done((bf16[256,512]{1,0:T(8,128)(2,1)}, bf16[256,512]{1,0:T(8,128)(2,1)}, u32[]{:S(2)}, u32[]{:S(2)}) %collective-permute-start.37) | collective-permute-done | bytes 262176 | tf_op jit(solution)/shard_map/ppermute | solution.py:42
  364.1 7.3 %project_back.1 = (bf16[512,2048]{1,0:T(8,128)(2,1)}, f32[2,2048]{1,0:T(2,128)}) custom-call(bf16[512,256]{1,0:T(8,128)(2,1)} %get-tuple-element.195.refs_3_.query_ref, bf16[2,512,256]{2,1,0:T(8,128)(2,1)} %add_convert_fusion.4.pair_ref.refs_1_, bf16[512,2048]{1,0:T(8,128)(2,1)} %all-gather.6.cloned.1.call-done.tokens_ref, ...), custom_call_target="tpu_custom_call" | custom-call | flops 1 | bytes 1 | tf_op jit(solution)/shard_map/project_back/pallas_call | solution.py:527
  377.1 5.9 %collective-permute-start.54 = (bf16[256,512]{1,0:T(8,128)(2,1)}, bf16[256,512]{1,0:T(8,128)(2,1)}, u32[]{:S(2)}, u32[]{:S(2)}) collective-permute-start(bf16[256,512]{1,0:T(8,128)(2,1)} %get-tuple-element.248), channel_id=1, source_target_pairs={{0,16},{4,20},{8,24},{12,28},{16,0},{20,4},{24,8},{28,12},{1,17},{... | collective-permute-start | bytes 786440 | tf_op jit(solution)/shard_map/ppermute | solution.py:42
  389.6 7.3 %adam.5 = (f32[2048,256]{1,0:T(8,128)}, f32[2048,256]{1,0:T(8,128)}, f32[2048,256]{1,0:T(8,128)}, bf16[2048,256]{1,0:T(8,128)(2,1)}) custom-call(s32[1]{0:T(128)} %bitcast.at_ref, bf16[256,512]{1,0:T(8,128)(2,1)} %get-tuple-element.211.refs_0_, bf16[256,512]{1,0:T(8,128)(2,1)} %collective-permute-done.35.refs_1_, ...), custom_call_target="tpu_custom_call" | custom-call | flops 8049999872 | bytes 1 | tf_op jit(solution)/shard_map/adam/pallas_call | solution.py:838
  408.9 7.5 %collective-permute-done.55.refs_3_ = bf16[256,512]{1,0:T(8,128)(2,1)} collective-permute-done((bf16[256,512]{1,0:T(8,128)(2,1)}, bf16[256,512]{1,0:T(8,128)(2,1)}, u32[]{:S(2)}, u32[]{:S(2)}) %collective-permute-start.55) | collective-permute-done | bytes 262176 | tf_op jit(solution)/shard_map/ppermute | solution.py:42
  416.4 7.4 %adam.6 = (f32[256,2048]{1,0:T(8,128)}, f32[256,2048]{1,0:T(8,128)}, f32[256,2048]{1,0:T(8,128)}, bf16[256,2048]{1,0:T(8,128)(2,1)}) custom-call(s32[1]{0:T(128)} %bitcast.at_ref, bf16[256,512]{1,0:T(8,128)(2,1)} %get-tuple-element.219.refs_0_, bf16[256,512]{1,0:T(8,128)(2,1)} %collective-permute-done.53.refs_1_, ...), custom_call_target="tpu_custom_call" | custom-call | flops 8049999872 | bytes 1 | tf_op jit(solution)/shard_map/adam/pallas_call | solution.py:838
  441.6 14.8 %collective-permute-start.59 = (f32[4,256]{1,0:T(4,128)S(1)}, f32[4,256]{1,0:T(4,128)S(1)}, u32[]{:S(2)}, u32[]{:S(2)}) collective-permute-start(f32[4,256]{1,0:T(4,128)S(1)} %fusion.24), channel_id=1, source_target_pairs={{0,1},{1,0},{2,3},{3,2},{4,5},{5,4},{6,7},{7,6},{8,9},{9,8},{10,11... | collective-permute-start | bytes 12296 | tf_op jit(solution)/shard_map/ppermute | solution.py:42
  469.8 6.1 %adam.7 = (f32[3,256,512]{2,1,0:T(8,128)}, f32[3,256,512]{2,1,0:T(8,128)}, f32[3,256,512]{2,1,0:T(8,128)}, bf16[3,256,512]{2,1,0:T(8,128)(2,1)}) custom-call(s32[1]{0:T(128)} %bitcast.at_ref, bf16[256,256]{1,0:T(8,128)(2,1)} %get-tuple-element.207.refs_0_, bf16[256,256]{1,0:T(8,128)(2,1)} %copy-done.63, bf16[256,256]{1,0:T(8,128)(2,1)} %copy-done.64, ...), custom_call_target="tpu_custom_call" | custom-call | flops 8049999872 | bytes 1 | tf_op jit(solution)/shard_map/adam/pallas_call | solution.py:838
  (388 shorter events, 175.4 us)
Async XLA Ops:
  7.2 79.7 %all-gather.6.cloned.1.call-start = ((), (), s32[]{:S(2)}) async-start(), calls=%async_computation.4 | async-start | bytes 2359296 | tf_op jit(solution)/shard_map/all_gather | solution.py:185
  15.3 24.1 %collective-permute-start.2 = (bf16[272,512]{1,0:T(8,128)(2,1)}, bf16[272,512]{1,0:T(8,128)(2,1)S(1)}, u32[]{:S(2)}, u32[]{:S(2)}) collective-permute-start(bf16[272,512]{1,0:T(8,128)(2,1)} %get-tuple-element.135), channel_id=1, source_target_pairs={{0,24},{4,28},{8,16},{12,20},{16,8},{20,12},{24,0},{28,4},{1,25},{... | collective-permute-start | bytes 835592 | tf_op jit(solution)/shard_map/ppermute | solution.py:42
  39.4 100.3 %all-gather.8.cloned.1.call-start = ((), (), s32[]{:S(2)}) async-start(), calls=%async_computation.5 | async-start | bytes 2359296 | tf_op jit(solution)/shard_map/all_gather | solution.py:185
  42.4 142.3 %reduce-scatter.5.cloned.1.call-start = ((), (), s32[]{:S(2)}) async-start(), calls=%async_computation.6 | async-start | bytes 2359296 | tf_op jit(solution)/shard_map/reduce_scatter | solution.py:191
  42.4 24.6 %collective-permute-start.3 = (bf16[4,272,512]{2,1,0:T(8,128)(2,1)}, bf16[4,272,512]{2,1,0:T(8,128)(2,1)S(1)}, u32[]{:S(2)}, u32[]{:S(2)}) collective-permute-start(bf16[4,272,512]{2,1,0:T(8,128)(2,1)} %assemble.3.refs_0_), channel_id=1, source_target_pairs={{0,4},{4,0},{8,12},{12,8},{16,20},{20,16},{24,28},{28,24},{1,5},{5... | collective-permute-start | bytes 3342344 | tf_op jit(solution)/shard_map/ppermute | solution.py:42
  43.7 24.3 %collective-permute-start.7 = (bf16[4,272,512]{2,1,0:T(8,128)(2,1)}, bf16[4,272,512]{2,1,0:T(8,128)(2,1)S(1)}, u32[]{:S(2)}, u32[]{:S(2)}) collective-permute-start(bf16[4,272,512]{2,1,0:T(8,128)(2,1)} %assemble.3.refs_0_), channel_id=1, source_target_pairs={{0,2},{1,3},{2,0},{3,1},{4,6},{5,7},{6,4},{7,5},{8,10},{9,11},{10,... | collective-permute-start | bytes 3342344 | tf_op jit(solution)/shard_map/ppermute | solution.py:42
  45.5 32.8 %collective-permute-start.4 = (bf16[256,512]{1,0:T(8,128)(2,1)}, bf16[256,512]{1,0:T(8,128)(2,1)}, u32[]{:S(2)}, u32[]{:S(2)}) collective-permute-start(bf16[256,512]{1,0:T(8,128)(2,1)} %get-tuple-element.139), channel_id=1, source_target_pairs={{0,8},{4,12},{8,0},{12,4},{16,24},{20,28},{24,16},{28,20},{1,9},{5... | collective-permute-start | bytes 786440 | tf_op jit(solution)/shard_map/ppermute | solution.py:42
  45.5 32.8 %collective-permute-start.5 = (bf16[256,512]{1,0:T(8,128)(2,1)}, bf16[256,512]{1,0:T(8,128)(2,1)}, u32[]{:S(2)}, u32[]{:S(2)}) collective-permute-start(bf16[256,512]{1,0:T(8,128)(2,1)} %get-tuple-element.141), channel_id=1, source_target_pairs={{0,16},{4,20},{8,24},{12,28},{16,0},{20,4},{24,8},{28,12},{1,17},{... | collective-permute-start | bytes 786440 | tf_op jit(solution)/shard_map/ppermute | solution.py:42
  48.0 38.9 %collective-permute-start.6 = (bf16[256,512]{1,0:T(8,128)(2,1)}, bf16[256,512]{1,0:T(8,128)(2,1)}, u32[]{:S(2)}, u32[]{:S(2)}) collective-permute-start(bf16[256,512]{1,0:T(8,128)(2,1)} %get-tuple-element.143), channel_id=1, source_target_pairs={{0,24},{4,28},{8,16},{12,20},{16,8},{20,12},{24,0},{28,4},{1,25},{... | collective-permute-start | bytes 786440 | tf_op jit(solution)/shard_map/ppermute | solution.py:42
  96.3 24.1 %collective-permute-start.10 = (bf16[256,512]{1,0:T(8,128)(2,1)}, bf16[256,512]{1,0:T(8,128)(2,1)S(1)}, u32[]{:S(2)}, u32[]{:S(2)}) collective-permute-start(bf16[256,512]{1,0:T(8,128)(2,1)} %get-tuple-element.147), channel_id=1, source_target_pairs={{0,8},{4,12},{8,0},{12,4},{16,24},{20,28},{24,16},{28,20},{1,9},{5... | collective-permute-start | bytes 786440 | tf_op jit(solution)/shard_map/ppermute | solution.py:42
  98.7 30.8 %collective-permute-start.15 = (bf16[256,512]{1,0:T(8,128)(2,1)}, bf16[256,512]{1,0:T(8,128)(2,1)S(1)}, u32[]{:S(2)}, u32[]{:S(2)}) collective-permute-start(bf16[256,512]{1,0:T(8,128)(2,1)} %get-tuple-element.153), channel_id=1, source_target_pairs={{0,16},{4,20},{8,24},{12,28},{16,0},{20,4},{24,8},{28,12},{1,17},{... | collective-permute-start | bytes 786440 | tf_op jit(solution)/shard_map/ppermute | solution.py:42
  108.8 30.9 %collective-permute-start.16 = (bf16[256,512]{1,0:T(8,128)(2,1)}, bf16[256,512]{1,0:T(8,128)(2,1)S(1)}, u32[]{:S(2)}, u32[]{:S(2)}) collective-permute-start(bf16[256,512]{1,0:T(8,128)(2,1)} %get-tuple-element.155), channel_id=1, source_target_pairs={{0,24},{4,28},{8,16},{12,20},{16,8},{20,12},{24,0},{28,4},{1,25},{... | collective-permute-start | bytes 786440 | tf_op jit(solution)/shard_map/ppermute | solution.py:42
  144.2 81.7 %all-gather.10.cloned.1.call-start = ((), (), s32[]{:S(2)}) async-start(), calls=%async_computation.7 | async-start | bytes 2359296 | tf_op jit(solution)/shard_map/all_gather | solution.py:185
  146.5 24.1 %collective-permute-start.19 = (bf16[4,256,512]{2,1,0:T(8,128)(2,1)S(1)}, bf16[4,256,512]{2,1,0:T(8,128)(2,1)S(1)}, u32[]{:S(2)}, u32[]{:S(2)}) collective-permute-start(bf16[4,256,512]{2,1,0:T(8,128)(2,1)S(1)} %copy-done.6), channel_id=1, source_target_pairs={{0,4},{4,0},{8,12},{12,8},{16,20},{20,16},{24,28},{28,24},{1,5},{5... | collective-permute-start | bytes 3145736 | tf_op jit(solution)/shard_map/ppermute | solution.py:42
  187.1 80.7 %reduce-scatter.7.cloned.1.call-start = ((), (), s32[]{:S(2)}) async-start(), calls=%async_computation.8 | async-start | bytes 2359296 | tf_op jit(solution)/shard_map/reduce_scatter | solution.py:191
  235.7 68.9 %all-gather.12.cloned.1.call-start = ((), (), s32[]{:S(2)}) async-start(), calls=%async_computation.10 | async-start | bytes 2359296 | tf_op jit(solution)/shard_map/all_gather | solution.py:185
  271.2 79.8 %reduce-scatter.9.cloned.1.call-start = ((), (), s32[]{:S(2)}) async-start(), calls=%async_computation.9 | async-start | bytes 2359296 | tf_op jit(solution)/shard_map/reduce_scatter | solution.py:191
  273.4 183.0 %reduce-scatter.11.cloned.1.call-start = ((), (), s32[]{:S(2)}) async-start(), calls=%async_computation.12 | async-start | bytes 2359296 | tf_op jit(solution)/shard_map/reduce_scatter | solution.py:191
  311.0 26.2 %collective-permute-start.32 = (bf16[4,256,512]{2,1,0:T(8,128)(2,1)}, bf16[4,256,512]{2,1,0:T(8,128)(2,1)}, u32[]{:S(2)}, u32[]{:S(2)}) collective-permute-start(bf16[4,256,512]{2,1,0:T(8,128)(2,1)} %pad_maximum_fusion.3), channel_id=1, source_target_pairs={{0,4},{4,0},{8,12},{12,8},{16,20},{20,16},{24,28},{28,24},{1,5},{5... | collective-permute-start | bytes 3145736 | tf_op jit(solution)/shard_map/ppermute | solution.py:42
  312.5 24.7 %collective-permute-start.30 = (bf16[4,256,512]{2,1,0:T(8,128)(2,1)S(1)}, bf16[4,256,512]{2,1,0:T(8,128)(2,1)S(1)}, u32[]{:S(2)}, u32[]{:S(2)}) collective-permute-start(bf16[4,256,512]{2,1,0:T(8,128)(2,1)S(1)} %pad_maximum_fusion.2), channel_id=1, source_target_pairs={{0,2},{1,3},{2,0},{3,1},{4,6},{5,7},{6,4},{7,5},{8,10},{9,11},{10,... | collective-permute-start | bytes 3145736 | tf_op jit(solution)/shard_map/ppermute | solution.py:42
  329.5 24.8 %collective-permute-start.35 = (bf16[256,512]{1,0:T(8,128)(2,1)}, bf16[256,512]{1,0:T(8,128)(2,1)}, u32[]{:S(2)}, u32[]{:S(2)}) collective-permute-start(bf16[256,512]{1,0:T(8,128)(2,1)} %get-tuple-element.254), channel_id=1, source_target_pairs={{0,8},{4,12},{8,0},{12,4},{16,24},{20,28},{24,16},{28,20},{1,9},{5... | collective-permute-start | bytes 786440 | tf_op jit(solution)/shard_map/ppermute | solution.py:42
  329.8 25.3 %collective-permute-start.36 = (bf16[256,512]{1,0:T(8,128)(2,1)}, bf16[256,512]{1,0:T(8,128)(2,1)}, u32[]{:S(2)}, u32[]{:S(2)}) collective-permute-start(bf16[256,512]{1,0:T(8,128)(2,1)} %get-tuple-element.253), channel_id=1, source_target_pairs={{0,16},{4,20},{8,24},{12,28},{16,0},{20,4},{24,8},{28,12},{1,17},{... | collective-permute-start | bytes 786440 | tf_op jit(solution)/shard_map/ppermute | solution.py:42
  336.9 24.5 %collective-permute-start.37 = (bf16[256,512]{1,0:T(8,128)(2,1)}, bf16[256,512]{1,0:T(8,128)(2,1)}, u32[]{:S(2)}, u32[]{:S(2)}) collective-permute-start(bf16[256,512]{1,0:T(8,128)(2,1)} %get-tuple-element.252), channel_id=1, source_target_pairs={{0,24},{4,28},{8,16},{12,20},{16,8},{20,12},{24,0},{28,4},{1,25},{... | collective-permute-start | bytes 786440 | tf_op jit(solution)/shard_map/ppermute | solution.py:42
  371.4 105.2 %all-gather.14.cloned.1.call-start = ((), (), s32[]{:S(2)}) async-start(), calls=%async_computation.11 | async-start | bytes 1310720 | tf_op jit(solution)/shard_map/all_gather | solution.py:1029
  375.9 31.4 %collective-permute-start.53 = (bf16[256,512]{1,0:T(8,128)(2,1)}, bf16[256,512]{1,0:T(8,128)(2,1)}, u32[]{:S(2)}, u32[]{:S(2)}) collective-permute-start(bf16[256,512]{1,0:T(8,128)(2,1)} %get-tuple-element.249), channel_id=1, source_target_pairs={{0,8},{4,12},{8,0},{12,4},{16,24},{20,28},{24,16},{28,20},{1,9},{5... | collective-permute-start | bytes 786440 | tf_op jit(solution)/shard_map/ppermute | solution.py:42
  377.1 30.9 %collective-permute-start.54 = (bf16[256,512]{1,0:T(8,128)(2,1)}, bf16[256,512]{1,0:T(8,128)(2,1)}, u32[]{:S(2)}, u32[]{:S(2)}) collective-permute-start(bf16[256,512]{1,0:T(8,128)(2,1)} %get-tuple-element.248), channel_id=1, source_target_pairs={{0,16},{4,20},{8,24},{12,28},{16,0},{20,4},{24,8},{28,12},{1,17},{... | collective-permute-start | bytes 786440 | tf_op jit(solution)/shard_map/ppermute | solution.py:42
  383.0 33.4 %collective-permute-start.55 = (bf16[256,512]{1,0:T(8,128)(2,1)}, bf16[256,512]{1,0:T(8,128)(2,1)}, u32[]{:S(2)}, u32[]{:S(2)}) collective-permute-start(bf16[256,512]{1,0:T(8,128)(2,1)} %get-tuple-element.247), channel_id=1, source_target_pairs={{0,24},{4,28},{8,16},{12,20},{16,8},{20,12},{24,0},{28,4},{1,25},{... | collective-permute-start | bytes 786440 | tf_op jit(solution)/shard_map/ppermute | solution.py:42
  403.9 29.7 %collective-permute-start.43 = (bf16[4,256,256]{2,1,0:T(8,128)(2,1)}, bf16[4,256,256]{2,1,0:T(8,128)(2,1)}, u32[]{:S(2)}, u32[]{:S(2)}) collective-permute-start(bf16[4,256,256]{2,1,0:T(8,128)(2,1)} %pad_maximum_fusion.10), channel_id=1, source_target_pairs={{0,2},{1,3},{2,0},{3,1},{4,6},{5,7},{6,4},{7,5},{8,10},{9,11},{10,... | collective-permute-start | bytes 1572872 | tf_op jit(solution)/shard_map/ppermute | solution.py:42
  406.7 26.9 %collective-permute-start.45 = (bf16[4,256,256]{2,1,0:T(8,128)(2,1)}, bf16[4,256,256]{2,1,0:T(8,128)(2,1)}, u32[]{:S(2)}, u32[]{:S(2)}) collective-permute-start(bf16[4,256,256]{2,1,0:T(8,128)(2,1)} %pad_maximum_fusion.11), channel_id=1, source_target_pairs={{0,4},{4,0},{8,12},{12,8},{16,20},{20,16},{24,28},{28,24},{1,5},{5... | collective-permute-start | bytes 1572872 | tf_op jit(solution)/shard_map/ppermute | solution.py:42
  435.7 26.7 %collective-permute-start.46 = (bf16[256,256]{1,0:T(8,128)(2,1)S(1)}, bf16[256,256]{1,0:T(8,128)(2,1)S(1)}, u32[]{:S(2)}, u32[]{:S(2)}) collective-permute-start(bf16[256,256]{1,0:T(8,128)(2,1)S(1)} %get-tuple-element.261), channel_id=1, source_target_pairs={{0,8},{4,12},{8,0},{12,4},{16,24},{20,28},{24,16},{28,20},{1,9},{5... | collective-permute-start | bytes 393224 | tf_op jit(solution)/shard_map/ppermute | solution.py:42
  437.2 25.2 %collective-permute-start.47 = (bf16[256,256]{1,0:T(8,128)(2,1)S(1)}, bf16[256,256]{1,0:T(8,128)(2,1)S(1)}, u32[]{:S(2)}, u32[]{:S(2)}) collective-permute-start(bf16[256,256]{1,0:T(8,128)(2,1)S(1)} %get-tuple-element.260), channel_id=1, source_target_pairs={{0,16},{4,20},{8,24},{12,28},{16,0},{20,4},{24,8},{28,12},{1,17},{... | collective-permute-start | bytes 393224 | tf_op jit(solution)/shard_map/ppermute | solution.py:42
  441.6 25.8 %collective-permute-start.59 = (f32[4,256]{1,0:T(4,128)S(1)}, f32[4,256]{1,0:T(4,128)S(1)}, u32[]{:S(2)}, u32[]{:S(2)}) collective-permute-start(f32[4,256]{1,0:T(4,128)S(1)} %fusion.24), channel_id=1, source_target_pairs={{0,1},{1,0},{2,3},{3,2},{4,5},{5,4},{6,7},{7,6},{8,9},{9,8},{10,11... | collective-permute-start | bytes 12296 | tf_op jit(solution)/shard_map/ppermute | solution.py:42
  (104 other events, 997.4 us)
Sparse Core Ops, SparseCore 0:
  39.6 46.5 all-gather.5
  88.3 46.9 all-gather.7
  144.3 30.2 reduce-scatter.4
  187.3 30.3 all-gather.9
  235.8 31.9 reduce-scatter.6
  271.4 33.1 all-gather.11
  307.4 29.8 reduce-scatter.8
  371.5 59.4 reduce-scatter.10
  432.6 14.8 all-gather.13

commit v4 on v3

--- a/solution.py
+++ b/solution.py
@@ -239,7 +239,7 @@
         pl.when(pl.program_id(0) == step)(partial(body, step))
 
 
-def pack_attention_kernel(at_ref, weight_ref, turned_ref, norm_ref, marks_ref, *refs):
+def pack_attention_kernel(at_ref, span_ref, weight_ref, turned_ref, norm_ref, label_ref, *refs):
     outs, aux = refs[:4], refs[4]
     rows, head = weight_ref.shape[1:]
 
@@ -249,35 +249,38 @@
         outs[step][:rows, 3 * head :] = turned_ref[...].T.astype(BF16)
         aux[...] = jnp.zeros_like(aux)
         aux[:4, : norm_ref.shape[1]] = norm_ref[...]
-        aux[8:10, : marks_ref.shape[1]] = marks_ref[...].astype(F32)
+        aux[8:9, : label_ref.shape[1]] = label_ref[...].astype(F32)
+        for i in range(label_ref.shape[1] // SPAN):
+            place = jnp.full((1, SPAN), lax.rem(span_ref[i], ROW_LEN // SPAN), jnp.int32)
+            aux[9:10, i * SPAN : (i + 1) * SPAN] = place.astype(F32)
         outs[step][rows:, :] = aux[...].astype(BF16)
 
     at_steps(body)
 
 
-def pack_attention(at, weight, turned, norms, marks):
+def pack_attention(at, spans, weight, turned, norms, labels):
     _, rows, width = weight.shape
     head = width // 4
     shape = (rows + AUX, 4 * head)
     return pl.pallas_call(
         pack_attention_kernel,
         grid_spec=pltpu.PrefetchScalarGridSpec(
-            num_scalar_prefetch=1,
+            num_scalar_prefetch=2,
             grid=(4,),
             in_specs=[
-                pl.BlockSpec((3, rows, head), lambda i, at: (0, 0, at[0] ^ i)),
-                pl.BlockSpec((head, rows), lambda i, at: (at[0] ^ i, 0)),
-                pl.BlockSpec(norms.shape, lambda i, at: (0, 0)),
-                pl.BlockSpec(marks.shape, lambda i, at: (0, 0)),
+                pl.BlockSpec((3, rows, head), lambda i, at, _: (0, 0, at[0] ^ i)),
+                pl.BlockSpec((head, rows), lambda i, at, _: (at[0] ^ i, 0)),
+                pl.BlockSpec(norms.shape, lambda i, at, _: (0, 0)),
+                pl.BlockSpec(labels.shape, lambda i, at, _: (0, 0)),
             ],
-            out_specs=[pl.BlockSpec(shape, lambda i, at: (0, 0))] * 4,
+            out_specs=[pl.BlockSpec(shape, lambda i, at, _: (0, 0))] * 4,
             scratch_shapes=[pltpu.VMEM((AUX, 4 * head), F32)],
         ),
         out_shape=[jax.ShapeDtypeStruct(shape, BF16)] * 4,
         compiler_params=PARAMS,
         cost_estimate=SMALL,
         name="pack_attention",
-    )(at, weight, turned, norms, marks)
+    )(at, spans, weight, turned, norms, labels)
 
 
 def pack_kernel(turns, at_ref, *refs):
@@ -607,7 +610,7 @@
         out_shape=[jax.ShapeDtypeStruct(shape, BF16) for shape in shapes],
         scratch_shapes=[pltpu.VMEM((AUX, units), F32)] if extra else [],
         compiler_params=PARAMS,
-        cost_estimate=cost(6),
+        cost_estimate=cost(3),
         name="weight_grads",
     )(*[left for left, _ in pairs], *[right for _, right in pairs], *([sums] if extra else []))
     return {
@@ -631,21 +634,24 @@
         i += parts
 
 
+LOG2E = 1.4426950408889634
+
+
 def attend_kernel(scaling, layout, q_ref, qm_ref, km_ref, *refs):
     members, (out_ref, low_ref, lse_ref, kv_ref) = refs[:-4], refs[-4:]
     pl.when(pl.program_id(1) == 0)(lambda: collect(layout, members, kv_ref))
     head = q_ref.shape[1]
     keys, values = kv_ref[:, :head], kv_ref[:, head:]
-    scores = dot(q_ref[...], keys, COLS_BY_COLS) * scaling
+    scores = dot(q_ref[...], keys, COLS_BY_COLS)
     scores = jnp.where(visible(qm_ref[...], km_ref[...]), scores, -1e30)
     largest = jnp.max(scores, axis=1, keepdims=True)
-    weights = jnp.exp(scores - largest)
+    weights = jnp.exp2((scores - largest) * (scaling * LOG2E))
     totals = jnp.sum(weights, axis=1, keepdims=True)
     probs = (weights * (1.0 / totals)).astype(BF16)
     attended = dot(probs, values)
     out_ref[...] = attended
     low_ref[...] = attended.astype(BF16)
-    lse_ref[0] = largest + jnp.log(totals)
+    lse_ref[0] = largest * scaling + jnp.log(totals)
 
 
 def attend_back_kernel(
@@ -660,9 +666,9 @@
     keys, values = kv_ref[:, :head], kv_ref[:, head:]
     grad = grad_ref[...]
     row_dots = jnp.sum(grad.astype(F32) * out_ref[...], axis=1, keepdims=True)
-    scores = dot(q_ref[...], keys, COLS_BY_COLS) * scaling
+    scores = dot(q_ref[...], keys, COLS_BY_COLS)
     scores = jnp.where(visible(qm_ref[...], km_ref[...]), scores, -1e30)
-    probs = jnp.exp(scores - lse_ref[0])
+    probs = jnp.exp2(scores * (scaling * LOG2E) - lse_ref[0] * LOG2E)
     prob_grad = dot(grad, values, COLS_BY_COLS)
     score_grad = (probs * (prob_grad - row_dots)).astype(BF16)
     dq_ref[...] = (dot(score_grad, keys) * scaling).astype(BF16)
@@ -695,7 +701,7 @@
             at += count_out(*key)
 
 
-BLOCK = 256
+BLOCK = 512
 
 
 def member_specs(members):
@@ -717,19 +723,20 @@
     arrays, specs, layout = member_specs(members)
     count, head = queries.shape[0], queries.shape[1] // 2
     length = key_marks.shape[1]
+    block = BLOCK if length <= 2048 else 256
     return pl.pallas_call(
         partial(attend_kernel, scaling, layout),
-        grid=(2, count // BLOCK),
+        grid=(2, count // block),
         in_specs=[
-            pl.BlockSpec((BLOCK, head), lambda h, i: (i, h)),
-            pl.BlockSpec((BLOCK, 2), lambda h, i: (i, 0)),
+            pl.BlockSpec((block, head), lambda h, i: (i, h)),
+            pl.BlockSpec((block, 2), lambda h, i: (i, 0)),
             pl.BlockSpec((2, length), lambda h, i: (0, 0)),
         ]
         + specs,
         out_specs=[
-            pl.BlockSpec((BLOCK, head), lambda h, i: (i, h)),
-            pl.BlockSpec((BLOCK, head), lambda h, i: (i, h)),
-            pl.BlockSpec((1, BLOCK, 1), lambda h, i: (h, i, 0)),
+            pl.BlockSpec((block, head), lambda h, i: (i, h)),
+            pl.BlockSpec((block, head), lambda h, i: (i, h)),
+            pl.BlockSpec((1, block, 1), lambda h, i: (h, i, 0)),
         ],
         out_shape=[
             jax.ShapeDtypeStruct((count, 2 * head), F32),
@@ -747,7 +754,7 @@
     arrays, specs, layout = member_specs(members)
     count, head = queries.shape[0], queries.shape[1] // 2
     length = key_marks.shape[1]
-    block = BLOCK if length <= 2048 else 128
+    block = 512 if length <= 2048 else 128
     rows = pl.BlockSpec((block, head), lambda h, i: (i, h))
     outs = pl.pallas_call(
         partial(attend_back_kernel, scaling, layout),
@@ -780,7 +787,7 @@
             pltpu.VMEM((length, 2 * head), BF16),
         ],
         compiler_params=PARAMS,
-        cost_estimate=SMALL,
+        cost_estimate=cost(12),
         name="attend_back",
     )(queries, query_marks, key_marks, attended, logsum, grad, *arrays)
     pieces, at = {}, 1
@@ -936,14 +943,14 @@
     def shares(total, ready=None):
         return exchange(blocks_of(total), ready)
 
-    span_places = jnp.repeat(span_map % (ROW_LEN // SPAN), SPAN)
     input_cube = attention_input.transpose(1, 0, 2)
     first_packed = pack_attention(
         at_word,
+        span_map,
         input_cube,
         attention_output,
         norm_params,
-        jnp.stack([segment_ids, span_places]),
+        segment_ids[None],
     )
     first_parts = exchange(first_packed)
     own_tokens = to_relative(after(own_rows(tokens), first_packed[0]))
@@ -952,11 +959,11 @@
     )
     own_cotangent = to_relative(after(own_rows(cotangent), expand_packed[0]))
     group_tokens = gather_tokens(after(own_tokens, own_cotangent, *first_parts[1:]))
-    expand_parts = exchange(expand_packed, first_parts[1:])
-    reduce_parts = exchange(reduce_packed, expand_parts[1:])
     (first_own,) = assemble(at_word, [after(first_parts[0], own_cotangent)] + first_parts[1:])
     low = gather_groups(first_own)
-    group_cotangent = gather_tokens(after(own_cotangent, first_own))
+    expand_parts = exchange(expand_packed, first_parts[1:])
+    group_cotangent = gather_tokens(after(own_cotangent, expand_parts[2]))
+    reduce_parts = exchange(reduce_packed, expand_parts[1:])
 
     aux = jnp.stack([low[0, t][0][:, shard:] for t in range(groups)])
     norm_values = aux[:, :, :4, :shard].transpose(2, 0, 1, 3).reshape(4, width).astype(F32)
@@ -973,9 +980,9 @@
     normed_one, queries, own_kv = project(
         after(group_tokens, key_marks, *expand_parts[1:]), norm_values, low, shard, head
     )
-    kv_low = gather_groups(own_kv)
     (expand_own,) = assemble(at_word, expand_parts)
-    expand_low = gather_groups(expand_own, kv_low[1, 1])
+    kv_low = gather_groups(own_kv, (), tuple(expand_parts[1:]))
+    expand_low = gather_groups(expand_own, first_level(kv_low))
     attended, mixed, logsum = attend(
         after(queries, expand_own, reduce_parts[1]),
         kv_low,
@@ -983,46 +990,54 @@
         key_marks,
         scaling,
     )
-    (reduce_own,) = assemble(at_word, [after(reduce_parts[0], mixed)] + reduce_parts[1:])
-    reduce_low = gather_groups(reduce_own, expand_low[1, 1])
-    branch = scatter_tokens(to_features(after(mixed, group_cotangent, *reduce_parts[2:]), low, shard, (head, 3), width))
+    (reduce_own,) = assemble(at_word, [after(reduce_parts[0], own_kv)] + reduce_parts[1:])
+    reduce_low = gather_groups(reduce_own, first_level(expand_low))
+    branch = scatter_tokens(
+        to_features(after(mixed, group_cotangent, *reduce_parts[2:]), low, shard, (head, 3), width)
+    )
     middle = own_tokens.astype(F32) + branch.astype(F32)
 
-    shape_two, scale_two = normalize(after(middle, *expand_low[1, 1]))
-    normed_two = gather_tokens((shape_two * norm_values[2] + norm_values[3]).astype(BF16))
-    active_grad = to_units(group_cotangent, reduce_low, shard, (units, 0), F32, cost(25))
+    shape_two, scale_two = normalize(middle)
+    normed_two = gather_tokens(
+        (shape_two * norm_values[2] + norm_values[3]).astype(BF16)
+    )
+    active_grad = to_units(
+        group_cotangent, reduce_low, shard, (units, 0), F32, cost(25)
+    )
     active, hidden_grad, second_terms = feed_forward(
         normed_two, active_grad, expand_low, shard, units
     )
     second_grad = scatter_tokens(second_terms)
     reduce_pieces = weight_grads([(group_cotangent, active)], groups)
     reduce_sum, reduce_first, reduce_came, reduce_sent = reduce_groups(reduce_pieces)
-    expand_pieces = weight_grads([(normed_two, after(hidden_grad, reduce_pieces[0, 0][0]))], groups)
-    feed_terms = to_features(
-        after(active, expand_pieces[0, 0][0]), reduce_low, shard, (units, 0), width, cost(6)
+    expand_pieces = weight_grads(
+        [(normed_two, after(hidden_grad, reduce_pieces[0, 0][0]))], groups
     )
     middle_part, gain_two, bias_two = norm_back(
-        shape_two, scale_two, norm_values[2], after(second_grad, feed_terms, *reduce_sent).astype(F32)
+        shape_two, scale_two, norm_values[2], after(second_grad, *reduce_sent).astype(F32)
     )
     middle_grad = own_cotangent.astype(F32) + middle_part
     middle_low = middle_grad.astype(BF16)
+    feed_terms = to_features(
+        after(active, middle_low), reduce_low, shard, (units, 0), width, SMALL
+    )
     branch_grad = gather_tokens(middle_low)
+
+    mixed_grad = to_units(branch_grad, low, shard, (head, 3), BF16, cost(4))
     feed = scatter_tokens(after(feed_terms, middle_low))
-
-    mixed_grad = to_units(
-        branch_grad, low, shard, (head, 3), BF16
-    )
-    expand_sum, _, expand_came, _ = reduce_groups(expand_pieces, reduce_came, (mixed_grad,))
     query_grad, kv_pieces = attend_back(
         queries, kv_low, query_marks, key_marks, attended, logsum, mixed_grad, scaling
     )
-    own_kv_grad, kv_first, kv_came, _ = reduce_groups(kv_pieces, expand_came)
+    expand_sum, expand_first, expand_came, _ = reduce_groups(
+        expand_pieces, reduce_came, (mixed_grad,), ()
+    )
+    own_kv_grad, kv_first, kv_came, kv_sent = reduce_groups(kv_pieces, expand_came)
     reduce_shares = shares(after(reduce_sum, query_grad))
     expand_shares = shares(after(expand_sum, query_grad))
     query_pieces = weight_grads(
         [(branch_grad, after(mixed, kv_pieces[1, 1][0])), (normed_one, query_grad)], groups
     )
-    query_sum, _, query_came, _ = reduce_groups(query_pieces, kv_came)
+    query_sum, query_first, _, _ = reduce_groups(query_pieces, kv_came)
     natural_output = to_natural(
         (middle + after(feed, *kv_first).astype(F32)).astype(BF16)
     )
@@ -1038,8 +1053,12 @@
     first_grad = scatter_tokens(first_terms)
     all_sums = jnp.concatenate([norm_sums, gain_two[None], bias_two[None]])
     shape_one, scale_one = normalize(own_tokens.astype(F32))
+    input_part, _, _ = norm_back(
+        shape_one, scale_one, norm_values[0], first_grad.astype(F32)
+    )
+    natural_grad = to_natural((middle_grad + input_part).astype(BF16))
     pair_pieces = weight_grads(
-        [(normed_one, own_kv_grad)], groups, all_sums
+        [(normed_one, after(own_kv_grad, *query_first))], groups, all_sums
     )
     reduce_new = adam(
         at_word,
@@ -1056,8 +1075,8 @@
         "plain",
         [([after(expand_shares[0], *pair_sent)] + expand_shares[1:], 0, units)],
     )
-    query_shares = shares(query_sum)
-    pair_shares = shares(after(pair_sum, expand_new[0]))
+    query_shares = shares(after(query_sum, *pair_sent))
+    pair_shares = shares(after(pair_sum, expand_new[0], natural_grad))
     share_norm = sum(part[shard : shard + 4, :shard].astype(F32) for part in pair_shares)
     share_norm = share_norm + over_c(share_norm)
     share_norm = share_norm + over_x(share_norm)
@@ -1069,10 +1088,7 @@
         "turned",
         [(query_shares, 0, head)],
     )
-    input_part, _, _ = norm_back(
-        shape_one, scale_one, norm_values[0], first_grad.astype(F32)
-    )
-    input_grad = all_lanes(to_natural((middle_grad + input_part).astype(BF16))).astype(F32)
+    input_grad = all_lanes(natural_grad).astype(F32)
     input_new = adam(
         at_word,
         (
@@ -1083,7 +1099,7 @@
         input_rate,
         "cube",
         [
-            ([after(query_shares[0], output_new[0])] + query_shares[1:], head, 2 * head),
+            ([query_shares[0]] + query_shares[1:], head, 2 * head),
             (pair_shares, 0, 2 * head),
         ],
     )

time: 496 us -> 475 us (0.958)
  starting transfers between devices: 82.8 us -> 73.9 us
  local copies, waits for them, and re-layouts: 32.1 us -> 25.7 us
  other arithmetic: 42.5 us -> 36.6 us
    ppermute x61, waiting for transfers between devices: 171 us -> 131 us  [swap(): return lax.ppermute(value, axis, [(i, i ^ mask) for i in range(size)])]
    reduce_scatter x4, waiting for transfers between devices: 7.29 us -> 39.4 us  [scatter_tokens(): lax.psum_scatter(partial_sums, ('fsdp', 'mp'), axis_index_groups=token_gr...]
    all_gather x4, waiting for transfers between devices: 8.63 us -> 17.8 us  [gather_tokens(): lax.all_gather(own, ('fsdp', 'mp'), axis_index_groups=token_groups(), axi...]
    ppermute x61, starting transfers between devices: 82 us -> 72.9 us  [swap(): return lax.ppermute(value, axis, [(i, i ^ mask) for i in range(size)])]
    unnamed x133 -> x137, local copies, waits for them, and re-layouts: 14.9 us -> 7.32 us
  transfers between devices with their start and end apart: 70 -> 70, of which waited for: 26 -> 31; matrix products, arithmetic and copies ran while one was open for 10% -> 10% of each run, Pallas kernels for 21% -> 22%
where the time goes in v4:
time: 475 us; the launch traced here: 466 us
  waiting for transfers between devices  188 us (40%)
  Pallas kernels  126 us (27%)
  starting transfers between devices  73.9 us (16%)
  other arithmetic  36.6 us (8%)
  local copies, waits for them, and re-layouts  25.7 us (5%)
  between operations  15.3 us (3%)
    ppermute x61, waiting for transfers between devices, swap(): return lax.ppermute(value, axis, [(i, i ^ mask) for i in range(size)])  131 us
    ppermute x61, starting transfers between devices, swap(): return lax.ppermute(value, axis, [(i, i ^ mask) for i in range(size)])  72.9 us
    reduce_scatter x4, waiting for transfers between devices, scatter_tokens(): lax.psum_scatter(partial_sums, ('fsdp', 'mp'), axis_index_groups=token_gr...  39.4 us
    pallas_call x4, Pallas kernels, adam(): pl.pallas_call(partial(adam_kernel, rate, shape, columns), grid_spec=pltp...  25.2 us
    pallas_call x4, Pallas kernels, weight_grads(): pl.pallas_call(partial(grads_kernel, groups, len(pairs), extra), grid=(gr...  22.8 us
    all_gather x4, waiting for transfers between devices, gather_tokens(): lax.all_gather(own, ('fsdp', 'mp'), axis_index_groups=token_groups(), axi...  17.8 us
    convert_element_type x15, other arithmetic, add(): return total.astype(BF16)  13.3 us
    pallas_call x1, Pallas kernels, attend_back(): pl.pallas_call(partial(attend_back_kernel, scaling, layout), grid=(2, cou...  10.4 us
  transfers between devices with their start and end apart: 70, of which 31 were waited for; matrix products, arithmetic and copies ran while one was open for 10% of the time, Pallas kernels for 22%

profile of v4, /device:TPU:9, one launch (start us, length us, event | category | flops | bytes accessed | tf_op | source)
XLA Modules:
  0.0 466.1 jit_solution(17330504573954436597)
XLA Ops:
  26.3 11.8 %collective-permute-done.2.refs_3_ = bf16[272,512]{1,0:T(8,128)(2,1)S(1)} collective-permute-done((bf16[272,512]{1,0:T(8,128)(2,1)}, bf16[272,512]{1,0:T(8,128)(2,1)S(1)}, u32[]{:S(2)}, u32[]{:S(2)}) %collective-permute-start.2) | collective-permute-done | bytes 278560 | tf_op jit(solution)/shard_map/ppermute | solution.py:42
  38.3 9.7 %collective-permute-done.5.refs_2_ = bf16[256,512]{1,0:T(8,128)(2,1)S(1)} collective-permute-done((bf16[256,512]{1,0:T(8,128)(2,1)S(1)}, bf16[256,512]{1,0:T(8,128)(2,1)S(1)}, u32[]{:S(2)}, u32[]{:S(2)}) %collective-permute-start.5) | collective-permute-done | bytes 262176 | tf_op jit(solution)/shard_map/ppermute | solution.py:42
  52.8 5.4 %collective-permute-start.4 = (bf16[256,512]{1,0:T(8,128)(2,1)}, bf16[256,512]{1,0:T(8,128)(2,1)}, u32[]{:S(2)}, u32[]{:S(2)}) collective-permute-start(bf16[256,512]{1,0:T(8,128)(2,1)} %get-tuple-element.141), channel_id=1, source_target_pairs={{0,8},{4,12},{8,0},{12,4},{16,24},{20,28},{24,16},{28,20},{1,9},{5... | collective-permute-start | bytes 786440 | tf_op jit(solution)/shard_map/ppermute | solution.py:42
  59.1 6.7 %collective-permute-done.3.refs_1_ = bf16[4,272,512]{2,1,0:T(8,128)(2,1)S(1)} collective-permute-done((bf16[4,272,512]{2,1,0:T(8,128)(2,1)}, bf16[4,272,512]{2,1,0:T(8,128)(2,1)S(1)}, u32[]{:S(2)}, u32[]{:S(2)}) %collective-permute-start.3) | collective-permute-done | bytes 1114144 | tf_op jit(solution)/shard_map/ppermute | solution.py:42
  75.9 7.3 %collective-permute-done.8.refs_3_ = bf16[2,272,512]{2,1,0:T(8,128)(2,1)S(1)} collective-permute-done((bf16[2,272,512]{2,1,0:T(8,128)(2,1)}, bf16[2,272,512]{2,1,0:T(8,128)(2,1)S(1)}, u32[]{:S(2)}, u32[]{:S(2)}) %collective-permute-start.8) | collective-permute-done | bytes 557088 | tf_op jit(solution)/shard_map/ppermute | solution.py:42
  84.2 6.9 %project.1 = (bf16[512,2048]{1,0:T(8,128)(2,1)}, bf16[512,256]{1,0:T(8,128)(2,1)}, bf16[2,512,256]{2,1,0:T(8,128)(2,1)}) custom-call(bf16[512,2048]{1,0:T(8,128)(2,1)} %all-gather.6.cloned.1.call-done.tokens_ref, f32[4,2048]{1,0:T(4,128)} %bitcast.110, bf16[4,272,512]{2,1,0:T(8,128)(2,1)} %assemble.3.refs_0_, bf16[4,272,512]{2,1,0:T(8,128)(2,1)} %copy-done, ...), custom_call_target="tpu_custom_call" | custom-call | flops 1 | bytes 1 | tf_op jit(solution)/shard_map/project/pallas_call | solution.py:399
  92.9 5.4 %collective-permute-start.10 = (bf16[256,512]{1,0:T(8,128)(2,1)}, bf16[256,512]{1,0:T(8,128)(2,1)S(1)}, u32[]{:S(2)}, u32[]{:S(2)}) collective-permute-start(bf16[256,512]{1,0:T(8,128)(2,1)} %get-tuple-element.149), channel_id=1, source_target_pairs={{0,8},{4,12},{8,0},{12,4},{16,24},{20,28},{24,16},{28,20},{1,9},{5... | collective-permute-start | bytes 786440 | tf_op jit(solution)/shard_map/ppermute | solution.py:42
  110.1 9.3 %attend.1 = (f32[512,256]{1,0:T(8,128)}, bf16[512,256]{1,0:T(8,128)(2,1)}, f32[2,512,1]{2,1,0:T(8,128)}) custom-call(bf16[512,256]{1,0:T(8,128)(2,1)} %get-tuple-element.150.q_ref, s32[512,2]{1,0:T(8,128)} %bitcast.99, s32[2,2048]{1,0:T(2,128)} %reshape.168.km_ref, bf16[2,512,256]{2,1,0:T(8,128)(2,1)} %get-tuple-element.151.refs_0_, ...), custom_call_target="tpu_custom_call" | custom-call | flops 1 | bytes 1 | tf_op jit(solution)/shard_map/attend/pallas_call | solution.py:727
  132.4 7.4 %collective-permute-done.17.refs_2_ = bf16[4,256,512]{2,1,0:T(8,128)(2,1)S(1)} collective-permute-done((bf16[4,256,512]{2,1,0:T(8,128)(2,1)S(1)}, bf16[4,256,512]{2,1,0:T(8,128)(2,1)S(1)}, u32[]{:S(2)}, u32[]{:S(2)}) %collective-permute-start.17) | collective-permute-done | bytes 1048608 | tf_op jit(solution)/shard_map/ppermute | solution.py:42
  143.5 26.4 %reduce-scatter.5.cloned.1.call-done = bf16[64,2048]{1,0:T(8,128)(2,1)} async-done(((bf16[512,2048]{1,0:T(8,128)(2,1)}), bf16[64,2048]{1,0:T(8,128)(2,1)}) %reduce-scatter.5.cloned.1.call-update) | async-done | bytes 262160 | tf_op jit(solution)/shard_map/reduce_scatter | solution.py:191
  180.8 4.9 %collective-permute-done.21.refs_3_ = bf16[2,256,512]{2,1,0:T(8,128)(2,1)S(1)} collective-permute-done((bf16[2,256,512]{2,1,0:T(8,128)(2,1)S(1)}, bf16[2,256,512]{2,1,0:T(8,128)(2,1)S(1)}, u32[]{:S(2)}, u32[]{:S(2)}) %collective-permute-start.21) | collective-permute-done | bytes 524320 | tf_op jit(solution)/shard_map/ppermute | solution.py:42
  186.5 6.1 %to_units.2.pull_ref = f32[512,1024]{1,0:T(8,128)} custom-call(bf16[512,2048]{1,0:T(8,128)(2,1)} %all-gather.8.cloned.1.call-done.value_ref.refs_0_, bf16[4,256,512]{2,1,0:T(8,128)(2,1)} %assemble.5.refs_0_, bf16[4,256,512]{2,1,0:T(8,128)(2,1)} %copy-done.5, bf16[4,256,512]{2,1,0:T(8,128)(2,1)} %copy-done.6, bf16[2,256,512]{2,1,0:T(8,128)(2,1)} %copy-done.26, ...), custom_call_target="tpu_custom_call" | custom-call | flops 28750000128 | bytes 1 | tf_op jit(solution)/shard_map/to_units/pallas_call | solution.py:430
  197.0 11.3 %all-gather.10.cloned.1.call-done.value_ref.refs_0_ = bf16[512,2048]{1,0:T(8,128)(2,1)} async-done(((bf16[64,2048]{1,0:T(8,128)(2,1)}), bf16[512,2048]{1,0:T(8,128)(2,1)}) %all-gather.10.cloned.1.call-update) | async-done | bytes 2097168 | tf_op jit(solution)/shard_map/all_gather | solution.py:185
  208.3 9.8 %feed_forward.1 = (bf16[512,1024]{1,0:T(8,128)(2,1)}, bf16[512,1024]{1,0:T(8,128)(2,1)}, bf16[512,2048]{1,0:T(8,128)(2,1)}) custom-call(bf16[512,2048]{1,0:T(8,128)(2,1)} %all-gather.10.cloned.1.call-done.value_ref.refs_0_, f32[512,1024]{1,0:T(8,128)} %to_units.2.pull_ref, bf16[4,256,512]{2,1,0:T(8,128)(2,1)} %assemble.4.refs_0_, ...), custom_call_target="tpu_custom_call" | custom-call | flops 1 | bytes 1 | tf_op jit(solution)/shard_map/feed_forward/pallas_call | solution.py:493
  218.2 6.2 %weight_grads.4 = (bf16[4,256,512]{2,1,0:T(8,128)(2,1)}, bf16[4,256,512]{2,1,0:T(8,128)(2,1)}, bf16[4,256,512]{2,1,0:T(8,128)(2,1)}, bf16[2,256,512]{2,1,0:T(8,128)(2,1)}, bf16[2,256,512]{2,1,0:T(8,128)(2,1)}) custom-call(bf16[512,2048]{1,0:T(8,128)(2,1)} %all-gather.8.cloned.1.call-done.value_ref.refs_0_, bf16[512,1024]{1,0:T(8,128)(2,1)} %get-tuple-element.172.refs_1_.value_ref), custom_call_target="tpu_custom_call" | custom-call | flops 3449999872 | bytes 1 | tf_op jit(solution)/shard_map/weight_grads/pallas_call | solution.py:603
  229.0 8.9 %collective-permute-done.25 = bf16[2,256,512]{2,1,0:T(8,128)(2,1)S(1)} collective-permute-done((bf16[2,256,512]{2,1,0:T(8,128)(2,1)}, bf16[2,256,512]{2,1,0:T(8,128)(2,1)S(1)}, u32[]{:S(2)}, u32[]{:S(2)}) %collective-permute-start.25) | collective-permute-done | bytes 524320 | tf_op jit(solution)/shard_map/ppermute | solution.py:42
  240.0 8.3 %reduce-scatter.7.cloned.1.call-done = bf16[64,2048]{1,0:T(8,128)(2,1)} async-done(((bf16[512,2048]{1,0:T(8,128)(2,1)}), bf16[64,2048]{1,0:T(8,128)(2,1)}) %reduce-scatter.7.cloned.1.call-update) | async-done | bytes 262160 | tf_op jit(solution)/shard_map/reduce_scatter | solution.py:191
  254.4 5.9 %to_features.3 = bf16[512,2048]{1,0:T(8,128)(2,1)} custom-call(bf16[512,1024]{1,0:T(8,128)(2,1)} %get-tuple-element.172.refs_1_.value_ref, bf16[4,256,512]{2,1,0:T(8,128)(2,1)} %assemble.5.refs_0_, bf16[4,256,512]{2,1,0:T(8,128)(2,1)} %copy-done.5, bf16[4,256,512]{2,1,0:T(8,128)(2,1)} %copy-done.6, bf16[2,256,512]{2,1,0:T(8,128)(2,1)} %copy-done.26, ...), custom_call_target="tpu_custom_call" | custom-call | flops 1 | bytes 1 | tf_op jit(solution)/shard_map/to_features/pallas_call | solution.py:455
  260.8 6.2 %weight_grads.5 = (bf16[4,256,512]{2,1,0:T(8,128)(2,1)}, bf16[4,256,512]{2,1,0:T(8,128)(2,1)}, bf16[4,256,512]{2,1,0:T(8,128)(2,1)}, bf16[2,256,512]{2,1,0:T(8,128)(2,1)}, bf16[2,256,512]{2,1,0:T(8,128)(2,1)}) custom-call(bf16[512,2048]{1,0:T(8,128)(2,1)} %all-gather.10.cloned.1.call-done.value_ref.refs_0_, bf16[512,1024]{1,0:T(8,128)(2,1)} %get-tuple-element.179.refs_1_), custom_call_target="tpu_custom_call" | custom-call | flops 3449999872 | bytes 1 | tf_op jit(solution)/shard_map/weight_grads/pallas_call | solution.py:603
  267.0 8.4 %collective-permute-done.27 = bf16[4,256,512]{2,1,0:T(8,128)(2,1)S(1)} collective-permute-done((bf16[4,256,512]{2,1,0:T(8,128)(2,1)S(1)}, bf16[4,256,512]{2,1,0:T(8,128)(2,1)S(1)}, u32[]{:S(2)}, u32[]{:S(2)}) %collective-permute-start.27) | collective-permute-done | bytes 1048608 | tf_op jit(solution)/shard_map/ppermute | solution.py:42
  279.1 6.5 %all-gather.12.cloned.1.call-done.value_ref.refs_0_ = bf16[512,2048]{1,0:T(8,128)(2,1)} async-done(((bf16[64,2048]{1,0:T(8,128)(2,1)}), bf16[512,2048]{1,0:T(8,128)(2,1)}) %all-gather.12.cloned.1.call-update) | async-done | bytes 2097168 | tf_op jit(solution)/shard_map/all_gather | solution.py:185
  295.4 10.4 %attend_back.1 = (bf16[512,256]{1,0:T(8,128)(2,1)}, bf16[2,512,256]{2,1,0:T(8,128)(2,1)}, bf16[2,512,256]{2,1,0:T(8,128)(2,1)}, bf16[2,512,256]{2,1,0:T(8,128)(2...) custom-call(bf16[512,256]{1,0:T(8,128)(2,1)} %get-tuple-element.150.q_ref, s32[512,2]{1,0:T(8,128)} %bitcast.100, ...), custom_call_target="tpu_custom_call" | custom-call | flops 13799999488 | bytes 1 | tf_op jit(solution)/shard_map/attend_back/pallas_call | solution.py:759
  307.0 7.3 %collective-permute-start.36 = (bf16[256,512]{1,0:T(8,128)(2,1)}, bf16[256,512]{1,0:T(8,128)(2,1)}, u32[]{:S(2)}, u32[]{:S(2)}) collective-permute-start(bf16[256,512]{1,0:T(8,128)(2,1)} %get-tuple-element.260), channel_id=1, source_target_pairs={{0,16},{4,20},{8,24},{12,28},{16,0},{20,4},{24,8},{28,12},{1,17},{... | collective-permute-start | bytes 786440 | tf_op jit(solution)/shard_map/ppermute | solution.py:42
  319.9 5.9 %weight_grads.6 = (bf16[4,256,256]{2,1,0:T(8,128)(2,1)}, bf16[4,256,256]{2,1,0:T(8,128)(2,1)}, bf16[4,256,256]{2,1,0:T(8,128)(2,1)}, bf16[2,256,256]{2,1,0:T(8,128)(2,1)}, bf16[2,256,256]{2,1,0:T(8,128)(2,1)}) custom-call(bf16[512,2048]{1,0:T(8,128)(2,1)} %all-gather.12.cloned.1.call-done.value_ref.refs_0_, ...), custom_call_target="tpu_custom_call" | custom-call | flops 3449999872 | bytes 1 | tf_op jit(solution)/shard_map/weight_grads/pallas_call | solution.py:603
  331.3 9.4 %collective-permute-done.37.refs_3_ = bf16[256,512]{1,0:T(8,128)(2,1)} collective-permute-done((bf16[256,512]{1,0:T(8,128)(2,1)S(1)}, bf16[256,512]{1,0:T(8,128)(2,1)}, u32[]{:S(2)}, u32[]{:S(2)}) %collective-permute-start.37) | collective-permute-done | bytes 262176 | tf_op jit(solution)/shard_map/ppermute | solution.py:42
  342.9 7.3 %project_back.1 = (bf16[512,2048]{1,0:T(8,128)(2,1)}, f32[2,2048]{1,0:T(2,128)}) custom-call(bf16[512,256]{1,0:T(8,128)(2,1)} %get-tuple-element.197.refs_3_.query_ref, bf16[2,512,256]{2,1,0:T(8,128)(2,1)} %add_convert_fusion.4.pair_ref.refs_1_, bf16[512,2048]{1,0:T(8,128)(2,1)} %all-gather.6.cloned.1.call-done.tokens_ref, ...), custom_call_target="tpu_custom_call" | custom-call | flops 1 | bytes 1 | tf_op jit(solution)/shard_map/project_back/pallas_call | solution.py:530
  370.1 7.4 %adam.4 = (f32[2048,256]{1,0:T(8,128)}, f32[2048,256]{1,0:T(8,128)}, f32[2048,256]{1,0:T(8,128)}, bf16[2048,256]{1,0:T(8,128)(2,1)}) custom-call(s32[1]{0:T(128)} %bitcast.at_ref, bf16[256,512]{1,0:T(8,128)(2,1)} %get-tuple-element.212.refs_0_, bf16[256,512]{1,0:T(8,128)(2,1)} %collective-permute-done.35.refs_1_, ...), custom_call_target="tpu_custom_call" | custom-call | flops 8049999872 | bytes 1 | tf_op jit(solution)/shard_map/adam/pallas_call | solution.py:845
  383.8 13.7 %collective-permute-done.55.refs_3_ = bf16[256,512]{1,0:T(8,128)(2,1)} collective-permute-done((bf16[256,512]{1,0:T(8,128)(2,1)S(1)}, bf16[256,512]{1,0:T(8,128)(2,1)}, u32[]{:S(2)}, u32[]{:S(2)}) %collective-permute-start.55) | collective-permute-done | bytes 262176 | tf_op jit(solution)/shard_map/ppermute | solution.py:42
  397.5 7.4 %adam.5 = (f32[256,2048]{1,0:T(8,128)}, f32[256,2048]{1,0:T(8,128)}, f32[256,2048]{1,0:T(8,128)}, bf16[256,2048]{1,0:T(8,128)(2,1)}) custom-call(s32[1]{0:T(128)} %bitcast.at_ref, bf16[256,512]{1,0:T(8,128)(2,1)} %get-tuple-element.222.refs_0_, bf16[256,512]{1,0:T(8,128)(2,1)} %collective-permute-done.53.refs_1_, ...), custom_call_target="tpu_custom_call" | custom-call | flops 8049999872 | bytes 1 | tf_op jit(solution)/shard_map/adam/pallas_call | solution.py:845
  405.2 4.7 %reduce-scatter.11.cloned.1.call-done = bf16[64,2048]{1,0:T(8,128)(2,1)} async-done(((bf16[512,2048]{1,0:T(8,128)(2,1)}), bf16[64,2048]{1,0:T(8,128)(2,1)}) %reduce-scatter.11.cloned.1.call-update) | async-done | bytes 262160 | tf_op jit(solution)/shard_map/reduce_scatter | solution.py:191
  424.1 11.9 %collective-permute-done.58.refs_7_ = bf16[272,256]{1,0:T(8,128)(2,1)S(1)} collective-permute-done((bf16[272,256]{1,0:T(8,128)(2,1)S(1)}, bf16[272,256]{1,0:T(8,128)(2,1)S(1)}, u32[]{:S(2)}, u32[]{:S(2)}) %collective-permute-start.58) | collective-permute-done | bytes 139296 | tf_op jit(solution)/shard_map/ppermute | solution.py:42
  449.4 6.1 %adam.6 = (f32[3,256,512]{2,1,0:T(8,128)}, f32[3,256,512]{2,1,0:T(8,128)}, f32[3,256,512]{2,1,0:T(8,128)}, bf16[3,256,512]{2,1,0:T(8,128)(2,1)}) custom-call(s32[1]{0:T(128)} %bitcast.at_ref, bf16[256,256]{1,0:T(8,128)(2,1)} %get-tuple-element.269.refs_0_, bf16[256,256]{1,0:T(8,128)(2,1)} %copy-done.65, bf16[256,256]{1,0:T(8,128)(2,1)} %copy-done.66, ...), custom_call_target="tpu_custom_call" | custom-call | flops 8049999872 | bytes 1 | tf_op jit(solution)/shard_map/adam/pallas_call | solution.py:845
  (387 shorter events, 180.5 us)
Async XLA Ops:
  7.2 68.7 %all-gather.6.cloned.1.call-start = ((), (), s32[]{:S(2)}) async-start(), calls=%async_computation.4 | async-start | bytes 2359296 | tf_op jit(solution)/shard_map/all_gather | solution.py:185
  14.0 24.1 %collective-permute-start.2 = (bf16[272,512]{1,0:T(8,128)(2,1)}, bf16[272,512]{1,0:T(8,128)(2,1)S(1)}, u32[]{:S(2)}, u32[]{:S(2)}) collective-permute-start(bf16[272,512]{1,0:T(8,128)(2,1)} %get-tuple-element.137), channel_id=1, source_target_pairs={{0,24},{4,28},{8,16},{12,20},{16,8},{20,12},{24,0},{28,4},{1,25},{... | collective-permute-start | bytes 835592 | tf_op jit(solution)/shard_map/ppermute | solution.py:42
  38.1 83.0 %all-gather.8.cloned.1.call-start = ((), (), s32[]{:S(2)}) async-start(), calls=%async_computation.5 | async-start | bytes 2359296 | tf_op jit(solution)/shard_map/all_gather | solution.py:185
  48.0 122.0 %reduce-scatter.5.cloned.1.call-start = ((), (), s32[]{:S(2)}) async-start(), calls=%async_computation.6 | async-start | bytes 2359296 | tf_op jit(solution)/shard_map/reduce_scatter | solution.py:191
  52.8 22.1 %collective-permute-start.4 = (bf16[256,512]{1,0:T(8,128)(2,1)}, bf16[256,512]{1,0:T(8,128)(2,1)}, u32[]{:S(2)}, u32[]{:S(2)}) collective-permute-start(bf16[256,512]{1,0:T(8,128)(2,1)} %get-tuple-element.141), channel_id=1, source_target_pairs={{0,8},{4,12},{8,0},{12,4},{16,24},{20,28},{24,16},{28,20},{1,9},{5... | collective-permute-start | bytes 786440 | tf_op jit(solution)/shard_map/ppermute | solution.py:42
  98.3 21.1 %collective-permute-start.15 = (bf16[256,512]{1,0:T(8,128)(2,1)}, bf16[256,512]{1,0:T(8,128)(2,1)S(1)}, u32[]{:S(2)}, u32[]{:S(2)}) collective-permute-start(bf16[256,512]{1,0:T(8,128)(2,1)} %get-tuple-element.157), channel_id=1, source_target_pairs={{0,16},{4,20},{8,24},{12,28},{16,0},{20,4},{24,8},{28,12},{1,17},{... | collective-permute-start | bytes 786440 | tf_op jit(solution)/shard_map/ppermute | solution.py:42
  125.0 83.3 %all-gather.10.cloned.1.call-start = ((), (), s32[]{:S(2)}) async-start(), calls=%async_computation.7 | async-start | bytes 2359296 | tf_op jit(solution)/shard_map/all_gather | solution.py:185
  141.3 34.8 %collective-permute-start.19 = (bf16[4,256,512]{2,1,0:T(8,128)(2,1)}, bf16[4,256,512]{2,1,0:T(8,128)(2,1)S(1)}, u32[]{:S(2)}, u32[]{:S(2)}) collective-permute-start(bf16[4,256,512]{2,1,0:T(8,128)(2,1)} %assemble.5.refs_0_), channel_id=1, source_target_pairs={{0,4},{4,0},{8,12},{12,8},{16,20},{20,16},{24,28},{28,24},{1,5},{5... | collective-permute-start | bytes 3145736 | tf_op jit(solution)/shard_map/ppermute | solution.py:42
  142.8 32.7 %collective-permute-start.20 = (bf16[4,256,512]{2,1,0:T(8,128)(2,1)}, bf16[4,256,512]{2,1,0:T(8,128)(2,1)S(1)}, u32[]{:S(2)}, u32[]{:S(2)}) collective-permute-start(bf16[4,256,512]{2,1,0:T(8,128)(2,1)} %assemble.5.refs_0_), channel_id=1, source_target_pairs={{0,2},{1,3},{2,0},{3,1},{4,6},{5,7},{6,4},{7,5},{8,10},{9,11},{10,... | collective-permute-start | bytes 3145736 | tf_op jit(solution)/shard_map/ppermute | solution.py:42
  175.2 73.1 %reduce-scatter.7.cloned.1.call-start = ((), (), s32[]{:S(2)}) async-start(), calls=%async_computation.8 | async-start | bytes 2359296 | tf_op jit(solution)/shard_map/reduce_scatter | solution.py:191
  178.3 18.7 %collective-permute-start.23 = (bf16[2,256,512]{2,1,0:T(8,128)(2,1)}, bf16[2,256,512]{2,1,0:T(8,128)(2,1)}, u32[]{:S(2)}, u32[]{:S(2)}) collective-permute-start(bf16[2,256,512]{2,1,0:T(8,128)(2,1)} %slice.186), channel_id=1, source_target_pairs={{0,4},{4,0},{8,12},{12,8},{16,20},{20,16},{24,28},{28,24},{1,5},{5... | collective-permute-start | bytes 1572872 | tf_op jit(solution)/shard_map/ppermute | solution.py:42
  218.1 67.5 %all-gather.12.cloned.1.call-start = ((), (), s32[]{:S(2)}) async-start(), calls=%async_computation.10 | async-start | bytes 2359296 | tf_op jit(solution)/shard_map/all_gather | solution.py:185
  252.3 73.5 %reduce-scatter.9.cloned.1.call-start = ((), (), s32[]{:S(2)}) async-start(), calls=%async_computation.9 | async-start | bytes 2359296 | tf_op jit(solution)/shard_map/reduce_scatter | solution.py:191
  252.4 23.0 %collective-permute-start.27 = (bf16[4,256,512]{2,1,0:T(8,128)(2,1)S(1)}, bf16[4,256,512]{2,1,0:T(8,128)(2,1)S(1)}, u32[]{:S(2)}, u32[]{:S(2)}) collective-permute-start(bf16[4,256,512]{2,1,0:T(8,128)(2,1)S(1)} %pad_maximum_fusion), channel_id=1, source_target_pairs={{0,2},{1,3},{2,0},{3,1},{4,6},{5,7},{6,4},{7,5},{8,10},{9,11},{10,... | collective-permute-start | bytes 3145736 | tf_op jit(solution)/shard_map/ppermute | solution.py:42
  253.1 22.4 %collective-permute-start.28 = (bf16[4,256,512]{2,1,0:T(8,128)(2,1)}, bf16[4,256,512]{2,1,0:T(8,128)(2,1)}, u32[]{:S(2)}, u32[]{:S(2)}) collective-permute-start(bf16[4,256,512]{2,1,0:T(8,128)(2,1)} %pad_maximum_fusion.1), channel_id=1, source_target_pairs={{0,4},{4,0},{8,12},{12,8},{16,20},{20,16},{24,28},{28,24},{1,5},{5... | collective-permute-start | bytes 3145736 | tf_op jit(solution)/shard_map/ppermute | solution.py:42
  260.3 149.6 %reduce-scatter.11.cloned.1.call-start = ((), (), s32[]{:S(2)}) async-start(), calls=%async_computation.12 | async-start | bytes 2359296 | tf_op jit(solution)/shard_map/reduce_scatter | solution.py:191
  290.7 24.0 %collective-permute-start.30 = (bf16[4,256,512]{2,1,0:T(8,128)(2,1)S(1)}, bf16[4,256,512]{2,1,0:T(8,128)(2,1)}, u32[]{:S(2)}, u32[]{:S(2)}) collective-permute-start(bf16[4,256,512]{2,1,0:T(8,128)(2,1)S(1)} %pad_maximum_fusion.2), channel_id=1, source_target_pairs={{0,2},{1,3},{2,0},{3,1},{4,6},{5,7},{6,4},{7,5},{8,10},{9,11},{10,... | collective-permute-start | bytes 3145736 | tf_op jit(solution)/shard_map/ppermute | solution.py:42
  294.2 23.8 %collective-permute-start.32 = (bf16[4,256,512]{2,1,0:T(8,128)(2,1)}, bf16[4,256,512]{2,1,0:T(8,128)(2,1)}, u32[]{:S(2)}, u32[]{:S(2)}) collective-permute-start(bf16[4,256,512]{2,1,0:T(8,128)(2,1)} %pad_maximum_fusion.3), channel_id=1, source_target_pairs={{0,4},{4,0},{8,12},{12,8},{16,20},{20,16},{24,28},{28,24},{1,5},{5... | collective-permute-start | bytes 3145736 | tf_op jit(solution)/shard_map/ppermute | solution.py:42
  306.7 24.6 %collective-permute-start.35 = (bf16[256,512]{1,0:T(8,128)(2,1)}, bf16[256,512]{1,0:T(8,128)(2,1)}, u32[]{:S(2)}, u32[]{:S(2)}) collective-permute-start(bf16[256,512]{1,0:T(8,128)(2,1)} %get-tuple-element.261), channel_id=1, source_target_pairs={{0,8},{4,12},{8,0},{12,4},{16,24},{20,28},{24,16},{28,20},{1,9},{5... | collective-permute-start | bytes 786440 | tf_op jit(solution)/shard_map/ppermute | solution.py:42
  307.0 24.3 %collective-permute-start.36 = (bf16[256,512]{1,0:T(8,128)(2,1)}, bf16[256,512]{1,0:T(8,128)(2,1)}, u32[]{:S(2)}, u32[]{:S(2)}) collective-permute-start(bf16[256,512]{1,0:T(8,128)(2,1)} %get-tuple-element.260), channel_id=1, source_target_pairs={{0,16},{4,20},{8,24},{12,28},{16,0},{20,4},{24,8},{28,12},{1,17},{... | collective-permute-start | bytes 786440 | tf_op jit(solution)/shard_map/ppermute | solution.py:42
  314.3 26.4 %collective-permute-start.37 = (bf16[256,512]{1,0:T(8,128)(2,1)S(1)}, bf16[256,512]{1,0:T(8,128)(2,1)}, u32[]{:S(2)}, u32[]{:S(2)}) collective-permute-start(bf16[256,512]{1,0:T(8,128)(2,1)S(1)} %get-tuple-element.259), channel_id=1, source_target_pairs={{0,24},{4,28},{8,16},{12,20},{16,8},{20,12},{24,0},{28,4},{1,25},{... | collective-permute-start | bytes 786440 | tf_op jit(solution)/shard_map/ppermute | solution.py:42
  350.2 96.3 %all-gather.14.cloned.1.call-start = ((), (), s32[]{:S(2)}) async-start(), calls=%async_computation.11 | async-start | bytes 1310720 | tf_op jit(solution)/shard_map/all_gather | solution.py:1044
  357.3 24.7 %collective-permute-start.53 = (bf16[256,512]{1,0:T(8,128)(2,1)}, bf16[256,512]{1,0:T(8,128)(2,1)}, u32[]{:S(2)}, u32[]{:S(2)}) collective-permute-start(bf16[256,512]{1,0:T(8,128)(2,1)} %get-tuple-element.256), channel_id=1, source_target_pairs={{0,8},{4,12},{8,0},{12,4},{16,24},{20,28},{24,16},{28,20},{1,9},{5... | collective-permute-start | bytes 786440 | tf_op jit(solution)/shard_map/ppermute | solution.py:42
  361.8 21.7 %collective-permute-start.54 = (bf16[256,512]{1,0:T(8,128)(2,1)}, bf16[256,512]{1,0:T(8,128)(2,1)}, u32[]{:S(2)}, u32[]{:S(2)}) collective-permute-start(bf16[256,512]{1,0:T(8,128)(2,1)} %get-tuple-element.255), channel_id=1, source_target_pairs={{0,16},{4,20},{8,24},{12,28},{16,0},{20,4},{24,8},{28,12},{1,17},{... | collective-permute-start | bytes 786440 | tf_op jit(solution)/shard_map/ppermute | solution.py:42
  362.7 34.8 %collective-permute-start.55 = (bf16[256,512]{1,0:T(8,128)(2,1)S(1)}, bf16[256,512]{1,0:T(8,128)(2,1)}, u32[]{:S(2)}, u32[]{:S(2)}) collective-permute-start(bf16[256,512]{1,0:T(8,128)(2,1)S(1)} %get-tuple-element.254), channel_id=1, source_target_pairs={{0,24},{4,28},{8,16},{12,20},{16,8},{20,12},{24,0},{28,4},{1,25},{... | collective-permute-start | bytes 786440 | tf_op jit(solution)/shard_map/ppermute | solution.py:42
  380.4 37.4 %collective-permute-start.45 = (bf16[4,256,256]{2,1,0:T(8,128)(2,1)}, bf16[4,256,256]{2,1,0:T(8,128)(2,1)}, u32[]{:S(2)}, u32[]{:S(2)}) collective-permute-start(bf16[4,256,256]{2,1,0:T(8,128)(2,1)} %pad_maximum_fusion.11), channel_id=1, source_target_pairs={{0,4},{4,0},{8,12},{12,8},{16,20},{20,16},{24,28},{28,24},{1,5},{5... | collective-permute-start | bytes 1572872 | tf_op jit(solution)/shard_map/ppermute | solution.py:42
  381.6 36.1 %collective-permute-start.43 = (bf16[4,256,256]{2,1,0:T(8,128)(2,1)}, bf16[4,256,256]{2,1,0:T(8,128)(2,1)}, u32[]{:S(2)}, u32[]{:S(2)}) collective-permute-start(bf16[4,256,256]{2,1,0:T(8,128)(2,1)} %pad_maximum_fusion.10), channel_id=1, source_target_pairs={{0,2},{1,3},{2,0},{3,1},{4,6},{5,7},{6,4},{7,5},{8,10},{9,11},{10,... | collective-permute-start | bytes 1572872 | tf_op jit(solution)/shard_map/ppermute | solution.py:42
  382.0 23.0 %collective-permute-start.52 = (bf16[4,272,256]{2,1,0:T(8,128)(2,1)S(1)}, bf16[4,272,256]{2,1,0:T(8,128)(2,1)S(1)}, u32[]{:S(2)}, u32[]{:S(2)}) collective-permute-start(bf16[4,272,256]{2,1,0:T(8,128)(2,1)S(1)} %pad_maximum_fusion.6), channel_id=1, source_target_pairs={{0,4},{4,0},{8,12},{12,8},{16,20},{20,16},{24,28},{28,24},{1,5},{5... | collective-permute-start | bytes 1671176 | tf_op jit(solution)/shard_map/ppermute | solution.py:42
  383.5 21.5 %collective-permute-start.51 = (bf16[4,272,256]{2,1,0:T(8,128)(2,1)S(1)}, bf16[4,272,256]{2,1,0:T(8,128)(2,1)S(1)}, u32[]{:S(2)}, u32[]{:S(2)}) collective-permute-start(bf16[4,272,256]{2,1,0:T(8,128)(2,1)S(1)} %pad_maximum_fusion.5), channel_id=1, source_target_pairs={{0,2},{1,3},{2,0},{3,1},{4,6},{5,7},{6,4},{7,5},{8,10},{9,11},{10,... | collective-permute-start | bytes 1671176 | tf_op jit(solution)/shard_map/ppermute | solution.py:42
  415.5 20.5 %collective-permute-start.58 = (bf16[272,256]{1,0:T(8,128)(2,1)S(1)}, bf16[272,256]{1,0:T(8,128)(2,1)S(1)}, u32[]{:S(2)}, u32[]{:S(2)}) collective-permute-start(bf16[272,256]{1,0:T(8,128)(2,1)S(1)} %get-tuple-element.262), channel_id=1, source_target_pairs={{0,24},{4,28},{8,16},{12,20},{16,8},{20,12},{24,0},{28,4},{1,25},{... | collective-permute-start | bytes 417800 | tf_op jit(solution)/shard_map/ppermute | solution.py:42
  421.1 20.5 %collective-permute-start.50 = (bf16[256,256]{1,0:T(8,128)(2,1)S(1)}, bf16[256,256]{1,0:T(8,128)(2,1)S(1)}, u32[]{:S(2)}, u32[]{:S(2)}) collective-permute-start(bf16[256,256]{1,0:T(8,128)(2,1)S(1)} %get-tuple-element.266), channel_id=1, source_target_pairs={{0,24},{4,28},{8,16},{12,20},{16,8},{20,12},{24,0},{28,4},{1,25},{... | collective-permute-start | bytes 393224 | tf_op jit(solution)/shard_map/ppermute | solution.py:42
  422.6 25.6 %collective-permute-start.40 = (bf16[64,2048]{1,0:T(8,128)(2,1)S(1)}, bf16[64,2048]{1,0:T(8,128)(2,1)S(1)}, u32[]{:S(2)}, u32[]{:S(2)}) collective-permute-start(bf16[64,2048]{1,0:T(8,128)(2,1)S(1)} %reshape.174), channel_id=1, source_target_pairs={{0,2},{1,3},{2,0},{3,1},{4,6},{5,7},{6,4},{7,5},{8,10},{9,11},{10,... | collective-permute-start | bytes 786440 | tf_op jit(solution)/shard_map/ppermute | solution.py:42
  (106 other events, 1077.7 us)
Sparse Core Ops, SparseCore 0:
  38.2 36.4 all-gather.5
  76.9 34.6 all-gather.7
  125.1 44.7 reduce-scatter.4
  175.3 33.0 all-gather.9
  218.2 29.9 reduce-scatter.6
  252.5 33.0 all-gather.11
  288.4 31.5 reduce-scatter.8
  350.3 59.4 reduce-scatter.10
  411.4 16.3 all-gather.13

commit v5 on v4

--- a/solution.py
+++ b/solution.py
@@ -745,7 +745,7 @@
         ],
         scratch_shapes=[pltpu.VMEM((length, 2 * head), BF16)],
         compiler_params=PARAMS,
-        cost_estimate=SMALL,
+        cost_estimate=cost(8),
         name="attend",
     )(queries, query_marks, key_marks, *arrays)
 
@@ -961,7 +961,7 @@
     group_tokens = gather_tokens(after(own_tokens, own_cotangent, *first_parts[1:]))
     (first_own,) = assemble(at_word, [after(first_parts[0], own_cotangent)] + first_parts[1:])
     low = gather_groups(first_own)
-    expand_parts = exchange(expand_packed, first_parts[1:])
+    expand_parts = exchange(expand_packed, None)
     group_cotangent = gather_tokens(after(own_cotangent, expand_parts[2]))
     reduce_parts = exchange(reduce_packed, expand_parts[1:])
 
@@ -1075,7 +1075,7 @@
         "plain",
         [([after(expand_shares[0], *pair_sent)] + expand_shares[1:], 0, units)],
     )
-    query_shares = shares(after(query_sum, *pair_sent))
+    query_shares = shares(query_sum)
     pair_shares = shares(after(pair_sum, expand_new[0], natural_grad))
     share_norm = sum(part[shard : shard + 4, :shard].astype(F32) for part in pair_shares)
     share_norm = share_norm + over_c(share_norm)

time: 475 us -> 475 us (level)
  waiting for transfers between devices: 188 us -> 181 us
  starting transfers between devices: 73.9 us -> 79.1 us
    reduce_scatter x4, waiting for transfers between devices: 39.4 us -> 24.3 us  [scatter_tokens(): lax.psum_scatter(partial_sums, ('fsdp', 'mp'), axis_index_groups=token_gr...]
    ppermute x61, waiting for transfers between devices: 131 us -> 145 us  [swap(): return lax.ppermute(value, axis, [(i, i ^ mask) for i in range(size)])]
    all_gather x4, waiting for transfers between devices: 17.8 us -> 11.8 us  [gather_tokens(): lax.all_gather(own, ('fsdp', 'mp'), axis_index_groups=token_groups(), axi...]
    ppermute x61, starting transfers between devices: 72.9 us -> 78.1 us  [swap(): return lax.ppermute(value, axis, [(i, i ^ mask) for i in range(size)])]
  transfers between devices with their start and end apart: 70 -> 70, of which waited for: 31 -> 33; matrix products, arithmetic and copies ran while one was open for 10% -> 10% of each run, Pallas kernels for 22% -> 22%
where the time goes in v5:
time: 475 us; the launch traced here: 465 us
  waiting for transfers between devices  181 us (38%)
  Pallas kernels  126 us (27%)
  starting transfers between devices  79.1 us (17%)
  other arithmetic  36.5 us (8%)
  local copies, waits for them, and re-layouts  27 us (6%)
  between operations  15.3 us (3%)
    ppermute x61, waiting for transfers between devices, swap(): return lax.ppermute(value, axis, [(i, i ^ mask) for i in range(size)])  145 us
    ppermute x61, starting transfers between devices, swap(): return lax.ppermute(value, axis, [(i, i ^ mask) for i in range(size)])  78.1 us
    pallas_call x4, Pallas kernels, adam(): pl.pallas_call(partial(adam_kernel, rate, shape, columns), grid_spec=pltp...  25.2 us
    reduce_scatter x4, waiting for transfers between devices, scatter_tokens(): lax.psum_scatter(partial_sums, ('fsdp', 'mp'), axis_index_groups=token_gr...  24.3 us
    pallas_call x4, Pallas kernels, weight_grads(): pl.pallas_call(partial(grads_kernel, groups, len(pairs), extra), grid=(gr...  22.8 us
    convert_element_type x15, other arithmetic, add(): return total.astype(BF16)  13.3 us
    all_gather x4, waiting for transfers between devices, gather_tokens(): lax.all_gather(own, ('fsdp', 'mp'), axis_index_groups=token_groups(), axi...  11.8 us
    pallas_call x1, Pallas kernels, attend_back(): pl.pallas_call(partial(attend_back_kernel, scaling, layout), grid=(2, cou...  10.4 us
  transfers between devices with their start and end apart: 70, of which 33 were waited for; matrix products, arithmetic and copies ran while one was open for 10% of the time, Pallas kernels for 22%

profile of v5, /device:TPU:9, one launch (start us, length us, event | category | flops | bytes accessed | tf_op | source)
XLA Modules:
  0.0 465.2 jit_solution(11805959419328753802)
XLA Ops:
  26.3 11.8 %collective-permute-done.2.refs_3_ = bf16[272,512]{1,0:T(8,128)(2,1)S(1)} collective-permute-done((bf16[272,512]{1,0:T(8,128)(2,1)}, bf16[272,512]{1,0:T(8,128)(2,1)S(1)}, u32[]{:S(2)}, u32[]{:S(2)}) %collective-permute-start.2) | collective-permute-done | bytes 278560 | tf_op jit(solution)/shard_map/ppermute | solution.py:42
  42.4 5.6 %collective-permute-done.5.refs_2_ = bf16[256,512]{1,0:T(8,128)(2,1)} collective-permute-done((bf16[256,512]{1,0:T(8,128)(2,1)S(1)}, bf16[256,512]{1,0:T(8,128)(2,1)}, u32[]{:S(2)}, u32[]{:S(2)}) %collective-permute-start.5) | collective-permute-done | bytes 262176 | tf_op jit(solution)/shard_map/ppermute | solution.py:42
  49.3 5.4 %collective-permute-start.4 = (bf16[256,512]{1,0:T(8,128)(2,1)}, bf16[256,512]{1,0:T(8,128)(2,1)}, u32[]{:S(2)}, u32[]{:S(2)}) collective-permute-start(bf16[256,512]{1,0:T(8,128)(2,1)} %get-tuple-element.136), channel_id=1, source_target_pairs={{0,8},{4,12},{8,0},{12,4},{16,24},{20,28},{24,16},{28,20},{1,9},{5... | collective-permute-start | bytes 786440 | tf_op jit(solution)/shard_map/ppermute | solution.py:42
  55.6 10.1 %collective-permute-done.3.refs_1_ = bf16[4,272,512]{2,1,0:T(8,128)(2,1)S(1)} collective-permute-done((bf16[4,272,512]{2,1,0:T(8,128)(2,1)}, bf16[4,272,512]{2,1,0:T(8,128)(2,1)S(1)}, u32[]{:S(2)}, u32[]{:S(2)}) %collective-permute-start.3) | collective-permute-done | bytes 1114144 | tf_op jit(solution)/shard_map/ppermute | solution.py:42
  80.8 6.7 %project.1 = (bf16[512,2048]{1,0:T(8,128)(2,1)}, bf16[512,256]{1,0:T(8,128)(2,1)}, bf16[2,512,256]{2,1,0:T(8,128)(2,1)}) custom-call(bf16[512,2048]{1,0:T(8,128)(2,1)} %all-gather.6.cloned.1.call-done.tokens_ref, f32[4,2048]{1,0:T(4,128)} %bitcast.110, bf16[4,272,512]{2,1,0:T(8,128)(2,1)} %assemble.3.refs_0_, bf16[4,272,512]{2,1,0:T(8,128)(2,1)} %copy-done, ...), custom_call_target="tpu_custom_call" | custom-call | flops 1 | bytes 1 | tf_op jit(solution)/shard_map/project/pallas_call | solution.py:399
  89.9 5.4 %collective-permute-start.10 = (bf16[256,512]{1,0:T(8,128)(2,1)}, bf16[256,512]{1,0:T(8,128)(2,1)S(1)}, u32[]{:S(2)}, u32[]{:S(2)}) collective-permute-start(bf16[256,512]{1,0:T(8,128)(2,1)} %get-tuple-element.142), channel_id=1, source_target_pairs={{0,8},{4,12},{8,0},{12,4},{16,24},{20,28},{24,16},{28,20},{1,9},{5... | collective-permute-start | bytes 786440 | tf_op jit(solution)/shard_map/ppermute | solution.py:42
  98.9 5.5 %collective-permute-start.15 = (bf16[256,512]{1,0:T(8,128)(2,1)}, bf16[256,512]{1,0:T(8,128)(2,1)S(1)}, u32[]{:S(2)}, u32[]{:S(2)}) collective-permute-start(bf16[256,512]{1,0:T(8,128)(2,1)} %get-tuple-element.150), channel_id=1, source_target_pairs={{0,16},{4,20},{8,24},{12,28},{16,0},{20,4},{24,8},{28,12},{1,17},{... | collective-permute-start | bytes 786440 | tf_op jit(solution)/shard_map/ppermute | solution.py:42
  110.3 9.3 %attend.1 = (f32[512,256]{1,0:T(8,128)}, bf16[512,256]{1,0:T(8,128)(2,1)}, f32[2,512,1]{2,1,0:T(8,128)}) custom-call(bf16[512,256]{1,0:T(8,128)(2,1)} %get-tuple-element.143.q_ref, s32[512,2]{1,0:T(8,128)} %bitcast.104, s32[2,2048]{1,0:T(2,128)} %reshape.168.km_ref, bf16[2,512,256]{2,1,0:T(8,128)(2,1)} %get-tuple-element.144.refs_0_, ...), custom_call_target="tpu_custom_call" | custom-call | flops 9200000000 | bytes 1 | tf_op jit(solution)/shard_map/attend/pallas_call | solution.py:727
  119.6 10.8 %collective-permute-done.16.refs_3_ = bf16[256,512]{1,0:T(8,128)(2,1)S(1)} collective-permute-done((bf16[256,512]{1,0:T(8,128)(2,1)}, bf16[256,512]{1,0:T(8,128)(2,1)S(1)}, u32[]{:S(2)}, u32[]{:S(2)}) %collective-permute-start.16) | collective-permute-done | bytes 262176 | tf_op jit(solution)/shard_map/ppermute | solution.py:42
  141.8 15.2 %collective-permute-done.17.refs_2_ = bf16[4,256,512]{2,1,0:T(8,128)(2,1)S(1)} collective-permute-done((bf16[4,256,512]{2,1,0:T(8,128)(2,1)S(1)}, bf16[4,256,512]{2,1,0:T(8,128)(2,1)S(1)}, u32[]{:S(2)}, u32[]{:S(2)}) %collective-permute-start.17) | collective-permute-done | bytes 1048608 | tf_op jit(solution)/shard_map/ppermute | solution.py:42
  159.8 8.8 %reduce-scatter.5.cloned.1.call-done = bf16[64,2048]{1,0:T(8,128)(2,1)} async-done(((bf16[512,2048]{1,0:T(8,128)(2,1)}), bf16[64,2048]{1,0:T(8,128)(2,1)}) %reduce-scatter.5.cloned.1.call-update) | async-done | bytes 262160 | tf_op jit(solution)/shard_map/reduce_scatter | solution.py:191
  183.4 8.0 %collective-permute-done.21.refs_3_ = bf16[2,256,512]{2,1,0:T(8,128)(2,1)S(1)} collective-permute-done((bf16[2,256,512]{2,1,0:T(8,128)(2,1)S(1)}, bf16[2,256,512]{2,1,0:T(8,128)(2,1)S(1)}, u32[]{:S(2)}, u32[]{:S(2)}) %collective-permute-start.21) | collective-permute-done | bytes 524320 | tf_op jit(solution)/shard_map/ppermute | solution.py:42
  192.2 6.0 %to_units.2.pull_ref = f32[512,1024]{1,0:T(8,128)} custom-call(bf16[512,2048]{1,0:T(8,128)(2,1)} %all-gather.8.cloned.1.call-done.value_ref.refs_0_, bf16[4,256,512]{2,1,0:T(8,128)(2,1)} %assemble.5.refs_0_, bf16[4,256,512]{2,1,0:T(8,128)(2,1)} %copy-done.5, bf16[4,256,512]{2,1,0:T(8,128)(2,1)} %copy-done.6, bf16[2,256,512]{2,1,0:T(8,128)(2,1)} %copy-done.24, ...), custom_call_target="tpu_custom_call" | custom-call | flops 28750000128 | bytes 1 | tf_op jit(solution)/shard_map/to_units/pallas_call | solution.py:430
  206.8 9.7 %feed_forward.1 = (bf16[512,1024]{1,0:T(8,128)(2,1)}, bf16[512,1024]{1,0:T(8,128)(2,1)}, bf16[512,2048]{1,0:T(8,128)(2,1)}) custom-call(bf16[512,2048]{1,0:T(8,128)(2,1)} %all-gather.10.cloned.1.call-done.value_ref.refs_0_, f32[512,1024]{1,0:T(8,128)} %to_units.2.pull_ref, bf16[4,256,512]{2,1,0:T(8,128)(2,1)} %assemble.4.refs_0_, ...), custom_call_target="tpu_custom_call" | custom-call | flops 1 | bytes 1 | tf_op jit(solution)/shard_map/feed_forward/pallas_call | solution.py:493
  216.6 6.2 %weight_grads.4 = (bf16[4,256,512]{2,1,0:T(8,128)(2,1)}, bf16[4,256,512]{2,1,0:T(8,128)(2,1)}, bf16[4,256,512]{2,1,0:T(8,128)(2,1)}, bf16[2,256,512]{2,1,0:T(8,128)(2,1)}, bf16[2,256,512]{2,1,0:T(8,128)(2,1)}) custom-call(bf16[512,2048]{1,0:T(8,128)(2,1)} %all-gather.8.cloned.1.call-done.value_ref.refs_0_, bf16[512,1024]{1,0:T(8,128)(2,1)} %get-tuple-element.165.refs_1_.value_ref), custom_call_target="tpu_custom_call" | custom-call | flops 3449999872 | bytes 1 | tf_op jit(solution)/shard_map/weight_grads/pallas_call | solution.py:603
  227.4 6.5 %collective-permute-done.25 = bf16[2,256,512]{2,1,0:T(8,128)(2,1)S(1)} collective-permute-done((bf16[2,256,512]{2,1,0:T(8,128)(2,1)}, bf16[2,256,512]{2,1,0:T(8,128)(2,1)S(1)}, u32[]{:S(2)}, u32[]{:S(2)}) %collective-permute-start.25) | collective-permute-done | bytes 524320 | tf_op jit(solution)/shard_map/ppermute | solution.py:42
  236.5 10.9 %reduce-scatter.7.cloned.1.call-done = bf16[64,2048]{1,0:T(8,128)(2,1)} async-done(((bf16[512,2048]{1,0:T(8,128)(2,1)}), bf16[64,2048]{1,0:T(8,128)(2,1)}) %reduce-scatter.7.cloned.1.call-update) | async-done | bytes 262160 | tf_op jit(solution)/shard_map/reduce_scatter | solution.py:191
  253.4 5.9 %to_features.3 = bf16[512,2048]{1,0:T(8,128)(2,1)} custom-call(bf16[512,1024]{1,0:T(8,128)(2,1)} %get-tuple-element.165.refs_1_.value_ref, bf16[4,256,512]{2,1,0:T(8,128)(2,1)} %assemble.5.refs_0_, bf16[4,256,512]{2,1,0:T(8,128)(2,1)} %copy-done.5, bf16[4,256,512]{2,1,0:T(8,128)(2,1)} %copy-done.6, bf16[2,256,512]{2,1,0:T(8,128)(2,1)} %copy-done.24, ...), custom_call_target="tpu_custom_call" | custom-call | flops 1 | bytes 1 | tf_op jit(solution)/shard_map/to_features/pallas_call | solution.py:455
  259.8 6.2 %weight_grads.5 = (bf16[4,256,512]{2,1,0:T(8,128)(2,1)}, bf16[4,256,512]{2,1,0:T(8,128)(2,1)}, bf16[4,256,512]{2,1,0:T(8,128)(2,1)}, bf16[2,256,512]{2,1,0:T(8,128)(2,1)}, bf16[2,256,512]{2,1,0:T(8,128)(2,1)}) custom-call(bf16[512,2048]{1,0:T(8,128)(2,1)} %all-gather.10.cloned.1.call-done.value_ref.refs_0_, bf16[512,1024]{1,0:T(8,128)(2,1)} %get-tuple-element.172.refs_1_), custom_call_target="tpu_custom_call" | custom-call | flops 3449999872 | bytes 1 | tf_op jit(solution)/shard_map/weight_grads/pallas_call | solution.py:603
  266.0 8.6 %collective-permute-done.27 = bf16[4,256,512]{2,1,0:T(8,128)(2,1)S(1)} collective-permute-done((bf16[4,256,512]{2,1,0:T(8,128)(2,1)S(1)}, bf16[4,256,512]{2,1,0:T(8,128)(2,1)S(1)}, u32[]{:S(2)}, u32[]{:S(2)}) %collective-permute-start.27) | collective-permute-done | bytes 1048608 | tf_op jit(solution)/shard_map/ppermute | solution.py:42
  278.4 6.3 %all-gather.12.cloned.1.call-done.value_ref.refs_0_ = bf16[512,2048]{1,0:T(8,128)(2,1)} async-done(((bf16[64,2048]{1,0:T(8,128)(2,1)}), bf16[512,2048]{1,0:T(8,128)(2,1)}) %all-gather.12.cloned.1.call-update) | async-done | bytes 2097168 | tf_op jit(solution)/shard_map/all_gather | solution.py:185
  294.5 10.4 %attend_back.1 = (bf16[512,256]{1,0:T(8,128)(2,1)}, bf16[2,512,256]{2,1,0:T(8,128)(2,1)}, bf16[2,512,256]{2,1,0:T(8,128)(2,1)}, bf16[2,512,256]{2,1,0:T(8,128)(2...) custom-call(bf16[512,256]{1,0:T(8,128)(2,1)} %get-tuple-element.143.q_ref, s32[512,2]{1,0:T(8,128)} %bitcast.105, ...), custom_call_target="tpu_custom_call" | custom-call | flops 13799999488 | bytes 1 | tf_op jit(solution)/shard_map/attend_back/pallas_call | solution.py:759
  306.0 7.2 %collective-permute-start.36 = (bf16[256,512]{1,0:T(8,128)(2,1)}, bf16[256,512]{1,0:T(8,128)(2,1)}, u32[]{:S(2)}, u32[]{:S(2)}) collective-permute-start(bf16[256,512]{1,0:T(8,128)(2,1)} %get-tuple-element.252), channel_id=1, source_target_pairs={{0,16},{4,20},{8,24},{12,28},{16,0},{20,4},{24,8},{28,12},{1,17},{... | collective-permute-start | bytes 786440 | tf_op jit(solution)/shard_map/ppermute | solution.py:42
  319.0 5.9 %weight_grads.6 = (bf16[4,256,256]{2,1,0:T(8,128)(2,1)}, bf16[4,256,256]{2,1,0:T(8,128)(2,1)}, bf16[4,256,256]{2,1,0:T(8,128)(2,1)}, bf16[2,256,256]{2,1,0:T(8,128)(2,1)}, bf16[2,256,256]{2,1,0:T(8,128)(2,1)}) custom-call(bf16[512,2048]{1,0:T(8,128)(2,1)} %all-gather.12.cloned.1.call-done.value_ref.refs_0_, ...), custom_call_target="tpu_custom_call" | custom-call | flops 3449999872 | bytes 1 | tf_op jit(solution)/shard_map/weight_grads/pallas_call | solution.py:603
  333.4 6.7 %collective-permute-done.37.refs_3_ = bf16[256,512]{1,0:T(8,128)(2,1)} collective-permute-done((bf16[256,512]{1,0:T(8,128)(2,1)S(1)}, bf16[256,512]{1,0:T(8,128)(2,1)}, u32[]{:S(2)}, u32[]{:S(2)}) %collective-permute-start.37) | collective-permute-done | bytes 262176 | tf_op jit(solution)/shard_map/ppermute | solution.py:42
  342.3 7.3 %project_back.1 = (bf16[512,2048]{1,0:T(8,128)(2,1)}, f32[2,2048]{1,0:T(2,128)}) custom-call(bf16[512,256]{1,0:T(8,128)(2,1)} %get-tuple-element.190.refs_3_.query_ref, bf16[2,512,256]{2,1,0:T(8,128)(2,1)} %add_convert_fusion.4.pair_ref.refs_1_, bf16[512,2048]{1,0:T(8,128)(2,1)} %all-gather.6.cloned.1.call-done.tokens_ref, ...), custom_call_target="tpu_custom_call" | custom-call | flops 1 | bytes 1 | tf_op jit(solution)/shard_map/project_back/pallas_call | solution.py:530
  356.2 4.8 %collective-permute-start.53 = (bf16[256,512]{1,0:T(8,128)(2,1)}, bf16[256,512]{1,0:T(8,128)(2,1)}, u32[]{:S(2)}, u32[]{:S(2)}) collective-permute-start(bf16[256,512]{1,0:T(8,128)(2,1)} %get-tuple-element.248), channel_id=1, source_target_pairs={{0,8},{4,12},{8,0},{12,4},{16,24},{20,28},{24,16},{28,20},{1,9},{5... | collective-permute-start | bytes 786440 | tf_op jit(solution)/shard_map/ppermute | solution.py:42
  369.2 7.4 %adam.4 = (f32[2048,256]{1,0:T(8,128)}, f32[2048,256]{1,0:T(8,128)}, f32[2048,256]{1,0:T(8,128)}, bf16[2048,256]{1,0:T(8,128)(2,1)}) custom-call(s32[1]{0:T(128)} %bitcast.at_ref, bf16[256,512]{1,0:T(8,128)(2,1)} %get-tuple-element.205.refs_0_, bf16[256,512]{1,0:T(8,128)(2,1)} %collective-permute-done.35.refs_1_, ...), custom_call_target="tpu_custom_call" | custom-call | flops 8049999872 | bytes 1 | tf_op jit(solution)/shard_map/adam/pallas_call | solution.py:845
  382.9 13.8 %collective-permute-done.55.refs_3_ = bf16[256,512]{1,0:T(8,128)(2,1)} collective-permute-done((bf16[256,512]{1,0:T(8,128)(2,1)S(1)}, bf16[256,512]{1,0:T(8,128)(2,1)}, u32[]{:S(2)}, u32[]{:S(2)}) %collective-permute-start.55) | collective-permute-done | bytes 262176 | tf_op jit(solution)/shard_map/ppermute | solution.py:42
  396.7 7.4 %adam.5 = (f32[256,2048]{1,0:T(8,128)}, f32[256,2048]{1,0:T(8,128)}, f32[256,2048]{1,0:T(8,128)}, bf16[256,2048]{1,0:T(8,128)(2,1)}) custom-call(s32[1]{0:T(128)} %bitcast.at_ref, bf16[256,512]{1,0:T(8,128)(2,1)} %get-tuple-element.214.refs_0_, bf16[256,512]{1,0:T(8,128)(2,1)} %collective-permute-done.53.refs_1_, ...), custom_call_target="tpu_custom_call" | custom-call | flops 8049999872 | bytes 1 | tf_op jit(solution)/shard_map/adam/pallas_call | solution.py:845
  423.2 11.7 %collective-permute-done.58.refs_7_ = bf16[272,256]{1,0:T(8,128)(2,1)S(1)} collective-permute-done((bf16[272,256]{1,0:T(8,128)(2,1)S(1)}, bf16[272,256]{1,0:T(8,128)(2,1)S(1)}, u32[]{:S(2)}, u32[]{:S(2)}) %collective-permute-start.58) | collective-permute-done | bytes 139296 | tf_op jit(solution)/shard_map/ppermute | solution.py:42
  448.5 6.1 %adam.6 = (f32[3,256,512]{2,1,0:T(8,128)}, f32[3,256,512]{2,1,0:T(8,128)}, f32[3,256,512]{2,1,0:T(8,128)}, bf16[3,256,512]{2,1,0:T(8,128)(2,1)}) custom-call(s32[1]{0:T(128)} %bitcast.at_ref, bf16[256,256]{1,0:T(8,128)(2,1)} %get-tuple-element.261.refs_0_, bf16[256,256]{1,0:T(8,128)(2,1)} %copy-done.64, bf16[256,256]{1,0:T(8,128)(2,1)} %copy-done.65, ...), custom_call_target="tpu_custom_call" | custom-call | flops 8049999872 | bytes 1 | tf_op jit(solution)/shard_map/adam/pallas_call | solution.py:845
  (385 shorter events, 192.3 us)
Async XLA Ops:
  7.2 70.1 %all-gather.6.cloned.1.call-start = ((), (), s32[]{:S(2)}) async-start(), calls=%async_computation.4 | async-start | bytes 2359296 | tf_op jit(solution)/shard_map/all_gather | solution.py:185
  14.0 24.1 %collective-permute-start.2 = (bf16[272,512]{1,0:T(8,128)(2,1)}, bf16[272,512]{1,0:T(8,128)(2,1)S(1)}, u32[]{:S(2)}, u32[]{:S(2)}) collective-permute-start(bf16[272,512]{1,0:T(8,128)(2,1)} %get-tuple-element.133), channel_id=1, source_target_pairs={{0,24},{4,28},{8,16},{12,20},{16,8},{20,12},{24,0},{28,4},{1,25},{... | collective-permute-start | bytes 835592 | tf_op jit(solution)/shard_map/ppermute | solution.py:42
  38.1 92.2 %all-gather.8.cloned.1.call-start = ((), (), s32[]{:S(2)}) async-start(), calls=%async_computation.5 | async-start | bytes 2359296 | tf_op jit(solution)/shard_map/all_gather | solution.py:185
  41.0 24.6 %collective-permute-start.3 = (bf16[4,272,512]{2,1,0:T(8,128)(2,1)}, bf16[4,272,512]{2,1,0:T(8,128)(2,1)S(1)}, u32[]{:S(2)}, u32[]{:S(2)}) collective-permute-start(bf16[4,272,512]{2,1,0:T(8,128)(2,1)} %assemble.3.refs_0_), channel_id=1, source_target_pairs={{0,4},{4,0},{8,12},{12,8},{16,20},{20,16},{24,28},{28,24},{1,5},{5... | collective-permute-start | bytes 3342344 | tf_op jit(solution)/shard_map/ppermute | solution.py:42
  48.0 120.6 %reduce-scatter.5.cloned.1.call-start = ((), (), s32[]{:S(2)}) async-start(), calls=%async_computation.6 | async-start | bytes 2359296 | tf_op jit(solution)/shard_map/reduce_scatter | solution.py:191
  49.3 24.9 %collective-permute-start.4 = (bf16[256,512]{1,0:T(8,128)(2,1)}, bf16[256,512]{1,0:T(8,128)(2,1)}, u32[]{:S(2)}, u32[]{:S(2)}) collective-permute-start(bf16[256,512]{1,0:T(8,128)(2,1)} %get-tuple-element.136), channel_id=1, source_target_pairs={{0,8},{4,12},{8,0},{12,4},{16,24},{20,28},{24,16},{28,20},{1,9},{5... | collective-permute-start | bytes 786440 | tf_op jit(solution)/shard_map/ppermute | solution.py:42
  54.7 21.1 %collective-permute-start.6 = (bf16[256,512]{1,0:T(8,128)(2,1)}, bf16[256,512]{1,0:T(8,128)(2,1)}, u32[]{:S(2)}, u32[]{:S(2)}) collective-permute-start(bf16[256,512]{1,0:T(8,128)(2,1)} %get-tuple-element.138), channel_id=1, source_target_pairs={{0,24},{4,28},{8,16},{12,20},{16,8},{20,12},{24,0},{28,4},{1,25},{... | collective-permute-start | bytes 786440 | tf_op jit(solution)/shard_map/ppermute | solution.py:42
  104.5 25.9 %collective-permute-start.16 = (bf16[256,512]{1,0:T(8,128)(2,1)}, bf16[256,512]{1,0:T(8,128)(2,1)S(1)}, u32[]{:S(2)}, u32[]{:S(2)}) collective-permute-start(bf16[256,512]{1,0:T(8,128)(2,1)} %get-tuple-element.152), channel_id=1, source_target_pairs={{0,24},{4,28},{8,16},{12,20},{16,8},{20,12},{24,0},{28,4},{1,25},{... | collective-permute-start | bytes 786440 | tf_op jit(solution)/shard_map/ppermute | solution.py:42
  134.8 71.9 %all-gather.10.cloned.1.call-start = ((), (), s32[]{:S(2)}) async-start(), calls=%async_computation.7 | async-start | bytes 2359296 | tf_op jit(solution)/shard_map/all_gather | solution.py:185
  136.0 21.0 %collective-permute-start.17 = (bf16[4,256,512]{2,1,0:T(8,128)(2,1)S(1)}, bf16[4,256,512]{2,1,0:T(8,128)(2,1)S(1)}, u32[]{:S(2)}, u32[]{:S(2)}) collective-permute-start(bf16[4,256,512]{2,1,0:T(8,128)(2,1)S(1)} %copy-done.4), channel_id=1, source_target_pairs={{0,2},{1,3},{2,0},{3,1},{4,6},{5,7},{6,4},{7,5},{8,10},{9,11},{10,... | collective-permute-start | bytes 3145736 | tf_op jit(solution)/shard_map/ppermute | solution.py:42
  158.6 21.6 %collective-permute-start.19 = (bf16[4,256,512]{2,1,0:T(8,128)(2,1)}, bf16[4,256,512]{2,1,0:T(8,128)(2,1)S(1)}, u32[]{:S(2)}, u32[]{:S(2)}) collective-permute-start(bf16[4,256,512]{2,1,0:T(8,128)(2,1)} %assemble.5.refs_0_), channel_id=1, source_target_pairs={{0,4},{4,0},{8,12},{12,8},{16,20},{20,16},{24,28},{28,24},{1,5},{5... | collective-permute-start | bytes 3145736 | tf_op jit(solution)/shard_map/ppermute | solution.py:42
  173.8 73.5 %reduce-scatter.7.cloned.1.call-start = ((), (), s32[]{:S(2)}) async-start(), calls=%async_computation.8 | async-start | bytes 2359296 | tf_op jit(solution)/shard_map/reduce_scatter | solution.py:191
  181.9 20.9 %collective-permute-start.23 = (bf16[2,256,512]{2,1,0:T(8,128)(2,1)}, bf16[2,256,512]{2,1,0:T(8,128)(2,1)}, u32[]{:S(2)}, u32[]{:S(2)}) collective-permute-start(bf16[2,256,512]{2,1,0:T(8,128)(2,1)} %slice.186), channel_id=1, source_target_pairs={{0,4},{4,0},{8,12},{12,8},{16,20},{20,16},{24,28},{28,24},{1,5},{5... | collective-permute-start | bytes 1572872 | tf_op jit(solution)/shard_map/ppermute | solution.py:42
  216.5 68.1 %all-gather.12.cloned.1.call-start = ((), (), s32[]{:S(2)}) async-start(), calls=%async_computation.10 | async-start | bytes 2359296 | tf_op jit(solution)/shard_map/all_gather | solution.py:185
  251.5 73.5 %reduce-scatter.9.cloned.1.call-start = ((), (), s32[]{:S(2)}) async-start(), calls=%async_computation.9 | async-start | bytes 2359296 | tf_op jit(solution)/shard_map/reduce_scatter | solution.py:191
  251.5 23.0 %collective-permute-start.27 = (bf16[4,256,512]{2,1,0:T(8,128)(2,1)S(1)}, bf16[4,256,512]{2,1,0:T(8,128)(2,1)S(1)}, u32[]{:S(2)}, u32[]{:S(2)}) collective-permute-start(bf16[4,256,512]{2,1,0:T(8,128)(2,1)S(1)} %pad_maximum_fusion), channel_id=1, source_target_pairs={{0,2},{1,3},{2,0},{3,1},{4,6},{5,7},{6,4},{7,5},{8,10},{9,11},{10,... | collective-permute-start | bytes 3145736 | tf_op jit(solution)/shard_map/ppermute | solution.py:42
  252.4 22.4 %collective-permute-start.28 = (bf16[4,256,512]{2,1,0:T(8,128)(2,1)}, bf16[4,256,512]{2,1,0:T(8,128)(2,1)}, u32[]{:S(2)}, u32[]{:S(2)}) collective-permute-start(bf16[4,256,512]{2,1,0:T(8,128)(2,1)} %pad_maximum_fusion.1), channel_id=1, source_target_pairs={{0,4},{4,0},{8,12},{12,8},{16,20},{20,16},{24,28},{28,24},{1,5},{5... | collective-permute-start | bytes 3145736 | tf_op jit(solution)/shard_map/ppermute | solution.py:42
  259.3 149.7 %reduce-scatter.11.cloned.1.call-start = ((), (), s32[]{:S(2)}) async-start(), calls=%async_computation.12 | async-start | bytes 2359296 | tf_op jit(solution)/shard_map/reduce_scatter | solution.py:191
  289.7 23.9 %collective-permute-start.30 = (bf16[4,256,512]{2,1,0:T(8,128)(2,1)S(1)}, bf16[4,256,512]{2,1,0:T(8,128)(2,1)}, u32[]{:S(2)}, u32[]{:S(2)}) collective-permute-start(bf16[4,256,512]{2,1,0:T(8,128)(2,1)S(1)} %pad_maximum_fusion.2), channel_id=1, source_target_pairs={{0,2},{1,3},{2,0},{3,1},{4,6},{5,7},{6,4},{7,5},{8,10},{9,11},{10,... | collective-permute-start | bytes 3145736 | tf_op jit(solution)/shard_map/ppermute | solution.py:42
  293.3 23.7 %collective-permute-start.32 = (bf16[4,256,512]{2,1,0:T(8,128)(2,1)}, bf16[4,256,512]{2,1,0:T(8,128)(2,1)}, u32[]{:S(2)}, u32[]{:S(2)}) collective-permute-start(bf16[4,256,512]{2,1,0:T(8,128)(2,1)} %pad_maximum_fusion.3), channel_id=1, source_target_pairs={{0,4},{4,0},{8,12},{12,8},{16,20},{20,16},{24,28},{28,24},{1,5},{5... | collective-permute-start | bytes 3145736 | tf_op jit(solution)/shard_map/ppermute | solution.py:42
  305.8 24.4 %collective-permute-start.35 = (bf16[256,512]{1,0:T(8,128)(2,1)}, bf16[256,512]{1,0:T(8,128)(2,1)}, u32[]{:S(2)}, u32[]{:S(2)}) collective-permute-start(bf16[256,512]{1,0:T(8,128)(2,1)} %get-tuple-element.253), channel_id=1, source_target_pairs={{0,8},{4,12},{8,0},{12,4},{16,24},{20,28},{24,16},{28,20},{1,9},{5... | collective-permute-start | bytes 786440 | tf_op jit(solution)/shard_map/ppermute | solution.py:42
  306.0 27.4 %collective-permute-start.36 = (bf16[256,512]{1,0:T(8,128)(2,1)}, bf16[256,512]{1,0:T(8,128)(2,1)}, u32[]{:S(2)}, u32[]{:S(2)}) collective-permute-start(bf16[256,512]{1,0:T(8,128)(2,1)} %get-tuple-element.252), channel_id=1, source_target_pairs={{0,16},{4,20},{8,24},{12,28},{16,0},{20,4},{24,8},{28,12},{1,17},{... | collective-permute-start | bytes 786440 | tf_op jit(solution)/shard_map/ppermute | solution.py:42
  313.2 26.9 %collective-permute-start.37 = (bf16[256,512]{1,0:T(8,128)(2,1)S(1)}, bf16[256,512]{1,0:T(8,128)(2,1)}, u32[]{:S(2)}, u32[]{:S(2)}) collective-permute-start(bf16[256,512]{1,0:T(8,128)(2,1)S(1)} %get-tuple-element.251), channel_id=1, source_target_pairs={{0,24},{4,28},{8,16},{12,20},{16,8},{20,12},{24,0},{28,4},{1,25},{... | collective-permute-start | bytes 786440 | tf_op jit(solution)/shard_map/ppermute | solution.py:42
  349.7 95.8 %all-gather.14.cloned.1.call-start = ((), (), s32[]{:S(2)}) async-start(), calls=%async_computation.11 | async-start | bytes 1310720 | tf_op jit(solution)/shard_map/all_gather | solution.py:1044
  356.2 24.9 %collective-permute-start.53 = (bf16[256,512]{1,0:T(8,128)(2,1)}, bf16[256,512]{1,0:T(8,128)(2,1)}, u32[]{:S(2)}, u32[]{:S(2)}) collective-permute-start(bf16[256,512]{1,0:T(8,128)(2,1)} %get-tuple-element.248), channel_id=1, source_target_pairs={{0,8},{4,12},{8,0},{12,4},{16,24},{20,28},{24,16},{28,20},{1,9},{5... | collective-permute-start | bytes 786440 | tf_op jit(solution)/shard_map/ppermute | solution.py:42
  361.0 21.5 %collective-permute-start.54 = (bf16[256,512]{1,0:T(8,128)(2,1)}, bf16[256,512]{1,0:T(8,128)(2,1)}, u32[]{:S(2)}, u32[]{:S(2)}) collective-permute-start(bf16[256,512]{1,0:T(8,128)(2,1)} %get-tuple-element.247), channel_id=1, source_target_pairs={{0,16},{4,20},{8,24},{12,28},{16,0},{20,4},{24,8},{28,12},{1,17},{... | collective-permute-start | bytes 786440 | tf_op jit(solution)/shard_map/ppermute | solution.py:42
  361.8 34.9 %collective-permute-start.55 = (bf16[256,512]{1,0:T(8,128)(2,1)S(1)}, bf16[256,512]{1,0:T(8,128)(2,1)}, u32[]{:S(2)}, u32[]{:S(2)}) collective-permute-start(bf16[256,512]{1,0:T(8,128)(2,1)S(1)} %get-tuple-element.246), channel_id=1, source_target_pairs={{0,24},{4,28},{8,16},{12,20},{16,8},{20,12},{24,0},{28,4},{1,25},{... | collective-permute-start | bytes 786440 | tf_op jit(solution)/shard_map/ppermute | solution.py:42
  379.5 37.3 %collective-permute-start.45 = (bf16[4,256,256]{2,1,0:T(8,128)(2,1)}, bf16[4,256,256]{2,1,0:T(8,128)(2,1)}, u32[]{:S(2)}, u32[]{:S(2)}) collective-permute-start(bf16[4,256,256]{2,1,0:T(8,128)(2,1)} %pad_maximum_fusion.11), channel_id=1, source_target_pairs={{0,4},{4,0},{8,12},{12,8},{16,20},{20,16},{24,28},{28,24},{1,5},{5... | collective-permute-start | bytes 1572872 | tf_op jit(solution)/shard_map/ppermute | solution.py:42
  380.7 36.1 %collective-permute-start.43 = (bf16[4,256,256]{2,1,0:T(8,128)(2,1)}, bf16[4,256,256]{2,1,0:T(8,128)(2,1)}, u32[]{:S(2)}, u32[]{:S(2)}) collective-permute-start(bf16[4,256,256]{2,1,0:T(8,128)(2,1)} %pad_maximum_fusion.10), channel_id=1, source_target_pairs={{0,2},{1,3},{2,0},{3,1},{4,6},{5,7},{6,4},{7,5},{8,10},{9,11},{10,... | collective-permute-start | bytes 1572872 | tf_op jit(solution)/shard_map/ppermute | solution.py:42
  381.1 23.0 %collective-permute-start.52 = (bf16[4,272,256]{2,1,0:T(8,128)(2,1)S(1)}, bf16[4,272,256]{2,1,0:T(8,128)(2,1)S(1)}, u32[]{:S(2)}, u32[]{:S(2)}) collective-permute-start(bf16[4,272,256]{2,1,0:T(8,128)(2,1)S(1)} %pad_maximum_fusion.6), channel_id=1, source_target_pairs={{0,4},{4,0},{8,12},{12,8},{16,20},{20,16},{24,28},{28,24},{1,5},{5... | collective-permute-start | bytes 1671176 | tf_op jit(solution)/shard_map/ppermute | solution.py:42
  382.4 21.7 %collective-permute-start.50 = (bf16[4,272,256]{2,1,0:T(8,128)(2,1)S(1)}, bf16[4,272,256]{2,1,0:T(8,128)(2,1)S(1)}, u32[]{:S(2)}, u32[]{:S(2)}) collective-permute-start(bf16[4,272,256]{2,1,0:T(8,128)(2,1)S(1)} %pad_maximum_fusion.5), channel_id=1, source_target_pairs={{0,2},{1,3},{2,0},{3,1},{4,6},{5,7},{6,4},{7,5},{8,10},{9,11},{10,... | collective-permute-start | bytes 1671176 | tf_op jit(solution)/shard_map/ppermute | solution.py:42
  421.7 25.7 %collective-permute-start.40 = (bf16[64,2048]{1,0:T(8,128)(2,1)S(1)}, bf16[64,2048]{1,0:T(8,128)(2,1)S(1)}, u32[]{:S(2)}, u32[]{:S(2)}) collective-permute-start(bf16[64,2048]{1,0:T(8,128)(2,1)S(1)} %reshape.174), channel_id=1, source_target_pairs={{0,2},{1,3},{2,0},{3,1},{4,6},{5,7},{6,4},{7,5},{8,10},{9,11},{10,... | collective-permute-start | bytes 786440 | tf_op jit(solution)/shard_map/ppermute | solution.py:42
  (105 other events, 1084.1 us)
Sparse Core Ops, SparseCore 0:
  38.2 39.0 all-gather.5
  79.5 39.8 all-gather.7
  134.9 33.6 reduce-scatter.4
  174.0 32.7 all-gather.9
  216.6 30.6 reduce-scatter.6
  251.6 32.9 all-gather.11
  287.5 31.5 reduce-scatter.8
  349.8 59.1 reduce-scatter.10
  410.5 16.3 all-gather.13
